TPU v7x, 128 devices: a whole 4x4x4 slice. The times are simulated.
128 devices in a mesh: dom: 8 (over x, core), grp: 16 (over y, z).
Axes of the slice: x: 4, y: 4, z: 4, core: 2. Of those that a mesh axis runs over, the one named last changes fastest.
Arguments:
- features: bfloat16 [524288, 1024], P(('dom', 'grp')), may hold values from -6 to 6
- requests: int32 [128, 128, 13], P(('dom', 'grp')), may hold values from 0 to 4095, as said below
- target_rows: int32 [4096], P(('dom', 'grp')), may hold values from 0 to 4095
- neighbour_slot: int32 [4096, 50], P(('dom', 'grp')), may hold values from 0 to 1663, as said below
- counts: int32 [4096, 50], P(('dom', 'grp')), may hold values from 1 to 63
- hidden_weight: bfloat16 [1024, 2048], P(None, 'grp'), may hold values from -0.1875 to 0.1875
- hidden_bias: float32 [2048], replicated, may hold values from -3 to 3
- output_weight: bfloat16 [3072, 1024], replicated, may hold values from -0.109375 to 0.109375
- output_bias: float32 [1024], replicated, may hold values from -3 to 3
Outputs:
- embedding: bfloat16 [4096, 1024], P(('dom', 'grp'))
Inputs may be any that keep to these rules, and one draw needn't show every extreme that they name: `requests`: the rows requested by one device from one owner are distinct; entries at slots that no neighbour names are arbitrary. `neighbour_slot`: the targets of one device name exactly 800 distinct slots; from owner p they are the first c slots p * 13 to p * 13 + c - 1 for some c of 0 to 13, and on every device some owner has all 13 slots named. Several neighbours may share a slot.
All inputs are finite; a program needn't handle non-finite values.
Results may differ from a plain program's by a relative error of at most 0.0065.
Values may be sent and summed in bfloat16 or wider, within the bound.
No kernel may reach another device: no remote copies, remote signals or barrier semaphores. Data moves between devices by JAX's collectives and lax.ppermute only.
A program may use at most 128 MiB of HBM per device.

v0:
```python
import jax
import jax.numpy as jnp
from jax import lax
from jax.sharding import PartitionSpec as P


def transform(rows, hidden_weight, hidden_bias):
    product = jnp.dot(
        rows,
        lax.all_gather(hidden_weight, "grp", axis=1, tiled=True),
        preferred_element_type=jnp.float32,
    )
    return jnp.maximum(product + hidden_bias, 0.0).astype(jnp.bfloat16)


def on_device(
    features,
    requests,
    target_rows,
    neighbour_slot,
    counts,
    hidden_weight,
    hidden_bias,
    output_weight,
    output_bias,
):
    wanted = requests[0]
    peers, capacity = wanted.shape
    served = lax.all_to_all(wanted, ("dom", "grp"), split_axis=0, concat_axis=0, tiled=True)
    outgoing = features[served.reshape(-1)]
    payload = outgoing.shape[1]
    blocks = outgoing.reshape(peers, capacity, payload)
    arrived = lax.all_to_all(blocks, ("dom", "grp"), split_axis=0, concat_axis=0, tiled=True)
    arrived = arrived.reshape(peers * capacity, payload)
    hidden_rows = transform(arrived, hidden_weight, hidden_bias)
    picked = hidden_rows[neighbour_slot]
    weight_low = counts.astype(jnp.bfloat16)
    summed = jnp.einsum("tk,tkh->th", weight_low, picked, preferred_element_type=jnp.float32)
    total = jnp.sum(counts.astype(jnp.float32), axis=1, keepdims=True)
    pooled = (summed / total).astype(jnp.bfloat16)
    own = features[target_rows]
    joined = jnp.concatenate([own, pooled], axis=1)
    combined = jnp.maximum(
        jnp.dot(joined, output_weight, preferred_element_type=jnp.float32) + output_bias, 0.0
    )
    scale = lax.rsqrt(jnp.mean(combined * combined, axis=1, keepdims=True) + 1e-06)
    return (combined * scale).astype(jnp.bfloat16)


def solution(mesh):
    placed = (
        P(("dom", "grp"), None),
        P(("dom", "grp"), None, None),
        P(("dom", "grp")),
        P(("dom", "grp"), None),
        P(("dom", "grp"), None),
        P(None, "grp"),
        P(),
        P(),
        P(),
    )
    return jax.shard_map(
        on_device, mesh=mesh, in_specs=placed, out_specs=P(("dom", "grp"), None), check_vma=False
    )
```

profile of v0, /device:TPU:1, one launch (start us, length us, event | category | flops | bytes accessed | tf_op | source)
XLA Modules:
  0.0 169.4 jit_solution(1231906363565614169)
XLA Ops:
  6.5 0.7 all-gather.2.cloned.1.call-update
  7.3 0.8 copy.13
  8.1 20.9 %all_to_all.14 = s32[128,1,13]{2,1,0:T(1,128)S(1)} all-to-all(s32[128,1,13]{2,1,0:T(1,128)S(1)} %copy.13), channel_id=1, replica_groups=mesh['dom'=8,'grp'=16] {'dom','grp'}, dimensions={0} | all-to-all | bytes 13312 | tf_op jit(solution)/shard_map/all_to_all | solution.py:29
  28.9 0.5 broadcast.44
  29.4 0.8 reduce.5
  30.3 0.2 reshape.52
  30.5 12.9 %gather_fusion.1 = bf16[1664,1024]{1,0:T(8,128)(2,1)S(1)} fusion(bf16[4096,1024]{1,0:T(8,128)(2,1)} %param.9, s32[2048]{0:T(1024)S(1)} %pad_clamp_fusion.1), kind=kCustom, calls=%fused_computation.1 | custom fusion | bytes 6822400 | tf_op jit(solution)/shard_map/gather | solution.py:30
  43.4 0.0 copy-start.1
  43.4 0.0 copy-start.4
  43.4 2.9 %reshape.53 = bf16[128,13,1024]{2,1,0:T(8,128)(2,1)} reshape(bf16[1664,1024]{1,0:T(8,128)(2,1)S(1)} %gather_fusion.1) | data formatting | bytes 6815744 | tf_op jit(solution)/shard_map/reshape | solution.py:32
  46.3 5.7 %all-to-all-start.1 = ((bf16[128,13,1024]{2,1,0:T(8,128)(2,1)}), bf16[128,13,1024]{2,1,0:T(8,128)(2,1)}, u32[]{:S(2)}, u32[]{:S(2)}) async-start(bf16[128,13,1024]{2,1,0:T(8,128)(2,1)} %reshape.53), calls=%async_computation.1 | async-start | bytes 8388608 | tf_op jit(solution)/shard_map/all_to_all | solution.py:33
  52.0 0.1 reshape.73
  52.2 5.2 %gather_fusion = bf16[32,1024]{1,0:T(8,128)(2,1)S(1)} fusion(bf16[4096,1024]{1,0:T(8,128)(2,1)} %param.9, s32[1024]{0:T(1024)S(1)} %pad_clamp_fusion.2), kind=kCustom, calls=%fused_computation | custom fusion | bytes 131200 | tf_op jit(solution)/shard_map/gather | solution.py:41
  57.4 0.1 convert_reduce_fusion
  57.5 50.3 %all-to-all-done.1 = bf16[128,13,1024]{2,1,0:T(8,128)(2,1)} async-done(((bf16[128,13,1024]{2,1,0:T(8,128)(2,1)}), bf16[128,13,1024]{2,1,0:T(8,128)(2,1)}, u32[]{:S(2)}, u32[]{:S(2)}) %all-to-all-start.1) | async-done | bytes 3407904 | tf_op jit(solution)/shard_map/all_to_all | solution.py:33
  107.8 4.3 %reshape.54 = bf16[1664,1024]{1,0:T(8,128)(2,1)S(1)} reshape(bf16[128,13,1024]{2,1,0:T(8,128)(2,1)} %all-to-all-done.1) | data formatting | bytes 6815744 | tf_op jit(solution)/shard_map/reshape | solution.py:34
  112.1 3.3 %all-gather.2.cloned.1.call-done = bf16[1024,2048]{1,0:T(8,128)(2,1)} async-done(((bf16[1024,128]{1,0:T(8,128)(2,1)}), bf16[1024,2048]{1,0:T(8,128)(2,1)}) %all-gather.2.cloned.1.call-update) | async-done | bytes 4194320 | tf_op jit(solution)/shard_map/all_gather | solution.py:10
  115.3 11.3 %maximum_convert_fusion = bf16[1664,2048]{1,0:T(8,128)(2,1)} fusion(bf16[1664,1024]{1,0:T(8,128)(2,1)S(1)} %reshape.54, bf16[1024,2048]{1,0:T(8,128)(2,1)} %all-gather.2.cloned.1.call-done, f32[2048]{0:T(1024)S(1)} %copy-done.3), kind=kOutput, calls=%fused_computation.3 | convolution fusion | flops 6989545472 | bytes 14426112 | tf_op jit(solution)/shard_map/dot_general | solution.py:8
  126.7 18.1 %gather_fusion.2 = bf16[1600,2048]{1,0:T(8,128)(2,1)} fusion(bf16[1664,2048]{1,0:T(8,128)(2,1)} %maximum_convert_fusion, s32[2048]{0:T(1024)S(1)} %pad_clamp_fusion), kind=kCustom, calls=%fused_computation.2 | custom fusion | bytes 13113600 | tf_op jit(solution)/shard_map/gather | solution.py:36
  144.8 8.7 %reshape.72 = bf16[32,50,2048]{2,1,0:T(8,128)(2,1)} reshape(bf16[1600,2048]{1,0:T(8,128)(2,1)} %gather_fusion.2) | data formatting | bytes 13107200 | tf_op jit(solution)/shard_map/gather | solution.py:36
  153.4 4.2 %fusion.5 = f32[32,1,2048]{2,1,0:T(1,128)S(1)} fusion(bf16[32,50,2048]{2,1,0:T(8,128)(2,1)} %reshape.72, bf16[32,50,1]{1,0,2:T(8,128)(2,1)S(1)} %convert_bitcast_fusion), kind=kOutput, calls=%fused_computation.15 | convolution fusion | flops 6553600 | bytes 6818944 | tf_op jit(solution)/shard_map/tk,tkh->th/dot_general | solution.py:38
  157.6 0.1 fusion.1
  157.7 4.1 %multiply_reduce_fusion = (f32[32]{0:T(128)S(1)}, f32[32,1024]{1,0:T(8,128)S(1)}) fusion(f32[1024]{0:T(1024)S(1)} %copy-done.2, bf16[3072,1024]{1,0:T(8,128)(2,1)} %param.16, bf16[32,2048]{1,0:T(8,128)(2,1)S(1)} %fusion.1, bf16[32,1024]{1,0:T(8,128)(2,1)S(1)} %gather_fusion), kind=kOutput, calls=%fused_computation.12 | convolution fusion | flops 201850848 | bytes 6623360 | tf_op jit(solution)/shard_map/dot_general | solution.py:44
  161.8 0.7 multiply_convert_fusion
  (17 shorter events, 0.1 us)
Async XLA Ops:
  6.5 108.8 %all-gather.2.cloned.1.call-start = ((), (), s32[]{:S(2)}) async-start(), calls=%async_computation.2 | async-start | bytes 4456448 | tf_op jit(solution)/shard_map/all_gather | solution.py:10
  43.4 8.6 %copy-start.1 = (s32[32,50]{1,0:T(8,128)S(1)}, s32[32,50]{1,0:T(8,128)}, u32[]{:S(2)}) copy-start(s32[32,50]{1,0:T(8,128)} %param.12) | copy-start | bytes 19204
  43.4 8.7 %copy-start.4 = (s32[32]{0:T(128)S(1)}, s32[32]{0:T(128)}, u32[]{:S(2)}) copy-start(s32[32]{0:T(128)} %param.11) | copy-start | bytes 388
  43.4 14.0 %copy-start = (s32[32,50]{1,0:T(8,128)S(1)}, s32[32,50]{1,0:T(8,128)}, u32[]{:S(2)}) copy-start(s32[32,50]{1,0:T(8,128)} %param.13) | copy-start | bytes 19204
  46.3 69.0 %copy-start.3 = (f32[2048]{0:T(1024)S(1)}, f32[2048]{0:T(1024)}, u32[]{:S(2)}) copy-start(f32[2048]{0:T(1024)} %param.15) | copy-start | bytes 24580
  46.3 61.5 %all-to-all-start.1 = ((bf16[128,13,1024]{2,1,0:T(8,128)(2,1)}), bf16[128,13,1024]{2,1,0:T(8,128)(2,1)}, u32[]{:S(2)}, u32[]{:S(2)}) async-start(bf16[128,13,1024]{2,1,0:T(8,128)(2,1)} %reshape.53), calls=%async_computation.1 | async-start | bytes 8388608 | tf_op jit(solution)/shard_map/all_to_all | solution.py:33
  153.4 4.3 %copy-start.2 = (f32[1024]{0:T(1024)S(1)}, f32[1024]{0:T(1024)}, u32[]{:S(2)}) copy-start(f32[1024]{0:T(1024)} %param.17) | copy-start | bytes 12292
Sparse Core Ops, SparseCore 0:
  9.5 105.8 all-gather.1
where the time goes:
time: 170 us; the launch traced here: 169 us
  waiting for transfers between devices  54.2 us (32%)
  local copies, waits for them, and re-layouts  53.6 us (32%)
  blocking collectives  20.9 us (12%)
  matrix products  19.6 us (12%)
  between operations  13.6 us (8%)
  starting transfers between devices  5.66 us (3%)
  other arithmetic  1.8 us (1%)
    all_to_all x1, waiting for transfers between devices, on_device(): lax.all_to_all(blocks, ('dom', 'grp'), split_axis=0, concat_axis=0, tiled...  50.3 us
    gather x2, local copies, waits for them, and re-layouts, on_device(): picked = hidden_rows[neighbour_slot]  26.8 us
    all_to_all x1, blocking collectives, on_device(): lax.all_to_all(wanted, ('dom', 'grp'), split_axis=0, concat_axis=0, tiled...  20.9 us
    gather x1, local copies, waits for them, and re-layouts, on_device(): outgoing = features[served.reshape(-1)]  12.9 us
    dot_general x1, matrix products, transform(): jnp.dot(rows, lax.all_gather(hidden_weight, 'grp', axis=1, tiled=True), p...  11.3 us
    all_to_all x1, starting transfers between devices, on_device(): lax.all_to_all(blocks, ('dom', 'grp'), split_axis=0, concat_axis=0, tiled...  5.66 us
    gather x1, local copies, waits for them, and re-layouts, on_device(): own = features[target_rows]  5.22 us
    reshape x1, local copies, waits for them, and re-layouts, on_device(): arrived = arrived.reshape(peers * capacity, payload)  4.26 us
  transfers between devices with their start and end apart: 2, of which 2 were waited for; matrix products, arithmetic and copies ran while one was open for 16% of the time, Pallas kernels for 0%

commit v1 on v0

v1 whole, which is shorter than its diff:
```python
import functools

import jax
import jax.numpy as jnp
from jax import lax
from jax.experimental import pallas as pl
from jax.experimental.pallas import tpu as pltpu
from jax.sharding import PartitionSpec as P

LIVE = 800
LANES = 128
ROWS_AT_ONCE = 256
BLOCK = 256
AXES = ("dom", "grp")
SHIFTS = (0, 1, 3, 2)
GRANT = pltpu.CompilerParams(vmem_limit_bytes=60 * 2**20)


def relayout_kernel(features, rows, held, spread, out, in_sems, out_sems):
    steps = features.shape[0] // ROWS_AT_ONCE
    chunks = features.shape[1] // LANES

    def load(step):
        part = pl.ds(step * ROWS_AT_ONCE, ROWS_AT_ONCE)
        return pltpu.make_async_copy(features.at[part], held.at[part], in_sems.at[step])

    def store(step):
        part = pl.ds(step * ROWS_AT_ONCE, ROWS_AT_ONCE)
        return pltpu.make_async_copy(out.at[part], rows.at[part], out_sems.at[step])

    for step in range(steps):
        load(step).start()
    for step in range(steps):
        load(step).wait()
        part = pl.ds(step * ROWS_AT_ONCE, ROWS_AT_ONCE)
        for chunk in range(chunks):
            piece = held[part, pl.ds(chunk * LANES, LANES)].astype(jnp.float32)
            spread[step % 2, pl.ds(chunk, ROWS_AT_ONCE, stride=chunks), :] = piece
        whole = spread[step % 2].reshape(ROWS_AT_ONCE, chunks, LANES)
        out[part] = whole.astype(jnp.bfloat16)
        store(step).start()
    for step in range(steps):
        store(step).wait()


def relayout(features):
    count, width = features.shape
    chunks = width // LANES
    steps = count // ROWS_AT_ONCE
    hbm = pl.BlockSpec(memory_space=pltpu.HBM)
    return pl.pallas_call(
        relayout_kernel,
        out_shape=jax.ShapeDtypeStruct((count, chunks, LANES), jnp.bfloat16),
        in_specs=[hbm],
        out_specs=hbm,
        scratch_shapes=[
            pltpu.VMEM((count, width), jnp.bfloat16),
            pltpu.VMEM((2, ROWS_AT_ONCE * chunks, LANES), jnp.float32),
            pltpu.VMEM((count, chunks, LANES), jnp.bfloat16),
            pltpu.SemaphoreType.DMA((steps,)),
            pltpu.SemaphoreType.DMA((steps,)),
        ],
        compiler_params=GRANT,
        name="relayout",
    )(features)


def pick_kernel(served, target_rows, rows, outgoing, own, index, own_index, all_rows, held, held_own, sems):
    peers, _, capacity = served.shape
    steps = sems.shape[0] - 4
    span = peers // steps
    first = [
        pltpu.make_async_copy(rows, all_rows, sems.at[steps]),
        pltpu.make_async_copy(served, index, sems.at[steps + 1]),
        pltpu.make_async_copy(target_rows, own_index, sems.at[steps + 2]),
    ]
    for copy in first:
        copy.start()
    for copy in first:
        copy.wait()
    copies = []
    for step in range(steps):

        def peer(p, carry):
            for slot in range(capacity):
                held[p * capacity + slot] = all_rows[index[p, 0, slot]]
            return carry

        lax.fori_loop(step * span, (step + 1) * span, peer, 0)
        part = pl.ds(step * span * capacity, span * capacity)
        copies.append(pltpu.make_async_copy(held.at[part], outgoing.at[part], sems.at[step]))
        copies[-1].start()

    def target(t, carry):
        held_own[t] = all_rows[own_index[t]]
        return carry

    lax.fori_loop(0, own.shape[0], target, 0)
    copies.append(pltpu.make_async_copy(held_own, own, sems.at[steps + 3]))
    copies[-1].start()
    for copy in copies:
        copy.wait()


def pick(served, target_rows, rows):
    peers, _, capacity = served.shape
    tile = rows.shape[1:]
    outgoing = jax.ShapeDtypeStruct((peers * capacity,) + tile, rows.dtype)
    own = jax.ShapeDtypeStruct((target_rows.shape[0],) + tile, rows.dtype)
    hbm = pl.BlockSpec(memory_space=pltpu.HBM)
    anywhere = pl.BlockSpec(memory_space=pl.ANY)
    return pl.pallas_call(
        pick_kernel,
        out_shape=(outgoing, own),
        in_specs=[anywhere, anywhere, hbm],
        out_specs=(hbm, hbm),
        scratch_shapes=[
            pltpu.SMEM(served.shape, jnp.int32),
            pltpu.SMEM(target_rows.shape, jnp.int32),
            pltpu.VMEM(rows.shape, rows.dtype),
            pltpu.VMEM(outgoing.shape, rows.dtype),
            pltpu.VMEM(own.shape, rows.dtype),
            pltpu.SemaphoreType.DMA((8,)),
        ],
        compiler_params=GRANT,
        name="pick",
    )(served, target_rows, rows)


def finish_kernel(
    source, blocks, arrived, own, shares, hidden_bias, output_weight, output_bias, *rest,
):
    mine, other = rest[:4], rest[4:8]
    embedding, spread, live_rows, own_rows, pooled, held_hidden, held_output, sems = rest[8:]
    chunks = arrived.shape[1]
    targets, width = own_rows.shape
    half, side = mine[0].shape[2:]
    copies = []
    for far, parts in enumerate((mine, other)):
        for second, part in enumerate(parts):
            for first in range(part.shape[0]):
                at = 16 * far + 4 * second + first
                rows = pl.ds(pl.multiple_of(blocks[0, at] * half, half), half)
                columns = pl.ds(pl.multiple_of(blocks[1, at] * side, side), side)
                copies.append(
                    pltpu.make_async_copy(part.at[first, 0], held_hidden.at[rows, columns], sems.at[at])
                )
    copies.append(pltpu.make_async_copy(output_weight, held_output, sems.at[32]))
    for copy in copies:
        copy.start()

    def group(g, carry):
        for row in range(16):
            j = g * 16 + row
            place = pl.multiple_of(j * chunks, chunks)
            spread[pl.ds(place, chunks), :] = arrived[source[j]].astype(jnp.float32)
        return carry

    lax.fori_loop(0, LIVE // 16, group, 0)
    for chunk in range(chunks):
        part = spread[pl.ds(chunk, LIVE, stride=chunks), :]
        live_rows[:, pl.ds(chunk * LANES, LANES)] = part.astype(jnp.bfloat16)
    spread[pl.ds(0, targets * chunks), :] = own[...].astype(jnp.float32).reshape(targets * chunks, LANES)
    for chunk in range(chunks):
        part = spread[pl.ds(chunk, targets, stride=chunks), :]
        own_rows[:, pl.ds(chunk * LANES, LANES)] = part.astype(jnp.bfloat16)

    share = shares[...]
    high = jnp.floor(share * (1.0 / 64.0))
    low = share - high * 64.0
    parts = jnp.concatenate([high, low], axis=0).astype(jnp.bfloat16)
    total = jnp.sum(share, axis=1, keepdims=True)
    for copy in copies[:-1]:
        copy.wait()

    def block(n, carry):
        columns = pl.ds(pl.multiple_of(n * BLOCK, BLOCK), BLOCK)
        product = jnp.dot(live_rows[...], held_hidden[:, columns], preferred_element_type=jnp.float32)
        hidden = jnp.maximum(product + hidden_bias[:, columns], 0.0).astype(jnp.bfloat16)
        both = jnp.dot(parts, hidden, preferred_element_type=jnp.float32)
        summed = both[:targets] * 64.0 + both[targets:]
        pooled[:, columns] = (summed / total).astype(jnp.bfloat16)
        return carry

    lax.fori_loop(0, held_hidden.shape[1] // BLOCK, block, 0)
    copies[-1].wait()
    combined = jnp.dot(own_rows[...], held_output[:width], preferred_element_type=jnp.float32)
    combined += jnp.dot(pooled[...], held_output[width:], preferred_element_type=jnp.float32)
    combined = jnp.maximum(combined + output_bias[...], 0.0)
    scale = lax.rsqrt(jnp.mean(combined * combined, axis=1, keepdims=True) + 1e-06)
    embedding[...] = (combined * scale).astype(jnp.bfloat16)


def finish(source, blocks, arrived, own, shares, hidden_bias, output_weight, output_bias, mine, other):
    chunks = arrived.shape[1]
    targets = own.shape[0]
    hidden = hidden_bias.shape[0]
    width = chunks * LANES
    vmem = pl.BlockSpec(memory_space=pltpu.VMEM)
    smem = pl.BlockSpec(memory_space=pltpu.SMEM)
    hbm = pl.BlockSpec(memory_space=pltpu.HBM)
    return pl.pallas_call(
        finish_kernel,
        out_shape=jax.ShapeDtypeStruct((targets, output_weight.shape[1]), jnp.bfloat16),
        in_specs=[smem, smem, vmem, vmem, vmem, vmem, hbm, vmem] + [hbm] * 8,
        out_specs=vmem,
        scratch_shapes=[
            pltpu.VMEM((LIVE * chunks, LANES), jnp.float32),
            pltpu.VMEM((LIVE, width), jnp.bfloat16),
            pltpu.VMEM((targets, width), jnp.bfloat16),
            pltpu.VMEM((targets, hidden), jnp.bfloat16),
            pltpu.VMEM((width, hidden), jnp.bfloat16),
            pltpu.VMEM(output_weight.shape, jnp.bfloat16),
            pltpu.SemaphoreType.DMA((33,)),
        ],
        compiler_params=GRANT,
        name="finish",
    )(
        source, blocks, arrived, own, shares, hidden_bias.reshape(1, -1), output_weight,
        output_bias.reshape(1, -1), *mine, *other,
    )


def plan(neighbour_slot, counts, peers, capacity):
    owner, slot = neighbour_slot // capacity, neighbour_slot % capacity
    same = owner[:, :, None] == jnp.arange(peers, dtype=jnp.int32)
    used = jnp.max(jnp.where(same, slot[:, :, None] + 1, 0), axis=(0, 1))
    before = jnp.arange(peers)[:, None] < jnp.arange(peers)[None, :]
    start = jnp.sum(jnp.where(before, used[:, None], 0), axis=0)
    place = jnp.sum(jnp.where(same, start, 0), axis=2) + slot
    live = jnp.arange(LIVE, dtype=jnp.int32)
    hit = place[:, :, None] == live
    shares = jnp.sum(jnp.where(hit, counts[:, :, None], 0), axis=1).astype(jnp.float32)
    within = (start <= live[:, None]) & (live[:, None] < start + used)
    first = jnp.arange(peers, dtype=jnp.int32) * capacity - start
    source = jnp.sum(jnp.where(within, first, 0), axis=1) + live
    return source, shares


def shifted(x, second, by):
    pairs = []
    for dom in range(8):
        for grp in range(16):
            row, column = grp // 4, grp % 4
            if (dom % 2 == 0) != second:
                row = (row + by) % 4
            else:
                column = (column + by) % 4
            pairs.append((dom * 16 + grp, dom * 16 + row * 4 + column))
    return lax.ppermute(x, AXES, pairs)


def own_half(weight):
    halves = weight.reshape(2, 1, weight.shape[0] // 2, weight.shape[1])
    return jnp.where(lax.axis_index("dom") % 2 == 0, halves[:1], halves[1:])


def block_places():
    core = lax.axis_index("dom") % 2
    row, column = lax.axis_index("grp") // 4, lax.axis_index("grp") % 4
    back = jnp.array(SHIFTS, jnp.int32)
    rows, columns = (row - back) % 4, (column - back) % 4
    of_core0 = (rows[None, :] * 4 + columns[:, None]).reshape(-1)
    of_core1 = (rows[:, None] * 4 + columns[None, :]).reshape(-1)
    same, across = jnp.where(core == 0, of_core0, of_core1), jnp.where(core == 0, of_core1, of_core0)
    half = jnp.repeat(jnp.stack([core, 1 - core]), 16)
    return jnp.stack([half, jnp.concatenate([same, across])]).astype(jnp.int32)


def on_device(
    features,
    requests,
    target_rows,
    neighbour_slot,
    counts,
    hidden_weight,
    hidden_bias,
    output_weight,
    output_bias,
):
    _, peers, capacity = requests.shape
    served = lax.all_to_all(requests.reshape(peers, 1, capacity), AXES, split_axis=0, concat_axis=0, tiled=True)
    own_part = own_half(hidden_weight)
    near = [own_part] + [shifted(own_part, False, by) for by in SHIFTS[1:]]
    rows = relayout(features)
    near = jnp.concatenate(near, axis=0)
    rows, near = lax.optimization_barrier((rows, near))
    mine = [near] + [shifted(near, True, by) for by in SHIFTS[1:]]
    outgoing, own = pick(served, target_rows, rows)
    tile = outgoing.shape[1:]
    blocks = outgoing.reshape(peers, capacity * tile[0], tile[1])
    blocks, neighbour_slot, counts, mine = lax.optimization_barrier((blocks, neighbour_slot, counts, mine))
    arrived = lax.all_to_all(blocks, AXES, split_axis=0, concat_axis=0, tiled=True)
    other = [lax.ppermute(part, "dom", [(dom, dom ^ 1) for dom in range(8)]) for part in mine]
    places = block_places()
    source, shares = plan(neighbour_slot, counts, peers, capacity)
    return finish(
        source, places, arrived.reshape((peers * capacity,) + tile), own, shares, hidden_bias, output_weight,
        output_bias, mine, other,
    )


def solution(mesh):
    placed = (
        P(AXES, None),
        P(AXES, None, None),
        P(AXES),
        P(AXES, None),
        P(AXES, None),
        P(None, "grp"),
        P(),
        P(),
        P(),
    )
    return jax.shard_map(on_device, mesh=mesh, in_specs=placed, out_specs=P(AXES, None), check_vma=False)
```

time: 170 us -> 110 us (0.65)
  local copies, waits for them, and re-layouts: 53.6 us -> 4.32 us
  Pallas kernels: 0 us -> 27.1 us
  matrix products: 19.6 us -> 0 us
  waiting for transfers between devices: 54.2 us -> 35.6 us
  between operations: 13.6 us -> 0.38 us
  starting transfers between devices: 5.66 us -> 16.6 us
  other arithmetic: 1.8 us -> 6.16 us
  blocking collectives: 20.9 us -> 19.1 us
    gather x4 -> x0, local copies, waits for them, and re-layouts: 44.8 us -> none  [the longest x2 26.8 us: on_device(): picked = hidden_rows[neighbour_slot]]
    pallas_call x0 -> x3, Pallas kernels: none -> 27.1 us  [the longest x1 12.9 us: finish(): pl.pallas_call(finish_kernel, out_shape=jax.ShapeDtypeStruct((targets, ou...]
    dot_general x3 -> x0, matrix products: 19.6 us -> none  [the longest x1 11.3 us: transform(): jnp.dot(rows, lax.all_gather(hidden_weight, 'grp', axis=1, tiled=True), p...]
    all_to_all x1, waiting for transfers between devices: 50.3 us -> 32.9 us  [on_device(): lax.all_to_all(blocks, AXES, split_axis=0, concat_axis=0, tiled=True)]
    ppermute x0 -> x10, starting transfers between devices: none -> 12.2 us  [the longest x6 10.4 us: shifted(): return lax.ppermute(x, AXES, pairs)]
    reshape x3 -> x0, local copies, waits for them, and re-layouts: 7.38 us -> none  [the longest x1 4.26 us: on_device(): arrived = arrived.reshape(peers * capacity, payload)]
    unnamed x10 -> x25, local copies, waits for them, and re-layouts: 0.03 us -> 3.82 us
    all_gather x1 -> x0, waiting for transfers between devices: 3.28 us -> none  [transform(): lax.all_gather(hidden_weight, 'grp', axis=1, tiled=True)]
  transfers between devices with their start and end apart: 2 -> 11, of which waited for: 2 -> 4; matrix products, arithmetic and copies ran while one was open for 16% -> 5% of each run, Pallas kernels for 0% -> 13%
where the time goes in v1:
time: 110 us; the launch traced here: 109 us
  waiting for transfers between devices  35.6 us (32%)
  Pallas kernels  27.1 us (25%)
  blocking collectives  19.1 us (17%)
  starting transfers between devices  16.6 us (15%)
  other arithmetic  6.16 us (6%)
  local copies, waits for them, and re-layouts  4.32 us (4%)
    all_to_all x1, waiting for transfers between devices, on_device(): lax.all_to_all(blocks, AXES, split_axis=0, concat_axis=0, tiled=True)  32.9 us
    all_to_all x1, blocking collectives, on_device(): lax.all_to_all(requests.reshape(peers, 1, capacity), AXES, split_axis=0,...  19.1 us
    pallas_call x1, Pallas kernels, finish(): pl.pallas_call(finish_kernel, out_shape=jax.ShapeDtypeStruct((targets, ou...  12.9 us
    ppermute x6, starting transfers between devices, shifted(): return lax.ppermute(x, AXES, pairs)  10.4 us
    pallas_call x1, Pallas kernels, relayout(): pl.pallas_call(relayout_kernel, out_shape=jax.ShapeDtypeStruct((count, ch...  7.29 us
    pallas_call x1, Pallas kernels, pick(): pl.pallas_call(pick_kernel, out_shape=(outgoing, own), in_specs=[anywhere...  6.84 us
    all_to_all x1, starting transfers between devices, on_device(): lax.all_to_all(blocks, AXES, split_axis=0, concat_axis=0, tiled=True)  4.46 us
    unnamed x25, local copies, waits for them, and re-layouts  3.82 us
  transfers between devices with their start and end apart: 11, of which 4 were waited for; matrix products, arithmetic and copies ran while one was open for 5% of the time, Pallas kernels for 13%

profile of v1, /device:TPU:1, one launch (start us, length us, event | category | flops | bytes accessed | tf_op | source)
XLA Modules:
  0.0 109.3 jit_solution(15487232904159954322)
XLA Ops:
  0.0 1.0 select_bitcast_fusion
  1.0 4.5 %collective-permute-start.2 = (bf16[1,1,512,128]{3,2,1,0:T(8,128)(2,1)S(1)}, bf16[1,1,512,128]{3,2,1,0:T(8,128)(2,1)S(1)}, u32[]{:S(2)}, u32[]{:S(2)}) collective-permute-start(bf16[1,1,512,128]{3,2,1,0:T(8,128)(2,1)S(1)} %select_bitcast_fusion), channel_id=1, source_target_pairs={{0,8},{1,9},{2,10},{3,11},{4,12},{5,13},{6,14},{7,15},{8,0},{9,1},... | collective-permute-start | bytes 393224 | tf_op jit(solution)/shard_map/ppermute | solution.py:250
  5.9 1.0 collective-permute-start
  7.0 7.3 %relayout.1.rows = bf16[4096,8,128]{2,1,0:T(8,128)(2,1)} custom-call(bf16[4096,1024]{1,0:T(8,128)(2,1)} %features.1), custom_call_target="tpu_custom_call" | custom-call | tf_op jit(solution)/shard_map/relayout/pallas_call | solution.py:51
  14.4 3.0 %collective-permute-start.5 = (bf16[4,1,512,128]{3,2,1,0:T(8,128)(2,1)S(1)}, bf16[4,1,512,128]{3,2,1,0:T(8,128)(2,1)S(1)}, u32[]{:S(2)}, u32[]{:S(2)}) collective-permute-start(bf16[4,1,512,128]{3,2,1,0:T(8,128)(2,1)S(1)} %pad_maximum_fusion.rest_0_), channel_id=1, source_target_pairs={{0,2},{1,3},{2,0},{3,1},{4,6},{5,7},{6,4},{7,5},{8,10},{9,11},{10,... | collective-permute-start | bytes 1572872 | tf_op jit(solution)/shard_map/ppermute | solution.py:250
  17.4 0.8 collective-permute-start.4
  18.2 0.7 collective-permute-start.3
  19.0 19.1 %all_to_all.10.served = s32[128,1,13]{2,1,0:T(1,128)} all-to-all(s32[128,1,13]{2,1,0:T(1,128)S(1)} %bitcast.13), channel_id=1, replica_groups=mesh['dom'=8,'grp'=16] {'dom','grp'}, dimensions={0} | all-to-all | bytes 13312 | tf_op jit(solution)/shard_map/all_to_all | solution.py:282
  38.1 6.8 %pick.1 = (bf16[1664,8,128]{2,1,0:T(8,128)(2,1)}, bf16[32,8,128]{2,1,0:T(8,128)(2,1)}) custom-call(s32[128,1,13]{2,1,0:T(1,128)} %all_to_all.10.served, s32[32]{0:T(128)} %target_rows.1, bf16[4096,8,128]{2,1,0:T(8,128)(2,1)} %relayout.1.rows), custom_call_target="tpu_custom_call" | custom-call | tf_op jit(solution)/shard_map/pick/pallas_call | solution.py:112
  45.0 0.8 copy-done.2
  46.2 4.5 %all-to-all-start.1 = ((bf16[128,104,128]{2,1,0:T(8,128)(2,1)}), bf16[128,104,128]{2,1,0:T(8,128)(2,1)S(1)}, u32[]{:S(2)}, u32[]{:S(2)}) async-start(bf16[128,104,128]{2,1,0:T(8,128)(2,1)} %bitcast.12), calls=%async_computation.1 | async-start | bytes 6815744 | tf_op jit(solution)/shard_map/all_to_all | solution.py:293
  51.2 0.6 pad_add_fusion.blocks
  52.0 0.6 select_reduce_fusion.2
  52.8 1.2 %select_reduce_fusion.1 = s32[32,50]{0,1:T(8,128)S(1)} fusion(s32[128]{0:T(128)S(1)} %select_reduce_fusion.4, s32[32,50]{0,1:T(8,128)S(1)} %get-tuple-element.27), kind=kLoop, calls=%fused_computation.2 | loop fusion | flops 612800 | bytes 13312 | tf_op jit(solution)/shard_map/reduce_sum | solution.py:230
  54.0 0.9 select_reduce_fusion
  54.8 0.7 convert_element_type.3.shares
  55.5 1.2 %collective-permute-start.6 = (bf16[4,1,512,128]{3,2,1,0:T(8,128)(2,1)}, bf16[4,1,512,128]{3,2,1,0:T(8,128)(2,1)S(1)}, u32[]{:S(2)}, u32[]{:S(2)}) collective-permute-start(bf16[4,1,512,128]{3,2,1,0:T(8,128)(2,1)} %copy-done.1), channel_id=1, source_target_pairs={{0,16},{16,0},{32,48},{48,32},{64,80},{80,64},{96,112},{112,96},{1... | collective-permute-start | bytes 1572872 | tf_op jit(solution)/shard_map/ppermute | solution.py:294
  57.4 0.6 iota_add_fusion.source
  58.4 1.5 %collective-permute-done.7.rest_5_ = bf16[4,1,512,128]{3,2,1,0:T(8,128)(2,1)S(1)} collective-permute-done((bf16[4,1,512,128]{3,2,1,0:T(8,128)(2,1)}, bf16[4,1,512,128]{3,2,1,0:T(8,128)(2,1)S(1)}, u32[]{:S(2)}, u32[]{:S(2)}) %collective-permute-start.7) | collective-permute-done | bytes 524320 | tf_op jit(solution)/shard_map/ppermute | solution.py:294
  59.9 0.7 collective-permute-done.8.rest_6_
  60.7 0.8 copy-done.7
  61.5 32.9 %all-to-all-done.1 = bf16[128,104,128]{2,1,0:T(8,128)(2,1)S(1)} async-done(((bf16[128,104,128]{2,1,0:T(8,128)(2,1)}), bf16[128,104,128]{2,1,0:T(8,128)(2,1)S(1)}, u32[]{:S(2)}, u32[]{:S(2)}) %all-to-all-start.1) | async-done | bytes 3407904 | tf_op jit(solution)/shard_map/all_to_all | solution.py:293
  94.5 1.7 %copy-done = bf16[128,104,128]{2,1,0:T(8,128)(2,1)} copy-done((bf16[128,104,128]{2,1,0:T(8,128)(2,1)}, bf16[128,104,128]{2,1,0:T(8,128)(2,1)S(1)}, u32[]{:S(2)}) %copy-start) | copy-done | bytes 3407896
  96.2 12.9 %finish.1 = bf16[32,1024]{1,0:T(8,128)(2,1)} custom-call(s32[800]{0:T(1024)} %iota_add_fusion.source, s32[2,32]{1,0:T(2,128)} %pad_add_fusion.blocks, bf16[1664,8,128]{2,1,0:T(8,128)(2,1)} %bitcast.11, bf16[32,8,128]{2,1,0:T(8,128)(2,1)} %get-tuple-element.21.own, f32[32,800]{1,0:T(8,128)} %convert_element_type.3.shares, f32[1,2048]{1,0:T(1,128)} %bitcast.14, ...), custom_call_target="tpu_custom_call" | custom-call | tf_op jit(solution)/shard_map/finish/pallas_call | solution.py:202
  (50 shorter events, 3.1 us)
Async XLA Ops:
  1.0 17.9 %copy-start.10 = (s32[1,128,13]{1,0,2:T(1,128)S(1)}, s32[1,128,13]{1,0,2:T(1,128)}, u32[]{:S(2)}) copy-start(s32[1,128,13]{1,0,2:T(1,128)} %param.11) | copy-start | bytes 19972
  1.0 13.3 %collective-permute-start.2 = (bf16[1,1,512,128]{3,2,1,0:T(8,128)(2,1)S(1)}, bf16[1,1,512,128]{3,2,1,0:T(8,128)(2,1)S(1)}, u32[]{:S(2)}, u32[]{:S(2)}) collective-permute-start(bf16[1,1,512,128]{3,2,1,0:T(8,128)(2,1)S(1)} %select_bitcast_fusion), channel_id=1, source_target_pairs={{0,8},{1,9},{2,10},{3,11},{4,12},{5,13},{6,14},{7,15},{8,0},{9,1},... | collective-permute-start | bytes 393224 | tf_op jit(solution)/shard_map/ppermute | solution.py:250
  5.5 8.8 %collective-permute-start.1 = (bf16[1,1,512,128]{3,2,1,0:T(8,128)(2,1)S(1)}, bf16[1,1,512,128]{3,2,1,0:T(8,128)(2,1)S(1)}, u32[]{:S(2)}, u32[]{:S(2)}) collective-permute-start(bf16[1,1,512,128]{3,2,1,0:T(8,128)(2,1)S(1)} %select_bitcast_fusion), channel_id=1, source_target_pairs={{0,12},{1,13},{2,14},{3,15},{4,0},{5,1},{6,2},{7,3},{8,4},{9,5},{1... | collective-permute-start | bytes 393224 | tf_op jit(solution)/shard_map/ppermute | solution.py:250
  5.9 8.4 %collective-permute-start = (bf16[1,1,512,128]{3,2,1,0:T(8,128)(2,1)S(1)}, bf16[1,1,512,128]{3,2,1,0:T(8,128)(2,1)S(1)}, u32[]{:S(2)}, u32[]{:S(2)}) collective-permute-start(bf16[1,1,512,128]{3,2,1,0:T(8,128)(2,1)S(1)} %select_bitcast_fusion), channel_id=1, source_target_pairs={{0,4},{1,5},{2,6},{3,7},{4,8},{5,9},{6,10},{7,11},{8,12},{9,13},{1... | collective-permute-start | bytes 393224 | tf_op jit(solution)/shard_map/ppermute | solution.py:250
  14.4 30.6 %copy-start.1 = (bf16[4,1,512,128]{3,2,1,0:T(8,128)(2,1)}, bf16[4,1,512,128]{3,2,1,0:T(8,128)(2,1)S(1)}, u32[]{:S(2)}) copy-start(bf16[4,1,512,128]{3,2,1,0:T(8,128)(2,1)S(1)} %pad_maximum_fusion.rest_0_) | copy-start | bytes 1572868
  14.4 30.6 %collective-permute-start.5 = (bf16[4,1,512,128]{3,2,1,0:T(8,128)(2,1)S(1)}, bf16[4,1,512,128]{3,2,1,0:T(8,128)(2,1)S(1)}, u32[]{:S(2)}, u32[]{:S(2)}) collective-permute-start(bf16[4,1,512,128]{3,2,1,0:T(8,128)(2,1)S(1)} %pad_maximum_fusion.rest_0_), channel_id=1, source_target_pairs={{0,2},{1,3},{2,0},{3,1},{4,6},{5,7},{6,4},{7,5},{8,10},{9,11},{10,... | collective-permute-start | bytes 1572872 | tf_op jit(solution)/shard_map/ppermute | solution.py:250
  17.4 27.6 %collective-permute-start.4 = (bf16[4,1,512,128]{3,2,1,0:T(8,128)(2,1)S(1)}, bf16[4,1,512,128]{3,2,1,0:T(8,128)(2,1)S(1)}, u32[]{:S(2)}, u32[]{:S(2)}) collective-permute-start(bf16[4,1,512,128]{3,2,1,0:T(8,128)(2,1)S(1)} %pad_maximum_fusion.rest_0_), channel_id=1, source_target_pairs={{0,3},{1,0},{2,1},{3,2},{4,7},{5,4},{6,5},{7,6},{8,11},{9,8},{10,9... | collective-permute-start | bytes 1572872 | tf_op jit(solution)/shard_map/ppermute | solution.py:250
  18.2 26.8 %collective-permute-start.3 = (bf16[4,1,512,128]{3,2,1,0:T(8,128)(2,1)S(1)}, bf16[4,1,512,128]{3,2,1,0:T(8,128)(2,1)S(1)}, u32[]{:S(2)}, u32[]{:S(2)}) collective-permute-start(bf16[4,1,512,128]{3,2,1,0:T(8,128)(2,1)S(1)} %pad_maximum_fusion.rest_0_), channel_id=1, source_target_pairs={{0,1},{1,2},{2,3},{3,0},{4,5},{5,6},{6,7},{7,4},{8,9},{9,10},{10,1... | collective-permute-start | bytes 1572872 | tf_op jit(solution)/shard_map/ppermute | solution.py:250
  38.1 12.8 %copy-start.11 = (s32[4]{0:T(128)S(1)}, s32[4]{0:T(128)}, u32[]{:S(2)}) copy-start(s32[4]{0:T(128)} %constant.90) | copy-start | bytes 52
  38.1 13.7 %copy-start.8 = (s32[32,50]{1,0:T(8,128)S(1)}, s32[32,50]{1,0:T(8,128)}, u32[]{:S(2)}) copy-start(s32[32,50]{1,0:T(8,128)} %param.13) | copy-start | bytes 19204
  38.1 13.8 %copy-start.9 = (s32[32,50]{1,0:T(8,128)S(1)}, s32[32,50]{1,0:T(8,128)}, u32[]{:S(2)}) copy-start(s32[32,50]{1,0:T(8,128)} %param.14) | copy-start | bytes 19204
  45.0 0.8 copy-start.2
  45.0 1.0 copy-start.3
  45.0 1.1 %copy-start.4 = (bf16[4,1,512,128]{3,2,1,0:T(8,128)(2,1)}, bf16[4,1,512,128]{3,2,1,0:T(8,128)(2,1)S(1)}, u32[]{:S(2)}) copy-start(bf16[4,1,512,128]{3,2,1,0:T(8,128)(2,1)S(1)} %collective-permute-done.3.rest_1_) | copy-start | bytes 1572868
  46.2 48.3 %all-to-all-start.1 = ((bf16[128,104,128]{2,1,0:T(8,128)(2,1)}), bf16[128,104,128]{2,1,0:T(8,128)(2,1)S(1)}, u32[]{:S(2)}, u32[]{:S(2)}) async-start(bf16[128,104,128]{2,1,0:T(8,128)(2,1)} %bitcast.12), calls=%async_computation.1 | async-start | bytes 6815744 | tf_op jit(solution)/shard_map/all_to_all | solution.py:293
  55.5 3.0 %collective-permute-start.6 = (bf16[4,1,512,128]{3,2,1,0:T(8,128)(2,1)}, bf16[4,1,512,128]{3,2,1,0:T(8,128)(2,1)S(1)}, u32[]{:S(2)}, u32[]{:S(2)}) collective-permute-start(bf16[4,1,512,128]{3,2,1,0:T(8,128)(2,1)} %copy-done.1), channel_id=1, source_target_pairs={{0,16},{16,0},{32,48},{48,32},{64,80},{80,64},{96,112},{112,96},{1... | collective-permute-start | bytes 1572872 | tf_op jit(solution)/shard_map/ppermute | solution.py:294
  56.7 3.2 %collective-permute-start.7 = (bf16[4,1,512,128]{3,2,1,0:T(8,128)(2,1)}, bf16[4,1,512,128]{3,2,1,0:T(8,128)(2,1)S(1)}, u32[]{:S(2)}, u32[]{:S(2)}) collective-permute-start(bf16[4,1,512,128]{3,2,1,0:T(8,128)(2,1)} %copy-done.4), channel_id=1, source_target_pairs={{0,16},{16,0},{32,48},{48,32},{64,80},{80,64},{96,112},{112,96},{1... | collective-permute-start | bytes 1572872 | tf_op jit(solution)/shard_map/ppermute | solution.py:294
  56.7 4.0 %collective-permute-start.8 = (bf16[4,1,512,128]{3,2,1,0:T(8,128)(2,1)}, bf16[4,1,512,128]{3,2,1,0:T(8,128)(2,1)S(1)}, u32[]{:S(2)}, u32[]{:S(2)}) collective-permute-start(bf16[4,1,512,128]{3,2,1,0:T(8,128)(2,1)} %copy-done.3), channel_id=1, source_target_pairs={{0,16},{16,0},{32,48},{48,32},{64,80},{80,64},{96,112},{112,96},{1... | collective-permute-start | bytes 1572872 | tf_op jit(solution)/shard_map/ppermute | solution.py:294
  57.2 4.3 %collective-permute-start.9 = (bf16[4,1,512,128]{3,2,1,0:T(8,128)(2,1)}, bf16[4,1,512,128]{3,2,1,0:T(8,128)(2,1)}, u32[]{:S(2)}, u32[]{:S(2)}) collective-permute-start(bf16[4,1,512,128]{3,2,1,0:T(8,128)(2,1)} %copy-done.2), channel_id=1, source_target_pairs={{0,16},{16,0},{32,48},{48,32},{64,80},{80,64},{96,112},{112,96},{1... | collective-permute-start | bytes 1572872 | tf_op jit(solution)/shard_map/ppermute | solution.py:294
  58.4 2.3 %copy-start.5 = (bf16[4,1,512,128]{3,2,1,0:T(8,128)(2,1)}, bf16[4,1,512,128]{3,2,1,0:T(8,128)(2,1)S(1)}, u32[]{:S(2)}) copy-start(bf16[4,1,512,128]{3,2,1,0:T(8,128)(2,1)S(1)} %collective-permute-done.6.rest_4_) | copy-start | bytes 1572868
  59.9 0.8 copy-start.6
  60.7 0.8 copy-start.7
  94.5 1.7 %copy-start = (bf16[128,104,128]{2,1,0:T(8,128)(2,1)}, bf16[128,104,128]{2,1,0:T(8,128)(2,1)S(1)}, u32[]{:S(2)}) copy-start(bf16[128,104,128]{2,1,0:T(8,128)(2,1)S(1)} %all-to-all-done.1) | copy-start | bytes 10223620

commit v2 on v1

--- a/solution.py
+++ b/solution.py
@@ -10,10 +10,18 @@
 LIVE = 800
 LANES = 128
 ROWS_AT_ONCE = 256
-BLOCK = 256
+BLOCK = 512
 AXES = ("dom", "grp")
 SHIFTS = (0, 1, 3, 2)
-GRANT = pltpu.CompilerParams(vmem_limit_bytes=60 * 2**20)
+GRANT = pltpu.CompilerParams(vmem_limit_bytes=32 * 2**20)
+
+
+def takes(microseconds):
+    return pl.CostEstimate(flops=int(microseconds * 1.15e9), bytes_accessed=1, transcendentals=0)
+
+
+def in_hbm(x):
+    return pltpu.with_memory_space_constraint(x, pltpu.HBM)
 
 
 def relayout_kernel(features, rows, held, spread, out, in_sems, out_sems):
@@ -50,7 +58,7 @@
     hbm = pl.BlockSpec(memory_space=pltpu.HBM)
     return pl.pallas_call(
         relayout_kernel,
-        out_shape=jax.ShapeDtypeStruct((count, chunks, LANES), jnp.bfloat16),
+        out_shape=pltpu.HBM((count, chunks, LANES), jnp.bfloat16),
         in_specs=[hbm],
         out_specs=hbm,
         scratch_shapes=[
@@ -61,8 +69,9 @@
             pltpu.SemaphoreType.DMA((steps,)),
         ],
         compiler_params=GRANT,
+        cost_estimate=takes(7),
         name="relayout",
-    )(features)
+    )(in_hbm(features))
 
 
 def pick_kernel(served, target_rows, rows, outgoing, own, index, own_index, all_rows, held, held_own, sems):
@@ -105,8 +114,8 @@
 def pick(served, target_rows, rows):
     peers, _, capacity = served.shape
     tile = rows.shape[1:]
-    outgoing = jax.ShapeDtypeStruct((peers * capacity,) + tile, rows.dtype)
-    own = jax.ShapeDtypeStruct((target_rows.shape[0],) + tile, rows.dtype)
+    outgoing = pltpu.HBM((peers * capacity,) + tile, rows.dtype)
+    own = pltpu.HBM((target_rows.shape[0],) + tile, rows.dtype)
     hbm = pl.BlockSpec(memory_space=pltpu.HBM)
     anywhere = pl.BlockSpec(memory_space=pl.ANY)
     return pl.pallas_call(
@@ -118,13 +127,14 @@
             pltpu.SMEM(served.shape, jnp.int32),
             pltpu.SMEM(target_rows.shape, jnp.int32),
             pltpu.VMEM(rows.shape, rows.dtype),
-            pltpu.VMEM(outgoing.shape, rows.dtype),
-            pltpu.VMEM(own.shape, rows.dtype),
+            pltpu.VMEM((peers * capacity,) + tile, rows.dtype),
+            pltpu.VMEM((target_rows.shape[0],) + tile, rows.dtype),
             pltpu.SemaphoreType.DMA((8,)),
         ],
         compiler_params=GRANT,
+        cost_estimate=takes(2),
         name="pick",
-    )(served, target_rows, rows)
+    )(served, target_rows, in_hbm(rows))
 
 
 def finish_kernel(
@@ -216,8 +226,9 @@
         compiler_params=GRANT,
         name="finish",
     )(
-        source, blocks, arrived, own, shares, hidden_bias.reshape(1, -1), output_weight,
-        output_bias.reshape(1, -1), *mine, *other,
+        source, blocks, pltpu.with_memory_space_constraint(arrived, pltpu.VMEM), own, shares,
+        hidden_bias.reshape(1, -1), in_hbm(output_weight), output_bias.reshape(1, -1),
+        *[in_hbm(part) for part in mine + other],
     )
 
 
@@ -284,7 +295,6 @@
     near = [own_part] + [shifted(own_part, False, by) for by in SHIFTS[1:]]
     rows = relayout(features)
     near = jnp.concatenate(near, axis=0)
-    rows, near = lax.optimization_barrier((rows, near))
     mine = [near] + [shifted(near, True, by) for by in SHIFTS[1:]]
     outgoing, own = pick(served, target_rows, rows)
     tile = outgoing.shape[1:]

time: 110 us -> 102 us (0.927)
  blocking collectives: 19.1 us -> 0 us
  starting transfers between devices: 16.6 us -> 31 us
  Pallas kernels: 27.1 us -> 23.9 us
  other arithmetic: 6.16 us -> 4.35 us
  waiting for transfers between devices: 35.6 us -> 37.2 us
    all_to_all x1 -> x0, blocking collectives: 19.1 us -> none  [on_device(): lax.all_to_all(requests.reshape(peers, 1, capacity), AXES, split_axis=0,...]
    all_to_all x0 -> x1, starting transfers between devices: none -> 9.9 us  [on_device(): lax.all_to_all(requests.reshape(peers, 1, capacity), AXES, split_axis=0,...]
    all_to_all x1, starting transfers between devices: 4.46 us -> 8.98 us  [on_device(): lax.all_to_all(blocks, AXES, split_axis=0, concat_axis=0, tiled=True)]
    pallas_call x1, Pallas kernels: 12.9 us -> 9.75 us  [finish(): pl.pallas_call(finish_kernel, out_shape=jax.ShapeDtypeStruct((targets, ou...]
    all_to_all x1, waiting for transfers between devices: 32.9 us -> 34.1 us  [on_device(): lax.all_to_all(blocks, AXES, split_axis=0, concat_axis=0, tiled=True)]
    unnamed x25 -> x29, local copies, waits for them, and re-layouts: 3.82 us -> 4.29 us
  transfers between devices with their start and end apart: 11 -> 12, of which waited for: 4 -> 4; matrix products, arithmetic and copies ran while one was open for 5% -> 5% of each run, Pallas kernels for 13% -> 14%
where the time goes in v2:
time: 102 us
  waiting for transfers between devices  37.2 us (36%)
  starting transfers between devices  31 us (30%)
  Pallas kernels  23.9 us (23%)
  local copies, waits for them, and re-layouts  4.79 us (5%)
  other arithmetic  4.35 us (4%)
    all_to_all x1, waiting for transfers between devices, on_device(): lax.all_to_all(blocks, AXES, split_axis=0, concat_axis=0, tiled=True)  34.1 us
    ppermute x6, starting transfers between devices, shifted(): return lax.ppermute(x, AXES, pairs)  10.4 us
    all_to_all x1, starting transfers between devices, on_device(): lax.all_to_all(requests.reshape(peers, 1, capacity), AXES, split_axis=0,...  9.9 us
    pallas_call x1, Pallas kernels, finish(): pl.pallas_call(finish_kernel, out_shape=jax.ShapeDtypeStruct((targets, ou...  9.75 us
    all_to_all x1, starting transfers between devices, on_device(): lax.all_to_all(blocks, AXES, split_axis=0, concat_axis=0, tiled=True)  8.98 us
    pallas_call x1, Pallas kernels, relayout(): pl.pallas_call(relayout_kernel, out_shape=pltpu.HBM((count, chunks, LANES...  7.31 us
    pallas_call x1, Pallas kernels, pick(): pl.pallas_call(pick_kernel, out_shape=(outgoing, own), in_specs=[anywhere...  6.8 us
    unnamed x29, local copies, waits for them, and re-layouts  4.29 us
  transfers between devices with their start and end apart: 12, of which 4 were waited for; matrix products, arithmetic and copies ran while one was open for 5% of the time, Pallas kernels for 14%

profile of v2, /device:TPU:1, one launch (start us, length us, event | category | flops | bytes accessed | tf_op | source)
XLA Modules:
  0.0 101.7 jit_solution(3796902241814145292)
XLA Ops:
  0.0 1.0 select_bitcast_fusion
  1.0 4.5 %collective-permute-start.2 = (bf16[1,1,512,128]{3,2,1,0:T(8,128)(2,1)S(1)}, bf16[1,1,512,128]{3,2,1,0:T(8,128)(2,1)S(1)}, u32[]{:S(2)}, u32[]{:S(2)}) collective-permute-start(bf16[1,1,512,128]{3,2,1,0:T(8,128)(2,1)S(1)} %select_bitcast_fusion), channel_id=1, source_target_pairs={{0,8},{1,9},{2,10},{3,11},{4,12},{5,13},{6,14},{7,15},{8,0},{9,1},... | collective-permute-start | bytes 393224 | tf_op jit(solution)/shard_map/ppermute | solution.py:261
  5.5 0.4 collective-permute-start.1
  5.9 1.0 %collective-permute-start = (bf16[1,1,512,128]{3,2,1,0:T(8,128)(2,1)S(1)}, bf16[1,1,512,128]{3,2,1,0:T(8,128)(2,1)S(1)}, u32[]{:S(2)}, u32[]{:S(2)}) collective-permute-start(bf16[1,1,512,128]{3,2,1,0:T(8,128)(2,1)S(1)} %select_bitcast_fusion), channel_id=1, source_target_pairs={{0,4},{1,5},{2,6},{3,7},{4,8},{5,9},{6,10},{7,11},{8,12},{9,13},{1... | collective-permute-start | bytes 393224 | tf_op jit(solution)/shard_map/ppermute | solution.py:261
  7.0 1.4 %copy.12 = s32[1,128,13]{2,1,0:T(8,128)} copy(s32[1,128,13]{1,0,2:T(1,128)} %param.11) | data formatting | bytes 13312 | tf_op args[1]
  8.4 9.9 %all-to-all-start = ((s32[128,1,13]{2,1,0:T(1,128)}), s32[128,1,13]{2,1,0:T(1,128)S(1)}, u32[]{:S(2)}, u32[]{:S(2)}) async-start(s32[128,1,13]{2,1,0:T(1,128)} %bitcast), calls=%async_computation | async-start | bytes 131072 | tf_op jit(solution)/shard_map/all_to_all | solution.py:293
  18.4 1.5 %collective-permute-start.3 = (bf16[4,1,512,128]{3,2,1,0:T(8,128)(2,1)S(1)}, bf16[4,1,512,128]{3,2,1,0:T(8,128)(2,1)S(1)}, u32[]{:S(2)}, u32[]{:S(2)}) collective-permute-start(bf16[4,1,512,128]{3,2,1,0:T(8,128)(2,1)S(1)} %pad_maximum_fusion.rest_0_), channel_id=1, source_target_pairs={{0,1},{1,2},{2,3},{3,0},{4,5},{5,6},{6,7},{7,4},{8,9},{9,10},{10,1... | collective-permute-start | bytes 1572872 | tf_op jit(solution)/shard_map/ppermute | solution.py:261
  19.9 1.3 %collective-permute-start.4 = (bf16[4,1,512,128]{3,2,1,0:T(8,128)(2,1)S(1)}, bf16[4,1,512,128]{3,2,1,0:T(8,128)(2,1)S(1)}, u32[]{:S(2)}, u32[]{:S(2)}) collective-permute-start(bf16[4,1,512,128]{3,2,1,0:T(8,128)(2,1)S(1)} %pad_maximum_fusion.rest_0_), channel_id=1, source_target_pairs={{0,3},{1,0},{2,1},{3,2},{4,7},{5,4},{6,5},{7,6},{8,11},{9,8},{10,9... | collective-permute-start | bytes 1572872 | tf_op jit(solution)/shard_map/ppermute | solution.py:261
  21.2 1.6 %collective-permute-start.5 = (bf16[4,1,512,128]{3,2,1,0:T(8,128)(2,1)S(1)}, bf16[4,1,512,128]{3,2,1,0:T(8,128)(2,1)S(1)}, u32[]{:S(2)}, u32[]{:S(2)}) collective-permute-start(bf16[4,1,512,128]{3,2,1,0:T(8,128)(2,1)S(1)} %pad_maximum_fusion.rest_0_), channel_id=1, source_target_pairs={{0,2},{1,3},{2,0},{3,1},{4,6},{5,7},{6,4},{7,5},{8,10},{9,11},{10,... | collective-permute-start | bytes 1572872 | tf_op jit(solution)/shard_map/ppermute | solution.py:261
  22.9 7.3 %relayout.1.rows = bf16[4096,8,128]{2,1,0:T(8,128)(2,1)} custom-call(bf16[4096,1024]{1,0:T(8,128)(2,1)} %features.1), custom_call_target="tpu_custom_call" | custom-call | flops 8049999872 | bytes 1 | tf_op jit(solution)/shard_map/relayout/pallas_call | solution.py:59
  30.2 6.8 %pick.1 = (bf16[1664,8,128]{2,1,0:T(8,128)(2,1)}, bf16[32,8,128]{2,1,0:T(8,128)(2,1)}) custom-call(s32[128,1,13]{2,1,0:T(1,128)S(1)} %all-to-all-done.served, s32[32]{0:T(128)S(1)} %copy-done.3, bf16[4096,8,128]{2,1,0:T(8,128)(2,1)} %relayout.1.rows), custom_call_target="tpu_custom_call" | custom-call | flops 2300000000 | bytes 1 | tf_op jit(solution)/shard_map/pick/pallas_call | solution.py:121
  37.1 0.8 copy-done.5
  38.3 9.0 %all-to-all-start.1 = ((bf16[128,104,128]{2,1,0:T(8,128)(2,1)}), bf16[128,104,128]{2,1,0:T(8,128)(2,1)S(1)}, u32[]{:S(2)}, u32[]{:S(2)}) async-start(bf16[128,104,128]{2,1,0:T(8,128)(2,1)} %bitcast.14), calls=%async_computation.1 | async-start | bytes 6815744 | tf_op jit(solution)/shard_map/all_to_all | solution.py:303
  48.1 0.6 select_reduce_fusion.2
  48.8 1.2 %select_reduce_fusion.1 = s32[32,50]{0,1:T(8,128)S(1)} fusion(s32[128]{0:T(128)S(1)} %select_reduce_fusion.4, s32[32,50]{0,1:T(8,128)S(1)} %get-tuple-element.23), kind=kLoop, calls=%fused_computation.2 | loop fusion | flops 612800 | bytes 13312 | tf_op jit(solution)/shard_map/reduce_sum | solution.py:241
  50.0 0.9 select_reduce_fusion
  50.9 1.1 %collective-permute-start.6 = (bf16[4,1,512,128]{3,2,1,0:T(8,128)(2,1)}, bf16[4,1,512,128]{3,2,1,0:T(8,128)(2,1)S(1)}, u32[]{:S(2)}, u32[]{:S(2)}) collective-permute-start(bf16[4,1,512,128]{3,2,1,0:T(8,128)(2,1)} %copy-done.4), channel_id=1, source_target_pairs={{0,16},{16,0},{32,48},{48,32},{64,80},{80,64},{96,112},{112,96},{1... | collective-permute-start | bytes 1572872 | tf_op jit(solution)/shard_map/ppermute | solution.py:304
  52.9 0.9 collective-permute-done.6.rest_4_
  53.8 1.5 %collective-permute-done.7.rest_5_ = bf16[4,1,512,128]{3,2,1,0:T(8,128)(2,1)S(1)} collective-permute-done((bf16[4,1,512,128]{3,2,1,0:T(8,128)(2,1)}, bf16[4,1,512,128]{3,2,1,0:T(8,128)(2,1)S(1)}, u32[]{:S(2)}, u32[]{:S(2)}) %collective-permute-start.7) | collective-permute-done | bytes 524320 | tf_op jit(solution)/shard_map/ppermute | solution.py:304
  55.3 0.7 collective-permute-done.8.rest_6_
  56.1 0.8 copy-done.10
  56.9 34.1 %all-to-all-done.1 = bf16[128,104,128]{2,1,0:T(8,128)(2,1)S(1)} async-done(((bf16[128,104,128]{2,1,0:T(8,128)(2,1)}), bf16[128,104,128]{2,1,0:T(8,128)(2,1)S(1)}, u32[]{:S(2)}, u32[]{:S(2)}) %all-to-all-start.1) | async-done | bytes 3407904 | tf_op jit(solution)/shard_map/all_to_all | solution.py:303
  91.0 0.8 copy-done
  91.8 9.7 %finish.1 = bf16[32,1024]{1,0:T(8,128)(2,1)} custom-call(s32[800]{0:T(1024)S(1)} %iota_add_fusion.source, s32[2,32]{1,0:T(2,128)S(1)} %pad_add_fusion.blocks, bf16[1664,8,128]{2,1,0:T(8,128)(2,1)S(1)} %bitcast.11, bf16[32,8,128]{2,1,0:T(8,128)(2,1)S(1)} %copy-done, f32[32,800]{1,0:T(8,128)S(1)} %convert_element_type.3.shares, f32[1,2048]{1,0:T(1,128)S(1)} %bitcast.12, ...), custom_call_target="tpu_custom_call" | custom-call | tf_op jit(solution)/shard_map/finish/pallas_call | solution.py:212
  (55 shorter events, 2.3 us)
Async XLA Ops:
  1.0 17.3 %collective-permute-start.2 = (bf16[1,1,512,128]{3,2,1,0:T(8,128)(2,1)S(1)}, bf16[1,1,512,128]{3,2,1,0:T(8,128)(2,1)S(1)}, u32[]{:S(2)}, u32[]{:S(2)}) collective-permute-start(bf16[1,1,512,128]{3,2,1,0:T(8,128)(2,1)S(1)} %select_bitcast_fusion), channel_id=1, source_target_pairs={{0,8},{1,9},{2,10},{3,11},{4,12},{5,13},{6,14},{7,15},{8,0},{9,1},... | collective-permute-start | bytes 393224 | tf_op jit(solution)/shard_map/ppermute | solution.py:261
  5.5 12.8 %collective-permute-start.1 = (bf16[1,1,512,128]{3,2,1,0:T(8,128)(2,1)S(1)}, bf16[1,1,512,128]{3,2,1,0:T(8,128)(2,1)S(1)}, u32[]{:S(2)}, u32[]{:S(2)}) collective-permute-start(bf16[1,1,512,128]{3,2,1,0:T(8,128)(2,1)S(1)} %select_bitcast_fusion), channel_id=1, source_target_pairs={{0,12},{1,13},{2,14},{3,15},{4,0},{5,1},{6,2},{7,3},{8,4},{9,5},{1... | collective-permute-start | bytes 393224 | tf_op jit(solution)/shard_map/ppermute | solution.py:261
  5.9 12.4 %collective-permute-start = (bf16[1,1,512,128]{3,2,1,0:T(8,128)(2,1)S(1)}, bf16[1,1,512,128]{3,2,1,0:T(8,128)(2,1)S(1)}, u32[]{:S(2)}, u32[]{:S(2)}) collective-permute-start(bf16[1,1,512,128]{3,2,1,0:T(8,128)(2,1)S(1)} %select_bitcast_fusion), channel_id=1, source_target_pairs={{0,4},{1,5},{2,6},{3,7},{4,8},{5,9},{6,10},{7,11},{8,12},{9,13},{1... | collective-permute-start | bytes 393224 | tf_op jit(solution)/shard_map/ppermute | solution.py:261
  8.4 21.8 %all-to-all-start = ((s32[128,1,13]{2,1,0:T(1,128)}), s32[128,1,13]{2,1,0:T(1,128)S(1)}, u32[]{:S(2)}, u32[]{:S(2)}) async-start(s32[128,1,13]{2,1,0:T(1,128)} %bitcast), calls=%async_computation | async-start | bytes 131072 | tf_op jit(solution)/shard_map/all_to_all | solution.py:293
  18.4 11.8 %copy-start.4 = (bf16[4,1,512,128]{3,2,1,0:T(8,128)(2,1)}, bf16[4,1,512,128]{3,2,1,0:T(8,128)(2,1)S(1)}, u32[]{:S(2)}) copy-start(bf16[4,1,512,128]{3,2,1,0:T(8,128)(2,1)S(1)} %pad_maximum_fusion.rest_0_) | copy-start | bytes 1572868
  18.4 11.8 %copy-start.3 = (s32[32]{0:T(128)S(1)}, s32[32]{0:T(128)}, u32[]{:S(2)}) copy-start(s32[32]{0:T(128)} %target_rows.1) | copy-start | bytes 388
  18.4 18.7 %collective-permute-start.3 = (bf16[4,1,512,128]{3,2,1,0:T(8,128)(2,1)S(1)}, bf16[4,1,512,128]{3,2,1,0:T(8,128)(2,1)S(1)}, u32[]{:S(2)}, u32[]{:S(2)}) collective-permute-start(bf16[4,1,512,128]{3,2,1,0:T(8,128)(2,1)S(1)} %pad_maximum_fusion.rest_0_), channel_id=1, source_target_pairs={{0,1},{1,2},{2,3},{3,0},{4,5},{5,6},{6,7},{7,4},{8,9},{9,10},{10,1... | collective-permute-start | bytes 1572872 | tf_op jit(solution)/shard_map/ppermute | solution.py:261
  19.9 17.2 %collective-permute-start.4 = (bf16[4,1,512,128]{3,2,1,0:T(8,128)(2,1)S(1)}, bf16[4,1,512,128]{3,2,1,0:T(8,128)(2,1)S(1)}, u32[]{:S(2)}, u32[]{:S(2)}) collective-permute-start(bf16[4,1,512,128]{3,2,1,0:T(8,128)(2,1)S(1)} %pad_maximum_fusion.rest_0_), channel_id=1, source_target_pairs={{0,3},{1,0},{2,1},{3,2},{4,7},{5,4},{6,5},{7,6},{8,11},{9,8},{10,9... | collective-permute-start | bytes 1572872 | tf_op jit(solution)/shard_map/ppermute | solution.py:261
  21.2 15.9 %collective-permute-start.5 = (bf16[4,1,512,128]{3,2,1,0:T(8,128)(2,1)S(1)}, bf16[4,1,512,128]{3,2,1,0:T(8,128)(2,1)S(1)}, u32[]{:S(2)}, u32[]{:S(2)}) collective-permute-start(bf16[4,1,512,128]{3,2,1,0:T(8,128)(2,1)S(1)} %pad_maximum_fusion.rest_0_), channel_id=1, source_target_pairs={{0,2},{1,3},{2,0},{3,1},{4,6},{5,7},{6,4},{7,5},{8,10},{9,11},{10,... | collective-permute-start | bytes 1572872 | tf_op jit(solution)/shard_map/ppermute | solution.py:261
  30.2 17.1 %copy-start.13 = (s32[4]{0:T(128)S(1)}, s32[4]{0:T(128)}, u32[]{:S(2)}) copy-start(s32[4]{0:T(128)} %constant.90) | copy-start | bytes 52
  30.2 17.7 %copy-start.11 = (s32[32,50]{1,0:T(8,128)S(1)}, s32[32,50]{1,0:T(8,128)}, u32[]{:S(2)}) copy-start(s32[32,50]{1,0:T(8,128)} %param.13) | copy-start | bytes 19204
  30.2 17.7 %copy-start.12 = (s32[32,50]{1,0:T(8,128)S(1)}, s32[32,50]{1,0:T(8,128)}, u32[]{:S(2)}) copy-start(s32[32,50]{1,0:T(8,128)} %param.14) | copy-start | bytes 19204
  37.0 53.9 %copy-start.1 = (f32[2048]{0:T(1024)S(1)}, f32[2048]{0:T(1024)}, u32[]{:S(2)}) copy-start(f32[2048]{0:T(1024)} %param.16) | copy-start | bytes 24580
  37.1 53.9 %copy-start.2 = (f32[1024]{0:T(1024)S(1)}, f32[1024]{0:T(1024)}, u32[]{:S(2)}) copy-start(f32[1024]{0:T(1024)} %param.18) | copy-start | bytes 12292
  37.1 0.8 copy-start.5
  37.1 1.0 copy-start.6
  37.1 1.1 %copy-start.7 = (bf16[4,1,512,128]{3,2,1,0:T(8,128)(2,1)}, bf16[4,1,512,128]{3,2,1,0:T(8,128)(2,1)S(1)}, u32[]{:S(2)}) copy-start(bf16[4,1,512,128]{3,2,1,0:T(8,128)(2,1)S(1)} %collective-permute-done.5.rest_3_) | copy-start | bytes 1572868
  38.3 52.7 %all-to-all-start.1 = ((bf16[128,104,128]{2,1,0:T(8,128)(2,1)}), bf16[128,104,128]{2,1,0:T(8,128)(2,1)S(1)}, u32[]{:S(2)}, u32[]{:S(2)}) async-start(bf16[128,104,128]{2,1,0:T(8,128)(2,1)} %bitcast.14), calls=%async_computation.1 | async-start | bytes 6815744 | tf_op jit(solution)/shard_map/all_to_all | solution.py:303
  50.9 2.9 %collective-permute-start.6 = (bf16[4,1,512,128]{3,2,1,0:T(8,128)(2,1)}, bf16[4,1,512,128]{3,2,1,0:T(8,128)(2,1)S(1)}, u32[]{:S(2)}, u32[]{:S(2)}) collective-permute-start(bf16[4,1,512,128]{3,2,1,0:T(8,128)(2,1)} %copy-done.4), channel_id=1, source_target_pairs={{0,16},{16,0},{32,48},{48,32},{64,80},{80,64},{96,112},{112,96},{1... | collective-permute-start | bytes 1572872 | tf_op jit(solution)/shard_map/ppermute | solution.py:304
  52.1 3.2 %collective-permute-start.7 = (bf16[4,1,512,128]{3,2,1,0:T(8,128)(2,1)}, bf16[4,1,512,128]{3,2,1,0:T(8,128)(2,1)S(1)}, u32[]{:S(2)}, u32[]{:S(2)}) collective-permute-start(bf16[4,1,512,128]{3,2,1,0:T(8,128)(2,1)} %copy-done.5), channel_id=1, source_target_pairs={{0,16},{16,0},{32,48},{48,32},{64,80},{80,64},{96,112},{112,96},{1... | collective-permute-start | bytes 1572872 | tf_op jit(solution)/shard_map/ppermute | solution.py:304
  52.1 3.9 %collective-permute-start.8 = (bf16[4,1,512,128]{3,2,1,0:T(8,128)(2,1)}, bf16[4,1,512,128]{3,2,1,0:T(8,128)(2,1)S(1)}, u32[]{:S(2)}, u32[]{:S(2)}) collective-permute-start(bf16[4,1,512,128]{3,2,1,0:T(8,128)(2,1)} %copy-done.6), channel_id=1, source_target_pairs={{0,16},{16,0},{32,48},{48,32},{64,80},{80,64},{96,112},{112,96},{1... | collective-permute-start | bytes 1572872 | tf_op jit(solution)/shard_map/ppermute | solution.py:304
  52.6 4.3 %collective-permute-start.9 = (bf16[4,1,512,128]{3,2,1,0:T(8,128)(2,1)}, bf16[4,1,512,128]{3,2,1,0:T(8,128)(2,1)}, u32[]{:S(2)}, u32[]{:S(2)}) collective-permute-start(bf16[4,1,512,128]{3,2,1,0:T(8,128)(2,1)} %copy-done.7), channel_id=1, source_target_pairs={{0,16},{16,0},{32,48},{48,32},{64,80},{80,64},{96,112},{112,96},{1... | collective-permute-start | bytes 1572872 | tf_op jit(solution)/shard_map/ppermute | solution.py:304
  53.8 2.3 %copy-start.8 = (bf16[4,1,512,128]{3,2,1,0:T(8,128)(2,1)}, bf16[4,1,512,128]{3,2,1,0:T(8,128)(2,1)S(1)}, u32[]{:S(2)}) copy-start(bf16[4,1,512,128]{3,2,1,0:T(8,128)(2,1)S(1)} %collective-permute-done.6.rest_4_) | copy-start | bytes 1572868
  91.0 0.8 copy-start
  (2 other events, 1.6 us)

commit v3 on v2

v3 whole, which is shorter than its diff:
```python
import functools

import jax
import jax.numpy as jnp
from jax import lax
from jax.experimental import pallas as pl
from jax.experimental.pallas import tpu as pltpu
from jax.sharding import PartitionSpec as P

LIVE = 800
LANES = 128
ROWS_AT_ONCE = 256
BLOCK = 1024
GROUP = 32
PEERS_AT_ONCE = 4
COST_PICK, COST_PREPARE = 7, 18
AXES = ("dom", "grp")
SHIFTS = (0, 1, 3, 2)
GRANT = pltpu.CompilerParams(vmem_limit_bytes=32 * 2**20)


def takes(microseconds):
    return pl.CostEstimate(flops=int(microseconds * 1.15e9), bytes_accessed=1, transcendentals=0)


def in_hbm(x):
    return pltpu.with_memory_space_constraint(x, pltpu.HBM)


def pick_kernel(
    served, target_rows, features, outgoing, own, index, own_index, held, rows, picked, picked_own, sems, out_sems
):
    peers, _, capacity = served.shape
    loads = features.shape[0] // ROWS_AT_ONCE
    chunks = features.shape[1] // LANES
    stores = out_sems.shape[0] - 1
    span = peers // stores

    def load(step):
        part = pl.ds(step * ROWS_AT_ONCE, ROWS_AT_ONCE)
        return pltpu.make_async_copy(features.at[part], held.at[part], sems.at[step])

    lists = [
        pltpu.make_async_copy(served, index, sems.at[loads]),
        pltpu.make_async_copy(target_rows, own_index, sems.at[loads + 1]),
    ]
    for step in range(loads):
        load(step).start()
    for copy in lists:
        copy.start()
    for step in range(loads):
        load(step).wait()
        part = pl.ds(step * ROWS_AT_ONCE, ROWS_AT_ONCE)
        rows[part] = pltpu.einshape("n(cl)->ncl", held[part, :], c=chunks)
    for copy in lists:
        copy.wait()
    copies = []
    for step in range(stores):

        def some_peers(group, carry):
            for peer in range(PEERS_AT_ONCE):
                for slot in range(capacity):
                    p = group * PEERS_AT_ONCE + peer
                    picked[p * capacity + slot] = rows[index[p, 0, slot]]
            return carry

        groups = span // PEERS_AT_ONCE
        lax.fori_loop(step * groups, (step + 1) * groups, some_peers, 0)
        part = pl.ds(step * span * capacity, span * capacity)
        copies.append(pltpu.make_async_copy(picked.at[part], outgoing.at[part], out_sems.at[step]))
        copies[-1].start()

    def target(t, carry):
        picked_own[t] = rows[own_index[t]]
        return carry

    lax.fori_loop(0, own.shape[0], target, 0)
    copies.append(pltpu.make_async_copy(picked_own, own, out_sems.at[stores]))
    copies[-1].start()
    for copy in copies:
        copy.wait()


def pick(served, target_rows, features):
    peers, _, capacity = served.shape
    count, width = features.shape
    tile = (width // LANES, LANES)
    targets = target_rows.shape[0]
    hbm = pl.BlockSpec(memory_space=pltpu.HBM)
    anywhere = pl.BlockSpec(memory_space=pl.ANY)
    return pl.pallas_call(
        pick_kernel,
        out_shape=(
            pltpu.HBM((peers * capacity,) + tile, features.dtype),
            pltpu.HBM((targets,) + tile, features.dtype),
        ),
        in_specs=[anywhere, anywhere, hbm],
        out_specs=(hbm, hbm),
        scratch_shapes=[
            pltpu.SMEM(served.shape, jnp.int32),
            pltpu.SMEM(target_rows.shape, jnp.int32),
            pltpu.VMEM((count, width), features.dtype),
            pltpu.VMEM((count,) + tile, features.dtype),
            pltpu.VMEM((peers * capacity,) + tile, features.dtype),
            pltpu.VMEM((targets,) + tile, features.dtype),
            pltpu.SemaphoreType.DMA((count // ROWS_AT_ONCE + 2,)),
            pltpu.SemaphoreType.DMA((9,)),
        ],
        compiler_params=GRANT,
        cost_estimate=takes(COST_PICK),
        name="pick",
    )(served, in_hbm(target_rows), in_hbm(features))


def prepare_kernel(
    blocks, own, shares, output_weight, output_bias, *rest,
):
    mine, other = rest[:4], rest[4:8]
    hidden_weight, base, parts, total = rest[8:12]
    whole, spread, own_rows, held, held_base, held_parts, held_total, sems = rest[12:]
    targets, chunks, _ = own.shape
    half, side = mine[0].shape[2:]
    first_rows = pltpu.make_async_copy(output_weight.at[pl.ds(0, held.shape[0])], held, sems.at[32])
    first_rows.start()
    copies = []
    for far, pieces in enumerate((mine, other)):
        for second, piece in enumerate(pieces):
            for first in range(piece.shape[0]):
                at = 16 * far + 4 * second + first
                rows = pl.ds(pl.multiple_of(blocks[0, at] * half, half), half)
                columns = pl.ds(pl.multiple_of(blocks[1, at] * side, side), side)
                copies.append(
                    pltpu.make_async_copy(piece.at[first, 0], whole.at[rows, columns], sems.at[at])
                )
    for copy in copies:
        copy.start()

    spread[...] = own[...].astype(jnp.float32).reshape(targets * chunks, LANES)
    for chunk in range(chunks):
        part = spread[pl.ds(chunk, targets, stride=chunks), :]
        own_rows[:, pl.ds(chunk * LANES, LANES)] = part.astype(jnp.bfloat16)
    share = shares[...]
    high = jnp.floor(share * (1.0 / 64.0))
    low = share - high * 64.0
    held_parts[...] = jnp.concatenate([high, low], axis=0).astype(jnp.bfloat16)
    held_total[...] = jnp.broadcast_to(jnp.sum(share, axis=1, keepdims=True), held_total.shape)
    first_rows.wait()
    held_base[...] = jnp.dot(own_rows[...], held[...], preferred_element_type=jnp.float32) + output_bias[...]
    for copy in copies:
        copy.wait()
    results = ((whole, hidden_weight), (held_base, base), (held_parts, parts), (held_total, total))
    stores = [pltpu.make_async_copy(held, out, sems.at[33 + at]) for at, (held, out) in enumerate(results)]
    for store in stores:
        store.start()
    for store in stores:
        store.wait()


def prepare(blocks, own, shares, output_weight, output_bias, mine, other):
    targets, chunks, _ = own.shape
    width = chunks * LANES
    units = output_weight.shape[1]
    hidden = output_weight.shape[0] - width
    vmem = pl.BlockSpec(memory_space=pltpu.VMEM)
    hbm = pl.BlockSpec(memory_space=pltpu.HBM)
    return pl.pallas_call(
        prepare_kernel,
        out_shape=(
            pltpu.HBM((width, hidden), jnp.bfloat16),
            pltpu.HBM((targets, units), jnp.float32),
            pltpu.HBM((2 * targets, LIVE), jnp.bfloat16),
            pltpu.HBM((targets, LANES), jnp.float32),
        ),
        in_specs=[pl.BlockSpec(memory_space=pltpu.SMEM), vmem, vmem, hbm, vmem] + [hbm] * 8,
        out_specs=(hbm,) * 4,
        scratch_shapes=[
            pltpu.VMEM((width, hidden), jnp.bfloat16),
            pltpu.VMEM((targets * chunks, LANES), jnp.float32),
            pltpu.VMEM((targets, width), jnp.bfloat16),
            pltpu.VMEM((width, units), jnp.bfloat16),
            pltpu.VMEM((targets, units), jnp.float32),
            pltpu.VMEM((2 * targets, LIVE), jnp.bfloat16),
            pltpu.VMEM((targets, LANES), jnp.float32),
            pltpu.SemaphoreType.DMA((37,)),
        ],
        compiler_params=GRANT,
        cost_estimate=takes(COST_PREPARE),
        name="prepare",
    )(
        blocks, own, shares, in_hbm(output_weight), output_bias.reshape(1, -1),
        *[in_hbm(piece) for piece in mine + other],
    )


def finish_kernel(
    source, arrived, parts_hbm, total_hbm, base_hbm, hidden_bias_hbm, hidden_weight, output_weight,
    embedding, spread, live_rows, pooled, held_hidden, held_output, parts, total, base, hidden_bias, sems,
):
    chunks = arrived.shape[1]
    targets, hidden = pooled.shape
    blocks = hidden // BLOCK
    small = ((parts_hbm, parts), (total_hbm, total), (base_hbm, base), (hidden_bias_hbm, hidden_bias))
    loads = []
    for block in range(blocks):
        columns = pl.ds(block * BLOCK, BLOCK)
        loads.append(
            pltpu.make_async_copy(hidden_weight.at[:, columns], held_hidden.at[:, columns], sems.at[block])
        )
        loads[-1].start()
    rest = [pltpu.make_async_copy(x, held, sems.at[blocks + 1 + at]) for at, (x, held) in enumerate(small)]
    for load in rest:
        load.start()

    def group(g, carry):
        at = lax.rem(g, 2) * (GROUP * chunks)
        for row in range(GROUP):
            place = pl.multiple_of(at + row * chunks, chunks)
            spread[pl.ds(place, chunks), :] = arrived[source[g * GROUP + row]].astype(jnp.float32)
        rows = pl.ds(pl.multiple_of(g * GROUP, GROUP), GROUP)
        for chunk in range(chunks):
            part = spread[pl.ds(at + chunk, GROUP, stride=chunks), :]
            live_rows[rows, pl.ds(chunk * LANES, LANES)] = part.astype(jnp.bfloat16)
        return carry

    lax.fori_loop(0, LIVE // GROUP, group, 0)
    skipped = output_weight.shape[0] - hidden
    last_rows = pltpu.make_async_copy(output_weight.at[pl.ds(skipped, hidden)], held_output, sems.at[blocks])
    last_rows.start()
    for load in rest:
        load.wait()
    for block in range(blocks):
        columns = pl.ds(block * BLOCK, BLOCK)
        loads[block].wait()
        product = jnp.dot(live_rows[...], held_hidden[:, columns], preferred_element_type=jnp.float32)
        transformed = jnp.maximum(product + hidden_bias[:, columns], 0.0).astype(jnp.bfloat16)
        both = jnp.dot(parts[...], transformed, preferred_element_type=jnp.float32)
        summed = both[:targets] * 64.0 + both[targets:]
        pooled[:, columns] = (summed / total[:, :1]).astype(jnp.bfloat16)
    last_rows.wait()
    combined = base[...] + jnp.dot(pooled[...], held_output[...], preferred_element_type=jnp.float32)
    combined = jnp.maximum(combined, 0.0)
    scale = lax.rsqrt(jnp.mean(combined * combined, axis=1, keepdims=True) + 1e-06)
    embedding[...] = (combined * scale).astype(jnp.bfloat16)


def finish(source, arrived, parts, total, base, hidden_bias, hidden_weight, output_weight):
    chunks = arrived.shape[1]
    targets = base.shape[0]
    width, hidden = hidden_weight.shape
    units = output_weight.shape[1]
    vmem = pl.BlockSpec(memory_space=pltpu.VMEM)
    smem = pl.BlockSpec(memory_space=pltpu.SMEM)
    hbm = pl.BlockSpec(memory_space=pltpu.HBM)
    return pl.pallas_call(
        finish_kernel,
        out_shape=jax.ShapeDtypeStruct((targets, units), jnp.bfloat16),
        in_specs=[smem, vmem] + [hbm] * 6,
        out_specs=vmem,
        scratch_shapes=[
            pltpu.VMEM((2 * GROUP * chunks, LANES), jnp.float32),
            pltpu.VMEM((LIVE, width), jnp.bfloat16),
            pltpu.VMEM((targets, hidden), jnp.bfloat16),
            pltpu.VMEM((width, hidden), jnp.bfloat16),
            pltpu.VMEM((hidden, units), jnp.bfloat16),
            pltpu.VMEM(parts.shape, jnp.bfloat16),
            pltpu.VMEM(total.shape, jnp.float32),
            pltpu.VMEM(base.shape, jnp.float32),
            pltpu.VMEM((1, hidden), jnp.float32),
            pltpu.SemaphoreType.DMA((hidden // BLOCK + 5,)),
        ],
        compiler_params=GRANT,
        name="finish",
    )(
        source, pltpu.with_memory_space_constraint(arrived, pltpu.VMEM), in_hbm(parts), in_hbm(total),
        in_hbm(base), in_hbm(hidden_bias.reshape(1, -1)), in_hbm(hidden_weight), in_hbm(output_weight),
    )


def plan(neighbour_slot, counts, peers, capacity):
    owner, slot = neighbour_slot // capacity, neighbour_slot % capacity
    same = owner[:, :, None] == jnp.arange(peers, dtype=jnp.int32)
    used = jnp.max(jnp.where(same, slot[:, :, None] + 1, 0), axis=(0, 1))
    before = jnp.arange(peers)[:, None] < jnp.arange(peers)[None, :]
    start = jnp.sum(jnp.where(before, used[:, None], 0), axis=0)
    place = jnp.sum(jnp.where(same, start, 0), axis=2) + slot
    live = jnp.arange(LIVE, dtype=jnp.int32)
    hit = place[:, :, None] == live
    shares = jnp.sum(jnp.where(hit, counts[:, :, None], 0), axis=1).astype(jnp.float32)
    within = (start <= live[:, None]) & (live[:, None] < start + used)
    first = jnp.arange(peers, dtype=jnp.int32) * capacity - start
    source = jnp.sum(jnp.where(within, first, 0), axis=1) + live
    return source, shares


def shifted(x, second, by):
    pairs = []
    for dom in range(8):
        for grp in range(16):
            row, column = grp // 4, grp % 4
            if (dom % 2 == 0) != second:
                row = (row + by) % 4
            else:
                column = (column + by) % 4
            pairs.append((dom * 16 + grp, dom * 16 + row * 4 + column))
    return lax.ppermute(x, AXES, pairs)


def own_half(weight):
    halves = weight.reshape(2, 1, weight.shape[0] // 2, weight.shape[1])
    return jnp.where(lax.axis_index("dom") % 2 == 0, halves[:1], halves[1:])


def block_places(back):
    core = lax.axis_index("dom") % 2
    row, column = lax.axis_index("grp") // 4, lax.axis_index("grp") % 4
    rows, columns = (row - back) % 4, (column - back) % 4
    of_core0 = (rows[None, :] * 4 + columns[:, None]).reshape(-1)
    of_core1 = (rows[:, None] * 4 + columns[None, :]).reshape(-1)
    same, across = jnp.where(core == 0, of_core0, of_core1), jnp.where(core == 0, of_core1, of_core0)
    half = jnp.repeat(jnp.stack([core, 1 - core]), 16)
    return jnp.stack([half, jnp.concatenate([same, across])]).astype(jnp.int32)


def on_device(
    features,
    requests,
    target_rows,
    neighbour_slot,
    counts,
    hidden_weight,
    hidden_bias,
    output_weight,
    output_bias,
):
    _, peers, capacity = requests.shape
    served = lax.all_to_all(requests.reshape(peers, 1, capacity), AXES, split_axis=0, concat_axis=0, tiled=True)
    own_part = own_half(hidden_weight)
    near = [own_part] + [shifted(own_part, False, by) for by in SHIFTS[1:]]
    near = jnp.concatenate(near, axis=0)
    mine = [near] + [shifted(near, True, by) for by in SHIFTS[1:]]
    outgoing, own = pick(served, target_rows, features)
    tile = outgoing.shape[1:]
    blocks = outgoing.reshape(peers, capacity * tile[0], tile[1])
    arrived = lax.all_to_all(blocks, AXES, split_axis=0, concat_axis=0, tiled=True)
    back = jnp.array(SHIFTS, jnp.int32)
    mine, neighbour_slot, counts, back = lax.optimization_barrier((mine, neighbour_slot, counts, back))
    places = block_places(back)
    other = [lax.ppermute(part, "dom", [(dom, dom ^ 1) for dom in range(8)]) for part in mine]
    source, shares = plan(neighbour_slot, counts, peers, capacity)
    weight, base, parts, total = prepare(places, own, shares, output_weight, output_bias, mine, other)
    return finish(
        source, arrived.reshape((peers * capacity,) + tile), parts, total, base, hidden_bias, weight, output_weight
    )


def solution(mesh):
    placed = (
        P(AXES, None),
        P(AXES, None, None),
        P(AXES),
        P(AXES, None),
        P(AXES, None),
        P(None, "grp"),
        P(),
        P(),
        P(),
    )
    return jax.shard_map(on_device, mesh=mesh, in_specs=placed, out_specs=P(AXES, None), check_vma=False)
```

time: 102 us -> 91.4 us (0.90)
  starting transfers between devices: 31 us -> 26.1 us
  Pallas kernels: 23.9 us -> 20.8 us
  waiting for transfers between devices: 37.2 us -> 35.1 us
  local copies, waits for them, and re-layouts: 4.79 us -> 3.59 us
    all_to_all x1, waiting for transfers between devices: 34.1 us -> 28 us  [on_device(): lax.all_to_all(blocks, AXES, split_axis=0, concat_axis=0, tiled=True)]
    all_to_all x1, starting transfers between devices: 8.98 us -> 4.92 us  [on_device(): lax.all_to_all(blocks, AXES, split_axis=0, concat_axis=0, tiled=True)]
    all_to_all x1, waiting for transfers between devices: 0.01 us -> 3.99 us  [on_device(): lax.all_to_all(requests.reshape(peers, 1, capacity), AXES, split_axis=0,...]
    pallas_call x3, Pallas kernels: 23.9 us -> 20.8 us  [the longest x1 8.71 us: finish(): pl.pallas_call(finish_kernel, out_shape=jax.ShapeDtypeStruct((targets, un...]
    unnamed x29 -> x19, local copies, waits for them, and re-layouts: 4.29 us -> 3.09 us
  transfers between devices with their start and end apart: 12 -> 12, of which waited for: 4 -> 6; matrix products, arithmetic and copies ran while one was open for 5% -> 7% of each run, Pallas kernels for 14% -> 13%
where the time goes in v3:
time: 91.4 us; the launch traced here: 91.1 us
  waiting for transfers between devices  35.1 us (38%)
  starting transfers between devices  26.1 us (29%)
  Pallas kernels  20.8 us (23%)
  other arithmetic  5.15 us (6%)
  local copies, waits for them, and re-layouts  3.59 us (4%)
    all_to_all x1, waiting for transfers between devices, on_device(): lax.all_to_all(blocks, AXES, split_axis=0, concat_axis=0, tiled=True)  28 us
    ppermute x6, starting transfers between devices, shifted(): return lax.ppermute(x, AXES, pairs)  10.3 us
    all_to_all x1, starting transfers between devices, on_device(): lax.all_to_all(requests.reshape(peers, 1, capacity), AXES, split_axis=0,...  9.18 us
    pallas_call x1, Pallas kernels, finish(): pl.pallas_call(finish_kernel, out_shape=jax.ShapeDtypeStruct((targets, un...  8.71 us
    pallas_call x1, Pallas kernels, pick(): pl.pallas_call(pick_kernel, out_shape=(pltpu.HBM((peers * capacity,) + ti...  6.42 us
    pallas_call x1, Pallas kernels, prepare(): pl.pallas_call(prepare_kernel, out_shape=(pltpu.HBM((width, hidden), jnp....  5.67 us
    all_to_all x1, starting transfers between devices, on_device(): lax.all_to_all(blocks, AXES, split_axis=0, concat_axis=0, tiled=True)  4.92 us
    all_to_all x1, waiting for transfers between devices, on_device(): lax.all_to_all(requests.reshape(peers, 1, capacity), AXES, split_axis=0,...  3.99 us
  transfers between devices with their start and end apart: 12, of which 6 were waited for; matrix products, arithmetic and copies ran while one was open for 7% of the time, Pallas kernels for 13%

profile of v3, /device:TPU:1, one launch (start us, length us, event | category | flops | bytes accessed | tf_op | source)
XLA Modules:
  0.0 91.1 jit_solution(9118237261969523197)
XLA Ops:
  0.0 1.0 %select_bitcast_fusion = bf16[1,1,512,128]{3,2,1,0:T(8,128)(2,1)S(1)} fusion(bf16[1024,128]{1,0:T(8,128)(2,1)} %param.15, pred[]{:T(512)S(6)} %eq.40), kind=kLoop, calls=%fused_computation.10 | loop fusion | flops 65536 | bytes 393217 | tf_op jit(solution)/shard_map/jit(_where)/select_n | solution.py:310
  1.0 2.5 %collective-permute-start = (bf16[1,1,512,128]{3,2,1,0:T(8,128)(2,1)S(1)}, bf16[1,1,512,128]{3,2,1,0:T(8,128)(2,1)S(1)}, u32[]{:S(2)}, u32[]{:S(2)}) collective-permute-start(bf16[1,1,512,128]{3,2,1,0:T(8,128)(2,1)S(1)} %select_bitcast_fusion), channel_id=1, source_target_pairs={{0,4},{1,5},{2,6},{3,7},{4,8},{5,9},{6,10},{7,11},{8,12},{9,13},{1... | collective-permute-start | bytes 393224 | tf_op jit(solution)/shard_map/ppermute | solution.py:305
  3.5 2.2 %collective-permute-start.1 = (bf16[1,1,512,128]{3,2,1,0:T(8,128)(2,1)S(1)}, bf16[1,1,512,128]{3,2,1,0:T(8,128)(2,1)S(1)}, u32[]{:S(2)}, u32[]{:S(2)}) collective-permute-start(bf16[1,1,512,128]{3,2,1,0:T(8,128)(2,1)S(1)} %select_bitcast_fusion), channel_id=1, source_target_pairs={{0,12},{1,13},{2,14},{3,15},{4,0},{5,1},{6,2},{7,3},{8,4},{9,5},{1... | collective-permute-start | bytes 393224 | tf_op jit(solution)/shard_map/ppermute | solution.py:305
  5.7 1.2 %collective-permute-start.2 = (bf16[1,1,512,128]{3,2,1,0:T(8,128)(2,1)S(1)}, bf16[1,1,512,128]{3,2,1,0:T(8,128)(2,1)S(1)}, u32[]{:S(2)}, u32[]{:S(2)}) collective-permute-start(bf16[1,1,512,128]{3,2,1,0:T(8,128)(2,1)S(1)} %select_bitcast_fusion), channel_id=1, source_target_pairs={{0,8},{1,9},{2,10},{3,11},{4,12},{5,13},{6,14},{7,15},{8,0},{9,1},... | collective-permute-start | bytes 393224 | tf_op jit(solution)/shard_map/ppermute | solution.py:305
  6.9 1.4 %copy.15 = s32[1,128,13]{2,1,0:T(8,128)} copy(s32[1,128,13]{1,0,2:T(1,128)} %param.11) | data formatting | bytes 13312 | tf_op args[1]
  8.4 9.2 %all-to-all-start = ((s32[128,1,13]{2,1,0:T(1,128)}), s32[128,1,13]{2,1,0:T(1,128)S(1)}, u32[]{:S(2)}, u32[]{:S(2)}) async-start(s32[128,1,13]{2,1,0:T(1,128)} %bitcast.1), calls=%async_computation | async-start | bytes 131072 | tf_op jit(solution)/shard_map/all_to_all | solution.py:336
  17.8 0.9 pad_maximum_fusion.rest_0_
  18.7 1.4 %collective-permute-start.3 = (bf16[4,1,512,128]{3,2,1,0:T(8,128)(2,1)}, bf16[4,1,512,128]{3,2,1,0:T(8,128)(2,1)}, u32[]{:S(2)}, u32[]{:S(2)}) collective-permute-start(bf16[4,1,512,128]{3,2,1,0:T(8,128)(2,1)} %pad_maximum_fusion.rest_0_), channel_id=1, source_target_pairs={{0,1},{1,2},{2,3},{3,0},{4,5},{5,6},{6,7},{7,4},{8,9},{9,10},{10,1... | collective-permute-start | bytes 1572872 | tf_op jit(solution)/shard_map/ppermute | solution.py:305
  20.1 1.3 %collective-permute-start.4 = (bf16[4,1,512,128]{3,2,1,0:T(8,128)(2,1)}, bf16[4,1,512,128]{3,2,1,0:T(8,128)(2,1)}, u32[]{:S(2)}, u32[]{:S(2)}) collective-permute-start(bf16[4,1,512,128]{3,2,1,0:T(8,128)(2,1)} %pad_maximum_fusion.rest_0_), channel_id=1, source_target_pairs={{0,3},{1,0},{2,1},{3,2},{4,7},{5,4},{6,5},{7,6},{8,11},{9,8},{10,9... | collective-permute-start | bytes 1572872 | tf_op jit(solution)/shard_map/ppermute | solution.py:305
  21.4 1.7 %collective-permute-start.5 = (bf16[4,1,512,128]{3,2,1,0:T(8,128)(2,1)}, bf16[4,1,512,128]{3,2,1,0:T(8,128)(2,1)}, u32[]{:S(2)}, u32[]{:S(2)}) collective-permute-start(bf16[4,1,512,128]{3,2,1,0:T(8,128)(2,1)} %pad_maximum_fusion.rest_0_), channel_id=1, source_target_pairs={{0,2},{1,3},{2,0},{3,1},{4,6},{5,7},{6,4},{7,5},{8,10},{9,11},{10,... | collective-permute-start | bytes 1572872 | tf_op jit(solution)/shard_map/ppermute | solution.py:305
  23.1 4.0 %all-to-all-done.served = s32[128,1,13]{2,1,0:T(1,128)S(1)} async-done(((s32[128,1,13]{2,1,0:T(1,128)}), s32[128,1,13]{2,1,0:T(1,128)S(1)}, u32[]{:S(2)}, u32[]{:S(2)}) %all-to-all-start) | async-done | bytes 6688 | tf_op jit(solution)/shard_map/all_to_all | solution.py:336
  27.1 6.4 %pick.1 = (bf16[1664,8,128]{2,1,0:T(8,128)(2,1)}, bf16[32,8,128]{2,1,0:T(8,128)(2,1)}) custom-call(s32[128,1,13]{2,1,0:T(1,128)S(1)} %all-to-all-done.served, s32[32]{0:T(128)} %target_rows.1, bf16[4096,1024]{1,0:T(8,128)(2,1)} %features.1), custom_call_target="tpu_custom_call" | custom-call | flops 8049999872 | bytes 1 | tf_op jit(solution)/shard_map/pick/pallas_call | solution.py:91
  33.5 4.9 %all-to-all-start.1 = ((bf16[128,104,128]{2,1,0:T(8,128)(2,1)}), bf16[128,104,128]{2,1,0:T(8,128)(2,1)S(1)}, u32[]{:S(2)}, u32[]{:S(2)}) async-start(bf16[128,104,128]{2,1,0:T(8,128)(2,1)} %bitcast.13), calls=%async_computation.1 | async-start | bytes 6815744 | tf_op jit(solution)/shard_map/all_to_all | solution.py:344
  39.4 1.2 %select_reduce_fusion.1 = s32[32,50]{0,1:T(8,128)S(1)} fusion(s32[128]{0:T(128)S(1)} %select_reduce_fusion.4, s32[32,50]{0,1:T(8,128)S(1)} %get-tuple-element.31), kind=kLoop, calls=%fused_computation.2 | loop fusion | flops 612800 | bytes 13312 | tf_op jit(solution)/shard_map/reduce_sum | solution.py:285
  40.7 0.9 select_reduce_fusion
  41.8 1.1 %collective-permute-start.6 = (bf16[4,1,512,128]{3,2,1,0:T(8,128)(2,1)}, bf16[4,1,512,128]{3,2,1,0:T(8,128)(2,1)S(1)}, u32[]{:S(2)}, u32[]{:S(2)}) collective-permute-start(bf16[4,1,512,128]{3,2,1,0:T(8,128)(2,1)} %pad_maximum_fusion.rest_0_), channel_id=1, source_target_pairs={{0,16},{16,0},{32,48},{48,32},{64,80},{80,64},{96,112},{112,96},{1... | collective-permute-start | bytes 1572872 | tf_op jit(solution)/shard_map/ppermute | solution.py:348
  43.8 0.8 collective-permute-done.6.rest_4_
  44.7 0.7 collective-permute-done.7.rest_5_
  45.4 0.7 collective-permute-done.8.rest_6_
  46.2 0.7 collective-permute-done.9.rest_7_
  47.7 0.8 copy-done.1
  48.5 5.7 %prepare.1 = (bf16[1024,2048]{1,0:T(8,128)(2,1)}, f32[32,1024]{1,0:T(8,128)}, bf16[64,800]{1,0:T(8,128)(2,1)}, f32[32,128]{1,0:T(8,128)}) custom-call(s32[2,32]{1,0:T(2,128)S(1)} %pad_add_fusion.blocks, bf16[32,8,128]{2,1,0:T(8,128)(2,1)S(1)} %copy-done.1, f32[32,800]{1,0:T(8,128)S(1)} %convert_element_type.3.shares, bf16[3072,1024]{1,0:T(8,128)(2,1)} %output_weight.3, ...), custom_call_target="tpu_custom_call" | custom-call | flops 20700000256 | bytes 1 | tf_op jit(solution)/shard_map/prepare/pallas_call | solution.py:166
  54.2 28.0 %all-to-all-done.1 = bf16[128,104,128]{2,1,0:T(8,128)(2,1)S(1)} async-done(((bf16[128,104,128]{2,1,0:T(8,128)(2,1)}), bf16[128,104,128]{2,1,0:T(8,128)(2,1)S(1)}, u32[]{:S(2)}, u32[]{:S(2)}) %all-to-all-start.1) | async-done | bytes 3407904 | tf_op jit(solution)/shard_map/all_to_all | solution.py:344
  82.2 8.7 %finish.1 = bf16[32,1024]{1,0:T(8,128)(2,1)} custom-call(s32[800]{0:T(1024)S(1)} %iota_add_fusion.source, bf16[1664,8,128]{2,1,0:T(8,128)(2,1)S(1)} %bitcast.11, bf16[64,800]{1,0:T(8,128)(2,1)} %get-tuple-element.27.parts_hbm, f32[32,128]{1,0:T(8,128)} %get-tuple-element.28.total_hbm, f32[32,1024]{1,0:T(8,128)} %get-tuple-element.29.base_hbm, ...), custom_call_target="tpu_custom_call" | custom-call | tf_op jit(solution)/shard_map/finish/pallas_call | solution.py:254
  (45 shorter events, 3.2 us)
Async XLA Ops:
  1.0 16.8 %collective-permute-start = (bf16[1,1,512,128]{3,2,1,0:T(8,128)(2,1)S(1)}, bf16[1,1,512,128]{3,2,1,0:T(8,128)(2,1)S(1)}, u32[]{:S(2)}, u32[]{:S(2)}) collective-permute-start(bf16[1,1,512,128]{3,2,1,0:T(8,128)(2,1)S(1)} %select_bitcast_fusion), channel_id=1, source_target_pairs={{0,4},{1,5},{2,6},{3,7},{4,8},{5,9},{6,10},{7,11},{8,12},{9,13},{1... | collective-permute-start | bytes 393224 | tf_op jit(solution)/shard_map/ppermute | solution.py:305
  3.5 14.3 %collective-permute-start.1 = (bf16[1,1,512,128]{3,2,1,0:T(8,128)(2,1)S(1)}, bf16[1,1,512,128]{3,2,1,0:T(8,128)(2,1)S(1)}, u32[]{:S(2)}, u32[]{:S(2)}) collective-permute-start(bf16[1,1,512,128]{3,2,1,0:T(8,128)(2,1)S(1)} %select_bitcast_fusion), channel_id=1, source_target_pairs={{0,12},{1,13},{2,14},{3,15},{4,0},{5,1},{6,2},{7,3},{8,4},{9,5},{1... | collective-permute-start | bytes 393224 | tf_op jit(solution)/shard_map/ppermute | solution.py:305
  5.7 12.1 %collective-permute-start.2 = (bf16[1,1,512,128]{3,2,1,0:T(8,128)(2,1)S(1)}, bf16[1,1,512,128]{3,2,1,0:T(8,128)(2,1)S(1)}, u32[]{:S(2)}, u32[]{:S(2)}) collective-permute-start(bf16[1,1,512,128]{3,2,1,0:T(8,128)(2,1)S(1)} %select_bitcast_fusion), channel_id=1, source_target_pairs={{0,8},{1,9},{2,10},{3,11},{4,12},{5,13},{6,14},{7,15},{8,0},{9,1},... | collective-permute-start | bytes 393224 | tf_op jit(solution)/shard_map/ppermute | solution.py:305
  8.4 18.7 %all-to-all-start = ((s32[128,1,13]{2,1,0:T(1,128)}), s32[128,1,13]{2,1,0:T(1,128)S(1)}, u32[]{:S(2)}, u32[]{:S(2)}) async-start(s32[128,1,13]{2,1,0:T(1,128)} %bitcast.1), calls=%async_computation | async-start | bytes 131072 | tf_op jit(solution)/shard_map/all_to_all | solution.py:336
  18.7 19.8 %collective-permute-start.3 = (bf16[4,1,512,128]{3,2,1,0:T(8,128)(2,1)}, bf16[4,1,512,128]{3,2,1,0:T(8,128)(2,1)}, u32[]{:S(2)}, u32[]{:S(2)}) collective-permute-start(bf16[4,1,512,128]{3,2,1,0:T(8,128)(2,1)} %pad_maximum_fusion.rest_0_), channel_id=1, source_target_pairs={{0,1},{1,2},{2,3},{3,0},{4,5},{5,6},{6,7},{7,4},{8,9},{9,10},{10,1... | collective-permute-start | bytes 1572872 | tf_op jit(solution)/shard_map/ppermute | solution.py:305
  20.1 18.4 %collective-permute-start.4 = (bf16[4,1,512,128]{3,2,1,0:T(8,128)(2,1)}, bf16[4,1,512,128]{3,2,1,0:T(8,128)(2,1)}, u32[]{:S(2)}, u32[]{:S(2)}) collective-permute-start(bf16[4,1,512,128]{3,2,1,0:T(8,128)(2,1)} %pad_maximum_fusion.rest_0_), channel_id=1, source_target_pairs={{0,3},{1,0},{2,1},{3,2},{4,7},{5,4},{6,5},{7,6},{8,11},{9,8},{10,9... | collective-permute-start | bytes 1572872 | tf_op jit(solution)/shard_map/ppermute | solution.py:305
  21.4 17.1 %collective-permute-start.5 = (bf16[4,1,512,128]{3,2,1,0:T(8,128)(2,1)}, bf16[4,1,512,128]{3,2,1,0:T(8,128)(2,1)}, u32[]{:S(2)}, u32[]{:S(2)}) collective-permute-start(bf16[4,1,512,128]{3,2,1,0:T(8,128)(2,1)} %pad_maximum_fusion.rest_0_), channel_id=1, source_target_pairs={{0,2},{1,3},{2,0},{3,1},{4,6},{5,7},{6,4},{7,5},{8,10},{9,11},{10,... | collective-permute-start | bytes 1572872 | tf_op jit(solution)/shard_map/ppermute | solution.py:305
  33.5 5.0 %copy-start.2 = (s32[32,50]{1,0:T(8,128)S(1)}, s32[32,50]{1,0:T(8,128)}, u32[]{:S(2)}) copy-start(s32[32,50]{1,0:T(8,128)} %param.13) | copy-start | bytes 19204
  33.5 7.1 %copy-start.3 = (s32[32,50]{1,0:T(8,128)S(1)}, s32[32,50]{1,0:T(8,128)}, u32[]{:S(2)}) copy-start(s32[32,50]{1,0:T(8,128)} %param.14) | copy-start | bytes 19204
  33.5 8.0 %copy-start.4 = (s32[4]{0:T(128)S(1)}, s32[4]{0:T(128)}, u32[]{:S(2)}) copy-start(s32[4]{0:T(128)} %constant.85.clone) | copy-start | bytes 52
  33.5 14.2 %copy-start = (f32[1024]{0:T(1024)S(1)}, f32[1024]{0:T(1024)}, u32[]{:S(2)}) copy-start(f32[1024]{0:T(1024)} %param.18) | copy-start | bytes 12292
  33.5 48.7 %all-to-all-start.1 = ((bf16[128,104,128]{2,1,0:T(8,128)(2,1)}), bf16[128,104,128]{2,1,0:T(8,128)(2,1)S(1)}, u32[]{:S(2)}, u32[]{:S(2)}) async-start(bf16[128,104,128]{2,1,0:T(8,128)(2,1)} %bitcast.13), calls=%async_computation.1 | async-start | bytes 6815744 | tf_op jit(solution)/shard_map/all_to_all | solution.py:344
  41.8 2.8 %collective-permute-start.6 = (bf16[4,1,512,128]{3,2,1,0:T(8,128)(2,1)}, bf16[4,1,512,128]{3,2,1,0:T(8,128)(2,1)S(1)}, u32[]{:S(2)}, u32[]{:S(2)}) collective-permute-start(bf16[4,1,512,128]{3,2,1,0:T(8,128)(2,1)} %pad_maximum_fusion.rest_0_), channel_id=1, source_target_pairs={{0,16},{16,0},{32,48},{48,32},{64,80},{80,64},{96,112},{112,96},{1... | collective-permute-start | bytes 1572872 | tf_op jit(solution)/shard_map/ppermute | solution.py:348
  42.9 2.5 %collective-permute-start.7 = (bf16[4,1,512,128]{3,2,1,0:T(8,128)(2,1)}, bf16[4,1,512,128]{3,2,1,0:T(8,128)(2,1)S(1)}, u32[]{:S(2)}, u32[]{:S(2)}) collective-permute-start(bf16[4,1,512,128]{3,2,1,0:T(8,128)(2,1)} %collective-permute-done.3.rest_1_), channel_id=1, source_target_pairs={{0,16},{16,0},{32,48},{48,32},{64,80},{80,64},{96,112},{112,96},{1... | collective-permute-start | bytes 1572872 | tf_op jit(solution)/shard_map/ppermute | solution.py:348
  43.0 3.2 %collective-permute-start.8 = (bf16[4,1,512,128]{3,2,1,0:T(8,128)(2,1)}, bf16[4,1,512,128]{3,2,1,0:T(8,128)(2,1)S(1)}, u32[]{:S(2)}, u32[]{:S(2)}) collective-permute-start(bf16[4,1,512,128]{3,2,1,0:T(8,128)(2,1)} %collective-permute-done.4.rest_2_), channel_id=1, source_target_pairs={{0,16},{16,0},{32,48},{48,32},{64,80},{80,64},{96,112},{112,96},{1... | collective-permute-start | bytes 1572872 | tf_op jit(solution)/shard_map/ppermute | solution.py:348
  43.4 3.5 %collective-permute-start.9 = (bf16[4,1,512,128]{3,2,1,0:T(8,128)(2,1)}, bf16[4,1,512,128]{3,2,1,0:T(8,128)(2,1)S(1)}, u32[]{:S(2)}, u32[]{:S(2)}) collective-permute-start(bf16[4,1,512,128]{3,2,1,0:T(8,128)(2,1)} %collective-permute-done.5.rest_3_), channel_id=1, source_target_pairs={{0,16},{16,0},{32,48},{48,32},{64,80},{80,64},{96,112},{112,96},{1... | collective-permute-start | bytes 1572872 | tf_op jit(solution)/shard_map/ppermute | solution.py:348
  44.7 2.3 %copy-start.5 = (bf16[4,1,512,128]{3,2,1,0:T(8,128)(2,1)}, bf16[4,1,512,128]{3,2,1,0:T(8,128)(2,1)S(1)}, u32[]{:S(2)}) copy-start(bf16[4,1,512,128]{3,2,1,0:T(8,128)(2,1)S(1)} %collective-permute-done.6.rest_4_) | copy-start | bytes 1572868
  45.4 1.5 %copy-start.6 = (bf16[4,1,512,128]{3,2,1,0:T(8,128)(2,1)}, bf16[4,1,512,128]{3,2,1,0:T(8,128)(2,1)S(1)}, u32[]{:S(2)}) copy-start(bf16[4,1,512,128]{3,2,1,0:T(8,128)(2,1)S(1)} %collective-permute-done.7.rest_5_) | copy-start | bytes 1572868
  46.2 0.8 copy-start.7
  46.9 0.8 copy-start.8
  47.7 0.8 copy-start.1

commit v4 on v3

--- a/solution.py
+++ b/solution.py
@@ -200,6 +200,9 @@
     targets, hidden = pooled.shape
     blocks = hidden // BLOCK
     small = ((parts_hbm, parts), (total_hbm, total), (base_hbm, base), (hidden_bias_hbm, hidden_bias))
+    rest = [pltpu.make_async_copy(x, held, sems.at[blocks + 1 + at]) for at, (x, held) in enumerate(small)]
+    for load in rest:
+        load.start()
     loads = []
     for block in range(blocks):
         columns = pl.ds(block * BLOCK, BLOCK)
@@ -207,9 +210,6 @@
             pltpu.make_async_copy(hidden_weight.at[:, columns], held_hidden.at[:, columns], sems.at[block])
         )
         loads[-1].start()
-    rest = [pltpu.make_async_copy(x, held, sems.at[blocks + 1 + at]) for at, (x, held) in enumerate(small)]
-    for load in rest:
-        load.start()
 
     def group(g, carry):
         at = lax.rem(g, 2) * (GROUP * chunks)

time: 91.4 us -> 91 us (level)
  no operation moved by 1% of the time
where the time goes in v4:
time: 91 us; the launch traced here: 90.6 us
  waiting for transfers between devices  35.1 us (39%)
  starting transfers between devices  26.1 us (29%)
  Pallas kernels  20.4 us (22%)
  other arithmetic  5.15 us (6%)
  local copies, waits for them, and re-layouts  3.59 us (4%)
    all_to_all x1, waiting for transfers between devices, on_device(): lax.all_to_all(blocks, AXES, split_axis=0, concat_axis=0, tiled=True)  28 us
    ppermute x6, starting transfers between devices, shifted(): return lax.ppermute(x, AXES, pairs)  10.3 us
    all_to_all x1, starting transfers between devices, on_device(): lax.all_to_all(requests.reshape(peers, 1, capacity), AXES, split_axis=0,...  9.18 us
    pallas_call x1, Pallas kernels, finish(): pl.pallas_call(finish_kernel, out_shape=jax.ShapeDtypeStruct((targets, un...  8.27 us
    pallas_call x1, Pallas kernels, pick(): pl.pallas_call(pick_kernel, out_shape=(pltpu.HBM((peers * capacity,) + ti...  6.42 us
    pallas_call x1, Pallas kernels, prepare(): pl.pallas_call(prepare_kernel, out_shape=(pltpu.HBM((width, hidden), jnp....  5.67 us
    all_to_all x1, starting transfers between devices, on_device(): lax.all_to_all(blocks, AXES, split_axis=0, concat_axis=0, tiled=True)  4.92 us
    all_to_all x1, waiting for transfers between devices, on_device(): lax.all_to_all(requests.reshape(peers, 1, capacity), AXES, split_axis=0,...  3.99 us
  transfers between devices with their start and end apart: 12, of which 6 were waited for; matrix products, arithmetic and copies ran while one was open for 7% of the time, Pallas kernels for 13%

profile of v4, /device:TPU:1, one launch (start us, length us, event | category | flops | bytes accessed | tf_op | source)
XLA Modules:
  0.0 90.6 jit_solution(11543864219049296557)
XLA Ops:
  0.0 1.0 %select_bitcast_fusion = bf16[1,1,512,128]{3,2,1,0:T(8,128)(2,1)S(1)} fusion(bf16[1024,128]{1,0:T(8,128)(2,1)} %param.15, pred[]{:T(512)S(6)} %eq.40), kind=kLoop, calls=%fused_computation.10 | loop fusion | flops 65536 | bytes 393217 | tf_op jit(solution)/shard_map/jit(_where)/select_n | solution.py:310
  1.0 2.5 %collective-permute-start = (bf16[1,1,512,128]{3,2,1,0:T(8,128)(2,1)S(1)}, bf16[1,1,512,128]{3,2,1,0:T(8,128)(2,1)S(1)}, u32[]{:S(2)}, u32[]{:S(2)}) collective-permute-start(bf16[1,1,512,128]{3,2,1,0:T(8,128)(2,1)S(1)} %select_bitcast_fusion), channel_id=1, source_target_pairs={{0,4},{1,5},{2,6},{3,7},{4,8},{5,9},{6,10},{7,11},{8,12},{9,13},{1... | collective-permute-start | bytes 393224 | tf_op jit(solution)/shard_map/ppermute | solution.py:305
  3.5 2.2 %collective-permute-start.1 = (bf16[1,1,512,128]{3,2,1,0:T(8,128)(2,1)S(1)}, bf16[1,1,512,128]{3,2,1,0:T(8,128)(2,1)S(1)}, u32[]{:S(2)}, u32[]{:S(2)}) collective-permute-start(bf16[1,1,512,128]{3,2,1,0:T(8,128)(2,1)S(1)} %select_bitcast_fusion), channel_id=1, source_target_pairs={{0,12},{1,13},{2,14},{3,15},{4,0},{5,1},{6,2},{7,3},{8,4},{9,5},{1... | collective-permute-start | bytes 393224 | tf_op jit(solution)/shard_map/ppermute | solution.py:305
  5.7 1.2 %collective-permute-start.2 = (bf16[1,1,512,128]{3,2,1,0:T(8,128)(2,1)S(1)}, bf16[1,1,512,128]{3,2,1,0:T(8,128)(2,1)S(1)}, u32[]{:S(2)}, u32[]{:S(2)}) collective-permute-start(bf16[1,1,512,128]{3,2,1,0:T(8,128)(2,1)S(1)} %select_bitcast_fusion), channel_id=1, source_target_pairs={{0,8},{1,9},{2,10},{3,11},{4,12},{5,13},{6,14},{7,15},{8,0},{9,1},... | collective-permute-start | bytes 393224 | tf_op jit(solution)/shard_map/ppermute | solution.py:305
  6.9 1.4 %copy.15 = s32[1,128,13]{2,1,0:T(8,128)} copy(s32[1,128,13]{1,0,2:T(1,128)} %param.11) | data formatting | bytes 13312 | tf_op args[1]
  8.4 9.2 %all-to-all-start = ((s32[128,1,13]{2,1,0:T(1,128)}), s32[128,1,13]{2,1,0:T(1,128)S(1)}, u32[]{:S(2)}, u32[]{:S(2)}) async-start(s32[128,1,13]{2,1,0:T(1,128)} %bitcast.1), calls=%async_computation | async-start | bytes 131072 | tf_op jit(solution)/shard_map/all_to_all | solution.py:336
  17.8 0.9 pad_maximum_fusion.rest_0_
  18.7 1.4 %collective-permute-start.3 = (bf16[4,1,512,128]{3,2,1,0:T(8,128)(2,1)}, bf16[4,1,512,128]{3,2,1,0:T(8,128)(2,1)}, u32[]{:S(2)}, u32[]{:S(2)}) collective-permute-start(bf16[4,1,512,128]{3,2,1,0:T(8,128)(2,1)} %pad_maximum_fusion.rest_0_), channel_id=1, source_target_pairs={{0,1},{1,2},{2,3},{3,0},{4,5},{5,6},{6,7},{7,4},{8,9},{9,10},{10,1... | collective-permute-start | bytes 1572872 | tf_op jit(solution)/shard_map/ppermute | solution.py:305
  20.1 1.3 %collective-permute-start.4 = (bf16[4,1,512,128]{3,2,1,0:T(8,128)(2,1)}, bf16[4,1,512,128]{3,2,1,0:T(8,128)(2,1)}, u32[]{:S(2)}, u32[]{:S(2)}) collective-permute-start(bf16[4,1,512,128]{3,2,1,0:T(8,128)(2,1)} %pad_maximum_fusion.rest_0_), channel_id=1, source_target_pairs={{0,3},{1,0},{2,1},{3,2},{4,7},{5,4},{6,5},{7,6},{8,11},{9,8},{10,9... | collective-permute-start | bytes 1572872 | tf_op jit(solution)/shard_map/ppermute | solution.py:305
  21.4 1.7 %collective-permute-start.5 = (bf16[4,1,512,128]{3,2,1,0:T(8,128)(2,1)}, bf16[4,1,512,128]{3,2,1,0:T(8,128)(2,1)}, u32[]{:S(2)}, u32[]{:S(2)}) collective-permute-start(bf16[4,1,512,128]{3,2,1,0:T(8,128)(2,1)} %pad_maximum_fusion.rest_0_), channel_id=1, source_target_pairs={{0,2},{1,3},{2,0},{3,1},{4,6},{5,7},{6,4},{7,5},{8,10},{9,11},{10,... | collective-permute-start | bytes 1572872 | tf_op jit(solution)/shard_map/ppermute | solution.py:305
  23.1 4.0 %all-to-all-done.served = s32[128,1,13]{2,1,0:T(1,128)S(1)} async-done(((s32[128,1,13]{2,1,0:T(1,128)}), s32[128,1,13]{2,1,0:T(1,128)S(1)}, u32[]{:S(2)}, u32[]{:S(2)}) %all-to-all-start) | async-done | bytes 6688 | tf_op jit(solution)/shard_map/all_to_all | solution.py:336
  27.1 6.4 %pick.1 = (bf16[1664,8,128]{2,1,0:T(8,128)(2,1)}, bf16[32,8,128]{2,1,0:T(8,128)(2,1)}) custom-call(s32[128,1,13]{2,1,0:T(1,128)S(1)} %all-to-all-done.served, s32[32]{0:T(128)} %target_rows.1, bf16[4096,1024]{1,0:T(8,128)(2,1)} %features.1), custom_call_target="tpu_custom_call" | custom-call | flops 8049999872 | bytes 1 | tf_op jit(solution)/shard_map/pick/pallas_call | solution.py:91
  33.5 4.9 %all-to-all-start.1 = ((bf16[128,104,128]{2,1,0:T(8,128)(2,1)}), bf16[128,104,128]{2,1,0:T(8,128)(2,1)S(1)}, u32[]{:S(2)}, u32[]{:S(2)}) async-start(bf16[128,104,128]{2,1,0:T(8,128)(2,1)} %bitcast.13), calls=%async_computation.1 | async-start | bytes 6815744 | tf_op jit(solution)/shard_map/all_to_all | solution.py:344
  39.4 1.2 %select_reduce_fusion.1 = s32[32,50]{0,1:T(8,128)S(1)} fusion(s32[128]{0:T(128)S(1)} %select_reduce_fusion.4, s32[32,50]{0,1:T(8,128)S(1)} %get-tuple-element.31), kind=kLoop, calls=%fused_computation.2 | loop fusion | flops 612800 | bytes 13312 | tf_op jit(solution)/shard_map/reduce_sum | solution.py:285
  40.7 0.9 select_reduce_fusion
  41.8 1.1 %collective-permute-start.6 = (bf16[4,1,512,128]{3,2,1,0:T(8,128)(2,1)}, bf16[4,1,512,128]{3,2,1,0:T(8,128)(2,1)S(1)}, u32[]{:S(2)}, u32[]{:S(2)}) collective-permute-start(bf16[4,1,512,128]{3,2,1,0:T(8,128)(2,1)} %pad_maximum_fusion.rest_0_), channel_id=1, source_target_pairs={{0,16},{16,0},{32,48},{48,32},{64,80},{80,64},{96,112},{112,96},{1... | collective-permute-start | bytes 1572872 | tf_op jit(solution)/shard_map/ppermute | solution.py:348
  43.8 0.8 collective-permute-done.6.rest_4_
  44.7 0.7 collective-permute-done.7.rest_5_
  45.4 0.7 collective-permute-done.8.rest_6_
  46.2 0.7 collective-permute-done.9.rest_7_
  47.7 0.8 copy-done.1
  48.5 5.7 %prepare.1 = (bf16[1024,2048]{1,0:T(8,128)(2,1)}, f32[32,1024]{1,0:T(8,128)}, bf16[64,800]{1,0:T(8,128)(2,1)}, f32[32,128]{1,0:T(8,128)}) custom-call(s32[2,32]{1,0:T(2,128)S(1)} %pad_add_fusion.blocks, bf16[32,8,128]{2,1,0:T(8,128)(2,1)S(1)} %copy-done.1, f32[32,800]{1,0:T(8,128)S(1)} %convert_element_type.3.shares, bf16[3072,1024]{1,0:T(8,128)(2,1)} %output_weight.3, ...), custom_call_target="tpu_custom_call" | custom-call | flops 20700000256 | bytes 1 | tf_op jit(solution)/shard_map/prepare/pallas_call | solution.py:166
  54.2 28.0 %all-to-all-done.1 = bf16[128,104,128]{2,1,0:T(8,128)(2,1)S(1)} async-done(((bf16[128,104,128]{2,1,0:T(8,128)(2,1)}), bf16[128,104,128]{2,1,0:T(8,128)(2,1)S(1)}, u32[]{:S(2)}, u32[]{:S(2)}) %all-to-all-start.1) | async-done | bytes 3407904 | tf_op jit(solution)/shard_map/all_to_all | solution.py:344
  82.2 8.3 %finish.1 = bf16[32,1024]{1,0:T(8,128)(2,1)} custom-call(s32[800]{0:T(1024)S(1)} %iota_add_fusion.source, bf16[1664,8,128]{2,1,0:T(8,128)(2,1)S(1)} %bitcast.11, bf16[64,800]{1,0:T(8,128)(2,1)} %get-tuple-element.27.parts_hbm, f32[32,128]{1,0:T(8,128)} %get-tuple-element.28.total_hbm, f32[32,1024]{1,0:T(8,128)} %get-tuple-element.29.base_hbm, ...), custom_call_target="tpu_custom_call" | custom-call | tf_op jit(solution)/shard_map/finish/pallas_call | solution.py:254
  (45 shorter events, 3.2 us)
Async XLA Ops:
  1.0 16.8 %collective-permute-start = (bf16[1,1,512,128]{3,2,1,0:T(8,128)(2,1)S(1)}, bf16[1,1,512,128]{3,2,1,0:T(8,128)(2,1)S(1)}, u32[]{:S(2)}, u32[]{:S(2)}) collective-permute-start(bf16[1,1,512,128]{3,2,1,0:T(8,128)(2,1)S(1)} %select_bitcast_fusion), channel_id=1, source_target_pairs={{0,4},{1,5},{2,6},{3,7},{4,8},{5,9},{6,10},{7,11},{8,12},{9,13},{1... | collective-permute-start | bytes 393224 | tf_op jit(solution)/shard_map/ppermute | solution.py:305
  3.5 14.3 %collective-permute-start.1 = (bf16[1,1,512,128]{3,2,1,0:T(8,128)(2,1)S(1)}, bf16[1,1,512,128]{3,2,1,0:T(8,128)(2,1)S(1)}, u32[]{:S(2)}, u32[]{:S(2)}) collective-permute-start(bf16[1,1,512,128]{3,2,1,0:T(8,128)(2,1)S(1)} %select_bitcast_fusion), channel_id=1, source_target_pairs={{0,12},{1,13},{2,14},{3,15},{4,0},{5,1},{6,2},{7,3},{8,4},{9,5},{1... | collective-permute-start | bytes 393224 | tf_op jit(solution)/shard_map/ppermute | solution.py:305
  5.7 12.1 %collective-permute-start.2 = (bf16[1,1,512,128]{3,2,1,0:T(8,128)(2,1)S(1)}, bf16[1,1,512,128]{3,2,1,0:T(8,128)(2,1)S(1)}, u32[]{:S(2)}, u32[]{:S(2)}) collective-permute-start(bf16[1,1,512,128]{3,2,1,0:T(8,128)(2,1)S(1)} %select_bitcast_fusion), channel_id=1, source_target_pairs={{0,8},{1,9},{2,10},{3,11},{4,12},{5,13},{6,14},{7,15},{8,0},{9,1},... | collective-permute-start | bytes 393224 | tf_op jit(solution)/shard_map/ppermute | solution.py:305
  8.4 18.7 %all-to-all-start = ((s32[128,1,13]{2,1,0:T(1,128)}), s32[128,1,13]{2,1,0:T(1,128)S(1)}, u32[]{:S(2)}, u32[]{:S(2)}) async-start(s32[128,1,13]{2,1,0:T(1,128)} %bitcast.1), calls=%async_computation | async-start | bytes 131072 | tf_op jit(solution)/shard_map/all_to_all | solution.py:336
  18.7 19.8 %collective-permute-start.3 = (bf16[4,1,512,128]{3,2,1,0:T(8,128)(2,1)}, bf16[4,1,512,128]{3,2,1,0:T(8,128)(2,1)}, u32[]{:S(2)}, u32[]{:S(2)}) collective-permute-start(bf16[4,1,512,128]{3,2,1,0:T(8,128)(2,1)} %pad_maximum_fusion.rest_0_), channel_id=1, source_target_pairs={{0,1},{1,2},{2,3},{3,0},{4,5},{5,6},{6,7},{7,4},{8,9},{9,10},{10,1... | collective-permute-start | bytes 1572872 | tf_op jit(solution)/shard_map/ppermute | solution.py:305
  20.1 18.4 %collective-permute-start.4 = (bf16[4,1,512,128]{3,2,1,0:T(8,128)(2,1)}, bf16[4,1,512,128]{3,2,1,0:T(8,128)(2,1)}, u32[]{:S(2)}, u32[]{:S(2)}) collective-permute-start(bf16[4,1,512,128]{3,2,1,0:T(8,128)(2,1)} %pad_maximum_fusion.rest_0_), channel_id=1, source_target_pairs={{0,3},{1,0},{2,1},{3,2},{4,7},{5,4},{6,5},{7,6},{8,11},{9,8},{10,9... | collective-permute-start | bytes 1572872 | tf_op jit(solution)/shard_map/ppermute | solution.py:305
  21.4 17.1 %collective-permute-start.5 = (bf16[4,1,512,128]{3,2,1,0:T(8,128)(2,1)}, bf16[4,1,512,128]{3,2,1,0:T(8,128)(2,1)}, u32[]{:S(2)}, u32[]{:S(2)}) collective-permute-start(bf16[4,1,512,128]{3,2,1,0:T(8,128)(2,1)} %pad_maximum_fusion.rest_0_), channel_id=1, source_target_pairs={{0,2},{1,3},{2,0},{3,1},{4,6},{5,7},{6,4},{7,5},{8,10},{9,11},{10,... | collective-permute-start | bytes 1572872 | tf_op jit(solution)/shard_map/ppermute | solution.py:305
  33.5 5.0 %copy-start.2 = (s32[32,50]{1,0:T(8,128)S(1)}, s32[32,50]{1,0:T(8,128)}, u32[]{:S(2)}) copy-start(s32[32,50]{1,0:T(8,128)} %param.13) | copy-start | bytes 19204
  33.5 7.1 %copy-start.3 = (s32[32,50]{1,0:T(8,128)S(1)}, s32[32,50]{1,0:T(8,128)}, u32[]{:S(2)}) copy-start(s32[32,50]{1,0:T(8,128)} %param.14) | copy-start | bytes 19204
  33.5 8.0 %copy-start.4 = (s32[4]{0:T(128)S(1)}, s32[4]{0:T(128)}, u32[]{:S(2)}) copy-start(s32[4]{0:T(128)} %constant.85.clone) | copy-start | bytes 52
  33.5 14.2 %copy-start = (f32[1024]{0:T(1024)S(1)}, f32[1024]{0:T(1024)}, u32[]{:S(2)}) copy-start(f32[1024]{0:T(1024)} %param.18) | copy-start | bytes 12292
  33.5 48.7 %all-to-all-start.1 = ((bf16[128,104,128]{2,1,0:T(8,128)(2,1)}), bf16[128,104,128]{2,1,0:T(8,128)(2,1)S(1)}, u32[]{:S(2)}, u32[]{:S(2)}) async-start(bf16[128,104,128]{2,1,0:T(8,128)(2,1)} %bitcast.13), calls=%async_computation.1 | async-start | bytes 6815744 | tf_op jit(solution)/shard_map/all_to_all | solution.py:344
  41.8 2.8 %collective-permute-start.6 = (bf16[4,1,512,128]{3,2,1,0:T(8,128)(2,1)}, bf16[4,1,512,128]{3,2,1,0:T(8,128)(2,1)S(1)}, u32[]{:S(2)}, u32[]{:S(2)}) collective-permute-start(bf16[4,1,512,128]{3,2,1,0:T(8,128)(2,1)} %pad_maximum_fusion.rest_0_), channel_id=1, source_target_pairs={{0,16},{16,0},{32,48},{48,32},{64,80},{80,64},{96,112},{112,96},{1... | collective-permute-start | bytes 1572872 | tf_op jit(solution)/shard_map/ppermute | solution.py:348
  42.9 2.5 %collective-permute-start.7 = (bf16[4,1,512,128]{3,2,1,0:T(8,128)(2,1)}, bf16[4,1,512,128]{3,2,1,0:T(8,128)(2,1)S(1)}, u32[]{:S(2)}, u32[]{:S(2)}) collective-permute-start(bf16[4,1,512,128]{3,2,1,0:T(8,128)(2,1)} %collective-permute-done.3.rest_1_), channel_id=1, source_target_pairs={{0,16},{16,0},{32,48},{48,32},{64,80},{80,64},{96,112},{112,96},{1... | collective-permute-start | bytes 1572872 | tf_op jit(solution)/shard_map/ppermute | solution.py:348
  43.0 3.2 %collective-permute-start.8 = (bf16[4,1,512,128]{3,2,1,0:T(8,128)(2,1)}, bf16[4,1,512,128]{3,2,1,0:T(8,128)(2,1)S(1)}, u32[]{:S(2)}, u32[]{:S(2)}) collective-permute-start(bf16[4,1,512,128]{3,2,1,0:T(8,128)(2,1)} %collective-permute-done.4.rest_2_), channel_id=1, source_target_pairs={{0,16},{16,0},{32,48},{48,32},{64,80},{80,64},{96,112},{112,96},{1... | collective-permute-start | bytes 1572872 | tf_op jit(solution)/shard_map/ppermute | solution.py:348
  43.4 3.5 %collective-permute-start.9 = (bf16[4,1,512,128]{3,2,1,0:T(8,128)(2,1)}, bf16[4,1,512,128]{3,2,1,0:T(8,128)(2,1)S(1)}, u32[]{:S(2)}, u32[]{:S(2)}) collective-permute-start(bf16[4,1,512,128]{3,2,1,0:T(8,128)(2,1)} %collective-permute-done.5.rest_3_), channel_id=1, source_target_pairs={{0,16},{16,0},{32,48},{48,32},{64,80},{80,64},{96,112},{112,96},{1... | collective-permute-start | bytes 1572872 | tf_op jit(solution)/shard_map/ppermute | solution.py:348
  44.7 2.3 %copy-start.5 = (bf16[4,1,512,128]{3,2,1,0:T(8,128)(2,1)}, bf16[4,1,512,128]{3,2,1,0:T(8,128)(2,1)S(1)}, u32[]{:S(2)}) copy-start(bf16[4,1,512,128]{3,2,1,0:T(8,128)(2,1)S(1)} %collective-permute-done.6.rest_4_) | copy-start | bytes 1572868
  45.4 1.5 %copy-start.6 = (bf16[4,1,512,128]{3,2,1,0:T(8,128)(2,1)}, bf16[4,1,512,128]{3,2,1,0:T(8,128)(2,1)S(1)}, u32[]{:S(2)}) copy-start(bf16[4,1,512,128]{3,2,1,0:T(8,128)(2,1)S(1)} %collective-permute-done.7.rest_5_) | copy-start | bytes 1572868
  46.2 0.8 copy-start.7
  46.9 0.8 copy-start.8
  47.7 0.8 copy-start.1

commit v5 on v4

--- a/solution.py
+++ b/solution.py
@@ -193,13 +193,15 @@
 
 
 def finish_kernel(
-    source, arrived, parts_hbm, total_hbm, base_hbm, hidden_bias_hbm, hidden_weight, output_weight,
-    embedding, spread, live_rows, pooled, held_hidden, held_output, parts, total, base, hidden_bias, sems,
+    source_hbm, arrived, parts_hbm, total_hbm, base_hbm, hidden_bias_hbm, hidden_weight, output_weight,
+    embedding, source, spread, live_rows, pooled, held_hidden, held_output, parts, total, base, hidden_bias, sems,
 ):
     chunks = arrived.shape[1]
     targets, hidden = pooled.shape
     blocks = hidden // BLOCK
     small = ((parts_hbm, parts), (total_hbm, total), (base_hbm, base), (hidden_bias_hbm, hidden_bias))
+    slots = pltpu.make_async_copy(source_hbm, source, sems.at[blocks + 5])
+    slots.start()
     rest = [pltpu.make_async_copy(x, held, sems.at[blocks + 1 + at]) for at, (x, held) in enumerate(small)]
     for load in rest:
         load.start()
@@ -222,6 +224,7 @@
             live_rows[rows, pl.ds(chunk * LANES, LANES)] = part.astype(jnp.bfloat16)
         return carry
 
+    slots.wait()
     lax.fori_loop(0, LIVE // GROUP, group, 0)
     skipped = output_weight.shape[0] - hidden
     last_rows = pltpu.make_async_copy(output_weight.at[pl.ds(skipped, hidden)], held_output, sems.at[blocks])
@@ -249,14 +252,14 @@
     width, hidden = hidden_weight.shape
     units = output_weight.shape[1]
     vmem = pl.BlockSpec(memory_space=pltpu.VMEM)
-    smem = pl.BlockSpec(memory_space=pltpu.SMEM)
     hbm = pl.BlockSpec(memory_space=pltpu.HBM)
     return pl.pallas_call(
         finish_kernel,
         out_shape=jax.ShapeDtypeStruct((targets, units), jnp.bfloat16),
-        in_specs=[smem, vmem] + [hbm] * 6,
+        in_specs=[hbm, vmem] + [hbm] * 6,
         out_specs=vmem,
         scratch_shapes=[
+            pltpu.SMEM(source.shape, jnp.int32),
             pltpu.VMEM((2 * GROUP * chunks, LANES), jnp.float32),
             pltpu.VMEM((LIVE, width), jnp.bfloat16),
             pltpu.VMEM((targets, hidden), jnp.bfloat16),
@@ -266,12 +269,12 @@
             pltpu.VMEM(total.shape, jnp.float32),
             pltpu.VMEM(base.shape, jnp.float32),
             pltpu.VMEM((1, hidden), jnp.float32),
-            pltpu.SemaphoreType.DMA((hidden // BLOCK + 5,)),
+            pltpu.SemaphoreType.DMA((hidden // BLOCK + 6,)),
         ],
         compiler_params=GRANT,
         name="finish",
     )(
-        source, pltpu.with_memory_space_constraint(arrived, pltpu.VMEM), in_hbm(parts), in_hbm(total),
+        in_hbm(source), pltpu.with_memory_space_constraint(arrived, pltpu.VMEM), in_hbm(parts), in_hbm(total),
         in_hbm(base), in_hbm(hidden_bias.reshape(1, -1)), in_hbm(hidden_weight), in_hbm(output_weight),
     )
 
@@ -305,13 +308,40 @@
     return lax.ppermute(x, AXES, pairs)
 
 
-def own_half(weight):
-    halves = weight.reshape(2, 1, weight.shape[0] // 2, weight.shape[1])
-    return jnp.where(lax.axis_index("dom") % 2 == 0, halves[:1], halves[1:])
+def join_kernel(*refs):
+    weights, (out, held, sems) = refs[:-3], refs[-3:]
+    half = out.shape[2]
+    core = lax.rem(lax.axis_index("dom"), 2)
+    rows = pl.ds(pl.multiple_of(core * half, half), half)
+    copies = [pltpu.make_async_copy(x.at[rows], held.at[at, 0], sems.at[at]) for at, x in enumerate(weights)]
+    for copy in copies:
+        copy.start()
+    for copy in copies:
+        copy.wait()
+    whole = pltpu.make_async_copy(held, out, sems.at[len(weights)])
+    whole.start()
+    whole.wait()
+
+
+def join(weights):
+    rows, columns = weights[0].shape
+    return pl.pallas_call(
+        join_kernel,
+        out_shape=pltpu.HBM((len(weights), 1, rows // 2, columns), weights[0].dtype),
+        in_specs=[pl.BlockSpec(memory_space=pl.ANY)] * len(weights),
+        out_specs=pl.BlockSpec(memory_space=pltpu.HBM),
+        scratch_shapes=[
+            pltpu.VMEM((len(weights), 1, rows // 2, columns), weights[0].dtype),
+            pltpu.SemaphoreType.DMA((len(weights) + 1,)),
+        ],
+        compiler_params=pltpu.CompilerParams(vmem_limit_bytes=4 * 2**20),
+        cost_estimate=takes(1),
+        name="join",
+    )(in_hbm(weights[0]), *weights[1:])
 
 
 def block_places(back):
-    core = lax.axis_index("dom") % 2
+    core = lax.axis_index("dom") % 2 + back[0]
     row, column = lax.axis_index("grp") // 4, lax.axis_index("grp") % 4
     rows, columns = (row - back) % 4, (column - back) % 4
     of_core0 = (rows[None, :] * 4 + columns[:, None]).reshape(-1)
@@ -334,9 +364,7 @@
 ):
     _, peers, capacity = requests.shape
     served = lax.all_to_all(requests.reshape(peers, 1, capacity), AXES, split_axis=0, concat_axis=0, tiled=True)
-    own_part = own_half(hidden_weight)
-    near = [own_part] + [shifted(own_part, False, by) for by in SHIFTS[1:]]
-    near = jnp.concatenate(near, axis=0)
+    near = join([hidden_weight] + [shifted(hidden_weight, False, by) for by in SHIFTS[1:]])
     mine = [near] + [shifted(near, True, by) for by in SHIFTS[1:]]
     outgoing, own = pick(served, target_rows, features)
     tile = outgoing.shape[1:]

time: 91 us -> 90.7 us (level)
  waiting for transfers between devices: 35.1 us -> 25.2 us
  other arithmetic: 5.15 us -> 8.69 us
  local copies, waits for them, and re-layouts: 3.59 us -> 6.96 us
  Pallas kernels: 20.4 us -> 22 us
    all_to_all x1, waiting for transfers between devices: 28 us -> 21.4 us  [on_device(): lax.all_to_all(blocks, AXES, split_axis=0, concat_axis=0, tiled=True)]
    ppermute x4, waiting for transfers between devices: 3.07 us -> 0.52 us  [on_device(): lax.ppermute(part, 'dom', [(dom, dom ^ 1) for dom in range(8)])]
    pallas_call x0 -> x1, Pallas kernels: none -> 1.78 us  [join(): pl.pallas_call(join_kernel, out_shape=pltpu.HBM((len(weights), 1, rows //...]
    select_n x1, local copies, waits for them, and re-layouts: 0.09 us -> 1.33 us  [block_places(): jnp.where(core == 0, of_core0, of_core1)]
    broadcast_in_dim x1, local copies, waits for them, and re-layouts: 0.07 us -> 1.26 us  [block_places(): half = jnp.repeat(jnp.stack([core, 1 - core]), 16)]
    select_n x1 -> x0, other arithmetic: 0.98 us -> none  [own_half(): return jnp.where(lax.axis_index('dom') % 2 == 0, halves[:1], halves[1:])]
    unnamed x19 -> x21, local copies, waits for them, and re-layouts: 3.09 us -> 2.26 us
  transfers between devices with their start and end apart: 12 -> 12, of which waited for: 6 -> 3; matrix products, arithmetic and copies ran while one was open for 7% -> 16% of each run, Pallas kernels for 13% -> 15%
where the time goes in v5:
time: 90.7 us; the launch traced here: 90.3 us
  starting transfers between devices  27 us (30%)
  waiting for transfers between devices  25.2 us (28%)
  Pallas kernels  22 us (24%)
  other arithmetic  8.69 us (10%)
  local copies, waits for them, and re-layouts  6.96 us (8%)
    all_to_all x1, waiting for transfers between devices, on_device(): lax.all_to_all(blocks, AXES, split_axis=0, concat_axis=0, tiled=True)  21.4 us
    ppermute x6, starting transfers between devices, shifted(): return lax.ppermute(x, AXES, pairs)  10.3 us
    all_to_all x1, starting transfers between devices, on_device(): lax.all_to_all(requests.reshape(peers, 1, capacity), AXES, split_axis=0,...  9.18 us
    pallas_call x1, Pallas kernels, finish(): pl.pallas_call(finish_kernel, out_shape=jax.ShapeDtypeStruct((targets, un...  8.11 us
    pallas_call x1, Pallas kernels, pick(): pl.pallas_call(pick_kernel, out_shape=(pltpu.HBM((peers * capacity,) + ti...  6.42 us
    all_to_all x1, starting transfers between devices, on_device(): lax.all_to_all(blocks, AXES, split_axis=0, concat_axis=0, tiled=True)  5.76 us
    pallas_call x1, Pallas kernels, prepare(): pl.pallas_call(prepare_kernel, out_shape=(pltpu.HBM((width, hidden), jnp....  5.69 us
    all_to_all x1, waiting for transfers between devices, on_device(): lax.all_to_all(requests.reshape(peers, 1, capacity), AXES, split_axis=0,...  3.24 us
  transfers between devices with their start and end apart: 12, of which 3 were waited for; matrix products, arithmetic and copies ran while one was open for 16% of the time, Pallas kernels for 15%

profile of v5, /device:TPU:1, one launch (start us, length us, event | category | flops | bytes accessed | tf_op | source)
XLA Modules:
  0.0 90.3 jit_solution(5071356282881037774)
XLA Ops:
  0.0 2.5 %collective-permute-start = (bf16[1024,128]{1,0:T(8,128)(2,1)}, bf16[1024,128]{1,0:T(8,128)(2,1)S(1)}, u32[]{:S(2)}, u32[]{:S(2)}) collective-permute-start(bf16[1024,128]{1,0:T(8,128)(2,1)} %refs_0_.1), channel_id=1, source_target_pairs={{0,4},{1,5},{2,6},{3,7},{4,8},{5,9},{6,10},{7,11},{8,12},{9,13},{1... | collective-permute-start | bytes 786440 | tf_op jit(solution)/shard_map/ppermute | solution.py:308
  2.5 2.1 %collective-permute-start.1 = (bf16[1024,128]{1,0:T(8,128)(2,1)}, bf16[1024,128]{1,0:T(8,128)(2,1)S(1)}, u32[]{:S(2)}, u32[]{:S(2)}) collective-permute-start(bf16[1024,128]{1,0:T(8,128)(2,1)} %refs_0_.1), channel_id=1, source_target_pairs={{0,12},{1,13},{2,14},{3,15},{4,0},{5,1},{6,2},{7,3},{8,4},{9,5},{1... | collective-permute-start | bytes 786440 | tf_op jit(solution)/shard_map/ppermute | solution.py:308
  4.6 1.3 %collective-permute-start.2 = (bf16[1024,128]{1,0:T(8,128)(2,1)}, bf16[1024,128]{1,0:T(8,128)(2,1)S(1)}, u32[]{:S(2)}, u32[]{:S(2)}) collective-permute-start(bf16[1024,128]{1,0:T(8,128)(2,1)} %refs_0_.1), channel_id=1, source_target_pairs={{0,8},{1,9},{2,10},{3,11},{4,12},{5,13},{6,14},{7,15},{8,0},{9,1},... | collective-permute-start | bytes 786440 | tf_op jit(solution)/shard_map/ppermute | solution.py:308
  5.9 1.4 %copy.15 = s32[1,128,13]{2,1,0:T(8,128)} copy(s32[1,128,13]{1,0,2:T(1,128)} %param.11) | data formatting | bytes 13312 | tf_op args[1]
  7.3 9.2 %all-to-all-start = ((s32[128,1,13]{2,1,0:T(1,128)}), s32[128,1,13]{2,1,0:T(1,128)S(1)}, u32[]{:S(2)}, u32[]{:S(2)}) async-start(s32[128,1,13]{2,1,0:T(1,128)} %bitcast), calls=%async_computation | async-start | bytes 131072 | tf_op jit(solution)/shard_map/all_to_all | solution.py:366
  16.6 1.8 %join.1.rest_0_ = bf16[4,1,512,128]{3,2,1,0:T(8,128)(2,1)} custom-call(bf16[1024,128]{1,0:T(8,128)(2,1)} %refs_0_.1, bf16[1024,128]{1,0:T(8,128)(2,1)S(1)} %collective-permute-done.refs_1_, bf16[1024,128]{1,0:T(8,128)(2,1)S(1)} %collective-permute-done.1.refs_2_, bf16[1024,128]{1,0:T(8,128)(2,1)S(1)} %collective-permute-done.2.refs_3_), custom_call_target="tpu_custom_call" | custom-call | flops 1150000000 | bytes 1 | tf_op jit(solution)/shard_map/join/pallas_call | solution.py:328
  18.3 1.5 %collective-permute-start.3 = (bf16[4,1,512,128]{3,2,1,0:T(8,128)(2,1)}, bf16[4,1,512,128]{3,2,1,0:T(8,128)(2,1)}, u32[]{:S(2)}, u32[]{:S(2)}) collective-permute-start(bf16[4,1,512,128]{3,2,1,0:T(8,128)(2,1)} %join.1.rest_0_), channel_id=1, source_target_pairs={{0,1},{1,2},{2,3},{3,0},{4,5},{5,6},{6,7},{7,4},{8,9},{9,10},{10,1... | collective-permute-start | bytes 1572872 | tf_op jit(solution)/shard_map/ppermute | solution.py:308
  19.8 1.3 %collective-permute-start.4 = (bf16[4,1,512,128]{3,2,1,0:T(8,128)(2,1)}, bf16[4,1,512,128]{3,2,1,0:T(8,128)(2,1)}, u32[]{:S(2)}, u32[]{:S(2)}) collective-permute-start(bf16[4,1,512,128]{3,2,1,0:T(8,128)(2,1)} %join.1.rest_0_), channel_id=1, source_target_pairs={{0,3},{1,0},{2,1},{3,2},{4,7},{5,4},{6,5},{7,6},{8,11},{9,8},{10,9... | collective-permute-start | bytes 1572872 | tf_op jit(solution)/shard_map/ppermute | solution.py:308
  21.2 1.6 %collective-permute-start.5 = (bf16[4,1,512,128]{3,2,1,0:T(8,128)(2,1)}, bf16[4,1,512,128]{3,2,1,0:T(8,128)(2,1)}, u32[]{:S(2)}, u32[]{:S(2)}) collective-permute-start(bf16[4,1,512,128]{3,2,1,0:T(8,128)(2,1)} %join.1.rest_0_), channel_id=1, source_target_pairs={{0,2},{1,3},{2,0},{3,1},{4,6},{5,7},{6,4},{7,5},{8,10},{9,11},{10,... | collective-permute-start | bytes 1572872 | tf_op jit(solution)/shard_map/ppermute | solution.py:308
  22.8 3.2 %all-to-all-done.served = s32[128,1,13]{2,1,0:T(1,128)S(1)} async-done(((s32[128,1,13]{2,1,0:T(1,128)}), s32[128,1,13]{2,1,0:T(1,128)S(1)}, u32[]{:S(2)}, u32[]{:S(2)}) %all-to-all-start) | async-done | bytes 6688 | tf_op jit(solution)/shard_map/all_to_all | solution.py:366
  26.0 6.4 %pick.1 = (bf16[1664,8,128]{2,1,0:T(8,128)(2,1)}, bf16[32,8,128]{2,1,0:T(8,128)(2,1)}) custom-call(s32[128,1,13]{2,1,0:T(1,128)S(1)} %all-to-all-done.served, s32[32]{0:T(128)} %target_rows.1, bf16[4096,1024]{1,0:T(8,128)(2,1)} %features.1), custom_call_target="tpu_custom_call" | custom-call | flops 8049999872 | bytes 1 | tf_op jit(solution)/shard_map/pick/pallas_call | solution.py:91
  32.5 5.8 %all-to-all-start.1 = ((bf16[128,104,128]{2,1,0:T(8,128)(2,1)}), bf16[128,104,128]{2,1,0:T(8,128)(2,1)S(1)}, u32[]{:S(2)}, u32[]{:S(2)}) async-start(bf16[128,104,128]{2,1,0:T(8,128)(2,1)} %bitcast.13), calls=%async_computation.1 | async-start | bytes 6815744 | tf_op jit(solution)/shard_map/all_to_all | solution.py:372
  41.0 1.3 %select_n.86 = s32[16]{0:T(128)} reshape(s32[4,4]{1,0:T(4,128)} %get-tuple-element.33) | data formatting | bytes 128 | tf_op jit(solution)/shard_map/jit(_where)/select_n | solution.py:349
  42.9 1.3 %broadcast_in_dim.76 = s32[2,16]{1,0:T(2,128)} broadcast(s32[2]{0:T(128)} %pad_add_fusion.1), dimensions={0} | broadcast | bytes 136 | tf_op jit(solution)/shard_map/broadcast_in_dim | solution.py:350
  44.2 0.7 stack_reshape.3
  44.9 0.7 copy.16
  45.6 1.7 %select_reduce_fusion.1 = s32[32,50]{0,1:T(8,128)S(1)} fusion(s32[128]{0:T(128)} %select_reduce_fusion.4, s32[32,50]{0,1:T(8,128)S(1)} %get-tuple-element.31), kind=kLoop, calls=%fused_computation.2 | loop fusion | flops 612800 | bytes 13312 | tf_op jit(solution)/shard_map/reduce_sum | solution.py:288
  47.4 1.6 %select_reduce_fusion = s32[32,800]{1,0:T(8,128)S(1)} fusion(s32[32,50]{0,1:T(8,128)} %copy.16, s32[32,50]{0,1:T(8,128)S(1)} %fusion.2), kind=kLoop, calls=%fused_computation | loop fusion | flops 3814400 | bytes 115200 | tf_op jit(solution)/shard_map/reduce_sum | solution.py:291
  49.0 1.1 %collective-permute-start.6 = (bf16[4,1,512,128]{3,2,1,0:T(8,128)(2,1)}, bf16[4,1,512,128]{3,2,1,0:T(8,128)(2,1)S(1)}, u32[]{:S(2)}, u32[]{:S(2)}) collective-permute-start(bf16[4,1,512,128]{3,2,1,0:T(8,128)(2,1)} %join.1.rest_0_), channel_id=1, source_target_pairs={{0,16},{16,0},{32,48},{48,32},{64,80},{80,64},{96,112},{112,96},{1... | collective-permute-start | bytes 1572872 | tf_op jit(solution)/shard_map/ppermute | solution.py:376
  50.7 0.8 add_bitcast_fusion
  52.2 0.8 select_reduce_fusion.3
  54.9 5.7 %prepare.1 = (bf16[1024,2048]{1,0:T(8,128)(2,1)}, f32[32,1024]{1,0:T(8,128)}, bf16[64,800]{1,0:T(8,128)(2,1)}, f32[32,128]{1,0:T(8,128)}) custom-call(s32[2,32]{1,0:T(2,128)S(1)} %pad_add_fusion.blocks, bf16[32,8,128]{2,1,0:T(8,128)(2,1)S(1)} %copy-done.1, f32[32,800]{1,0:T(8,128)S(1)} %convert_element_type.3.shares, bf16[3072,1024]{1,0:T(8,128)(2,1)} %output_weight.3, ...), custom_call_target="tpu_custom_call" | custom-call | flops 20700000256 | bytes 1 | tf_op jit(solution)/shard_map/prepare/pallas_call | solution.py:166
  60.6 21.4 %all-to-all-done.1 = bf16[128,104,128]{2,1,0:T(8,128)(2,1)S(1)} async-done(((bf16[128,104,128]{2,1,0:T(8,128)(2,1)}), bf16[128,104,128]{2,1,0:T(8,128)(2,1)S(1)}, u32[]{:S(2)}, u32[]{:S(2)}) %all-to-all-start.1) | async-done | bytes 3407904 | tf_op jit(solution)/shard_map/all_to_all | solution.py:372
  82.0 8.1 %finish.1 = bf16[32,1024]{1,0:T(8,128)(2,1)} custom-call(s32[800]{0:T(1024)} %iota_add_fusion.source_hbm, bf16[1664,8,128]{2,1,0:T(8,128)(2,1)S(1)} %bitcast.11, bf16[64,800]{1,0:T(8,128)(2,1)} %get-tuple-element.27.parts_hbm, f32[32,128]{1,0:T(8,128)} %get-tuple-element.28.total_hbm, f32[32,1024]{1,0:T(8,128)} %get-tuple-element.29.base_hbm, ...), custom_call_target="tpu_custom_call" | custom-call | tf_op jit(solution)/shard_map/finish/pallas_call | solution.py:256
  (46 shorter events, 6.5 us)
Async XLA Ops:
  0.0 16.5 %collective-permute-start = (bf16[1024,128]{1,0:T(8,128)(2,1)}, bf16[1024,128]{1,0:T(8,128)(2,1)S(1)}, u32[]{:S(2)}, u32[]{:S(2)}) collective-permute-start(bf16[1024,128]{1,0:T(8,128)(2,1)} %refs_0_.1), channel_id=1, source_target_pairs={{0,4},{1,5},{2,6},{3,7},{4,8},{5,9},{6,10},{7,11},{8,12},{9,13},{1... | collective-permute-start | bytes 786440 | tf_op jit(solution)/shard_map/ppermute | solution.py:308
  2.5 14.1 %collective-permute-start.1 = (bf16[1024,128]{1,0:T(8,128)(2,1)}, bf16[1024,128]{1,0:T(8,128)(2,1)S(1)}, u32[]{:S(2)}, u32[]{:S(2)}) collective-permute-start(bf16[1024,128]{1,0:T(8,128)(2,1)} %refs_0_.1), channel_id=1, source_target_pairs={{0,12},{1,13},{2,14},{3,15},{4,0},{5,1},{6,2},{7,3},{8,4},{9,5},{1... | collective-permute-start | bytes 786440 | tf_op jit(solution)/shard_map/ppermute | solution.py:308
  4.6 12.0 %collective-permute-start.2 = (bf16[1024,128]{1,0:T(8,128)(2,1)}, bf16[1024,128]{1,0:T(8,128)(2,1)S(1)}, u32[]{:S(2)}, u32[]{:S(2)}) collective-permute-start(bf16[1024,128]{1,0:T(8,128)(2,1)} %refs_0_.1), channel_id=1, source_target_pairs={{0,8},{1,9},{2,10},{3,11},{4,12},{5,13},{6,14},{7,15},{8,0},{9,1},... | collective-permute-start | bytes 786440 | tf_op jit(solution)/shard_map/ppermute | solution.py:308
  7.3 18.7 %all-to-all-start = ((s32[128,1,13]{2,1,0:T(1,128)}), s32[128,1,13]{2,1,0:T(1,128)S(1)}, u32[]{:S(2)}, u32[]{:S(2)}) async-start(s32[128,1,13]{2,1,0:T(1,128)} %bitcast), calls=%async_computation | async-start | bytes 131072 | tf_op jit(solution)/shard_map/all_to_all | solution.py:366
  18.3 19.9 %collective-permute-start.3 = (bf16[4,1,512,128]{3,2,1,0:T(8,128)(2,1)}, bf16[4,1,512,128]{3,2,1,0:T(8,128)(2,1)}, u32[]{:S(2)}, u32[]{:S(2)}) collective-permute-start(bf16[4,1,512,128]{3,2,1,0:T(8,128)(2,1)} %join.1.rest_0_), channel_id=1, source_target_pairs={{0,1},{1,2},{2,3},{3,0},{4,5},{5,6},{6,7},{7,4},{8,9},{9,10},{10,1... | collective-permute-start | bytes 1572872 | tf_op jit(solution)/shard_map/ppermute | solution.py:308
  19.8 18.5 %collective-permute-start.4 = (bf16[4,1,512,128]{3,2,1,0:T(8,128)(2,1)}, bf16[4,1,512,128]{3,2,1,0:T(8,128)(2,1)}, u32[]{:S(2)}, u32[]{:S(2)}) collective-permute-start(bf16[4,1,512,128]{3,2,1,0:T(8,128)(2,1)} %join.1.rest_0_), channel_id=1, source_target_pairs={{0,3},{1,0},{2,1},{3,2},{4,7},{5,4},{6,5},{7,6},{8,11},{9,8},{10,9... | collective-permute-start | bytes 1572872 | tf_op jit(solution)/shard_map/ppermute | solution.py:308
  21.2 17.1 %collective-permute-start.5 = (bf16[4,1,512,128]{3,2,1,0:T(8,128)(2,1)}, bf16[4,1,512,128]{3,2,1,0:T(8,128)(2,1)}, u32[]{:S(2)}, u32[]{:S(2)}) collective-permute-start(bf16[4,1,512,128]{3,2,1,0:T(8,128)(2,1)} %join.1.rest_0_), channel_id=1, source_target_pairs={{0,2},{1,3},{2,0},{3,1},{4,6},{5,7},{6,4},{7,5},{8,10},{9,11},{10,... | collective-permute-start | bytes 1572872 | tf_op jit(solution)/shard_map/ppermute | solution.py:308
  32.4 5.9 %copy-start.5 = (s32[4]{0:T(128)S(1)}, s32[4]{0:T(128)}, u32[]{:S(2)}) copy-start(s32[4]{0:T(128)} %constant.83.clone) | copy-start | bytes 52
  32.5 5.9 %copy-start.2 = (s32[32,50]{1,0:T(8,128)S(1)}, s32[32,50]{1,0:T(8,128)}, u32[]{:S(2)}) copy-start(s32[32,50]{1,0:T(8,128)} %param.13) | copy-start | bytes 19204
  32.5 12.5 %copy-start.3 = (s32[32,50]{1,0:T(8,128)S(1)}, s32[32,50]{1,0:T(8,128)}, u32[]{:S(2)}) copy-start(s32[32,50]{1,0:T(8,128)} %param.14) | copy-start | bytes 19204
  32.5 22.4 %copy-start = (f32[1024]{0:T(1024)S(1)}, f32[1024]{0:T(1024)}, u32[]{:S(2)}) copy-start(f32[1024]{0:T(1024)} %param.18) | copy-start | bytes 12292
  32.5 22.4 %copy-start.1 = (bf16[32,8,128]{2,1,0:T(8,128)(2,1)S(1)}, bf16[32,8,128]{2,1,0:T(8,128)(2,1)}, u32[]{:S(2)}) copy-start(bf16[32,8,128]{2,1,0:T(8,128)(2,1)} %get-tuple-element.21.own) | copy-start | bytes 196612
  32.5 49.5 %all-to-all-start.1 = ((bf16[128,104,128]{2,1,0:T(8,128)(2,1)}), bf16[128,104,128]{2,1,0:T(8,128)(2,1)S(1)}, u32[]{:S(2)}, u32[]{:S(2)}) async-start(bf16[128,104,128]{2,1,0:T(8,128)(2,1)} %bitcast.13), calls=%async_computation.1 | async-start | bytes 6815744 | tf_op jit(solution)/shard_map/all_to_all | solution.py:372
  39.2 1.3 %copy-start.4 = (s32[128]{0:T(128)}, s32[128]{0:T(128)S(1)}, u32[]{:S(2)}) copy-start(s32[128]{0:T(128)S(1)} %select_reduce_fusion.2) | copy-start | bytes 1540
  49.0 4.6 %collective-permute-start.6 = (bf16[4,1,512,128]{3,2,1,0:T(8,128)(2,1)}, bf16[4,1,512,128]{3,2,1,0:T(8,128)(2,1)S(1)}, u32[]{:S(2)}, u32[]{:S(2)}) collective-permute-start(bf16[4,1,512,128]{3,2,1,0:T(8,128)(2,1)} %join.1.rest_0_), channel_id=1, source_target_pairs={{0,16},{16,0},{32,48},{48,32},{64,80},{80,64},{96,112},{112,96},{1... | collective-permute-start | bytes 1572872 | tf_op jit(solution)/shard_map/ppermute | solution.py:376
  50.1 3.4 %collective-permute-start.7 = (bf16[4,1,512,128]{3,2,1,0:T(8,128)(2,1)}, bf16[4,1,512,128]{3,2,1,0:T(8,128)(2,1)S(1)}, u32[]{:S(2)}, u32[]{:S(2)}) collective-permute-start(bf16[4,1,512,128]{3,2,1,0:T(8,128)(2,1)} %collective-permute-done.3.rest_1_), channel_id=1, source_target_pairs={{0,16},{16,0},{32,48},{48,32},{64,80},{80,64},{96,112},{112,96},{1... | collective-permute-start | bytes 1572872 | tf_op jit(solution)/shard_map/ppermute | solution.py:376
  50.2 3.4 %collective-permute-start.8 = (bf16[4,1,512,128]{3,2,1,0:T(8,128)(2,1)}, bf16[4,1,512,128]{3,2,1,0:T(8,128)(2,1)S(1)}, u32[]{:S(2)}, u32[]{:S(2)}) collective-permute-start(bf16[4,1,512,128]{3,2,1,0:T(8,128)(2,1)} %collective-permute-done.4.rest_2_), channel_id=1, source_target_pairs={{0,16},{16,0},{32,48},{48,32},{64,80},{80,64},{96,112},{112,96},{1... | collective-permute-start | bytes 1572872 | tf_op jit(solution)/shard_map/ppermute | solution.py:376
  50.6 3.5 %collective-permute-start.9 = (bf16[4,1,512,128]{3,2,1,0:T(8,128)(2,1)}, bf16[4,1,512,128]{3,2,1,0:T(8,128)(2,1)S(1)}, u32[]{:S(2)}, u32[]{:S(2)}) collective-permute-start(bf16[4,1,512,128]{3,2,1,0:T(8,128)(2,1)} %collective-permute-done.5.rest_3_), channel_id=1, source_target_pairs={{0,16},{16,0},{32,48},{48,32},{64,80},{80,64},{96,112},{112,96},{1... | collective-permute-start | bytes 1572872 | tf_op jit(solution)/shard_map/ppermute | solution.py:376
  53.6 0.8 copy-start.6
  53.6 1.0 %copy-start.7 = (bf16[4,1,512,128]{3,2,1,0:T(8,128)(2,1)}, bf16[4,1,512,128]{3,2,1,0:T(8,128)(2,1)S(1)}, u32[]{:S(2)}) copy-start(bf16[4,1,512,128]{3,2,1,0:T(8,128)(2,1)S(1)} %collective-permute-done.7.rest_5_) | copy-start | bytes 1572868
  53.6 1.1 %copy-start.8 = (bf16[4,1,512,128]{3,2,1,0:T(8,128)(2,1)}, bf16[4,1,512,128]{3,2,1,0:T(8,128)(2,1)S(1)}, u32[]{:S(2)}) copy-start(bf16[4,1,512,128]{3,2,1,0:T(8,128)(2,1)S(1)} %collective-permute-done.8.rest_6_) | copy-start | bytes 1572868
  54.1 0.8 copy-start.9

commit v6 on v5

--- a/solution.py
+++ b/solution.py
@@ -135,7 +135,7 @@
     for copy in copies:
         copy.start()
 
-    spread[...] = own[...].astype(jnp.float32).reshape(targets * chunks, LANES)
+    spread[pl.ds(0, targets * chunks), :] = own[...].astype(jnp.float32).reshape(targets * chunks, LANES)
     for chunk in range(chunks):
         part = spread[pl.ds(chunk, targets, stride=chunks), :]
         own_rows[:, pl.ds(chunk * LANES, LANES)] = part.astype(jnp.bfloat16)
@@ -175,7 +175,7 @@
         out_specs=(hbm,) * 4,
         scratch_shapes=[
             pltpu.VMEM((width, hidden), jnp.bfloat16),
-            pltpu.VMEM((targets * chunks, LANES), jnp.float32),
+            pltpu.VMEM((targets * chunks + chunks, LANES), jnp.float32),
             pltpu.VMEM((targets, width), jnp.bfloat16),
             pltpu.VMEM((width, units), jnp.bfloat16),
             pltpu.VMEM((targets, units), jnp.float32),
@@ -260,7 +260,7 @@
         out_specs=vmem,
         scratch_shapes=[
             pltpu.SMEM(source.shape, jnp.int32),
-            pltpu.VMEM((2 * GROUP * chunks, LANES), jnp.float32),
+            pltpu.VMEM((2 * GROUP * chunks + chunks, LANES), jnp.float32),
             pltpu.VMEM((LIVE, width), jnp.bfloat16),
             pltpu.VMEM((targets, hidden), jnp.bfloat16),
             pltpu.VMEM((width, hidden), jnp.bfloat16),

time: 90.7 us -> 90.7 us (level)
  no operation moved by 1% of the time
where the time goes in v6:
time: 90.7 us; the launch traced here: 90.3 us
  starting transfers between devices  27 us (30%)
  waiting for transfers between devices  25.2 us (28%)
  Pallas kernels  22 us (24%)
  other arithmetic  8.69 us (10%)
  local copies, waits for them, and re-layouts  6.96 us (8%)
    all_to_all x1, waiting for transfers between devices, on_device(): lax.all_to_all(blocks, AXES, split_axis=0, concat_axis=0, tiled=True)  21.4 us
    ppermute x6, starting transfers between devices, shifted(): return lax.ppermute(x, AXES, pairs)  10.3 us
    all_to_all x1, starting transfers between devices, on_device(): lax.all_to_all(requests.reshape(peers, 1, capacity), AXES, split_axis=0,...  9.18 us
    pallas_call x1, Pallas kernels, finish(): pl.pallas_call(finish_kernel, out_shape=jax.ShapeDtypeStruct((targets, un...  8.11 us
    pallas_call x1, Pallas kernels, pick(): pl.pallas_call(pick_kernel, out_shape=(pltpu.HBM((peers * capacity,) + ti...  6.42 us
    all_to_all x1, starting transfers between devices, on_device(): lax.all_to_all(blocks, AXES, split_axis=0, concat_axis=0, tiled=True)  5.76 us
    pallas_call x1, Pallas kernels, prepare(): pl.pallas_call(prepare_kernel, out_shape=(pltpu.HBM((width, hidden), jnp....  5.69 us
    all_to_all x1, waiting for transfers between devices, on_device(): lax.all_to_all(requests.reshape(peers, 1, capacity), AXES, split_axis=0,...  3.24 us
  transfers between devices with their start and end apart: 12, of which 3 were waited for; matrix products, arithmetic and copies ran while one was open for 16% of the time, Pallas kernels for 15%

profile of v6, /device:TPU:1, one launch (start us, length us, event | category | flops | bytes accessed | tf_op | source)
XLA Modules:
  0.0 90.3 jit_solution(14508567082500036792)
XLA Ops:
  0.0 2.5 %collective-permute-start = (bf16[1024,128]{1,0:T(8,128)(2,1)}, bf16[1024,128]{1,0:T(8,128)(2,1)S(1)}, u32[]{:S(2)}, u32[]{:S(2)}) collective-permute-start(bf16[1024,128]{1,0:T(8,128)(2,1)} %refs_0_.1), channel_id=1, source_target_pairs={{0,4},{1,5},{2,6},{3,7},{4,8},{5,9},{6,10},{7,11},{8,12},{9,13},{1... | collective-permute-start | bytes 786440 | tf_op jit(solution)/shard_map/ppermute | solution.py:308
  2.5 2.1 %collective-permute-start.1 = (bf16[1024,128]{1,0:T(8,128)(2,1)}, bf16[1024,128]{1,0:T(8,128)(2,1)S(1)}, u32[]{:S(2)}, u32[]{:S(2)}) collective-permute-start(bf16[1024,128]{1,0:T(8,128)(2,1)} %refs_0_.1), channel_id=1, source_target_pairs={{0,12},{1,13},{2,14},{3,15},{4,0},{5,1},{6,2},{7,3},{8,4},{9,5},{1... | collective-permute-start | bytes 786440 | tf_op jit(solution)/shard_map/ppermute | solution.py:308
  4.6 1.3 %collective-permute-start.2 = (bf16[1024,128]{1,0:T(8,128)(2,1)}, bf16[1024,128]{1,0:T(8,128)(2,1)S(1)}, u32[]{:S(2)}, u32[]{:S(2)}) collective-permute-start(bf16[1024,128]{1,0:T(8,128)(2,1)} %refs_0_.1), channel_id=1, source_target_pairs={{0,8},{1,9},{2,10},{3,11},{4,12},{5,13},{6,14},{7,15},{8,0},{9,1},... | collective-permute-start | bytes 786440 | tf_op jit(solution)/shard_map/ppermute | solution.py:308
  5.9 1.4 %copy.15 = s32[1,128,13]{2,1,0:T(8,128)} copy(s32[1,128,13]{1,0,2:T(1,128)} %param.11) | data formatting | bytes 13312 | tf_op args[1]
  7.3 9.2 %all-to-all-start = ((s32[128,1,13]{2,1,0:T(1,128)}), s32[128,1,13]{2,1,0:T(1,128)S(1)}, u32[]{:S(2)}, u32[]{:S(2)}) async-start(s32[128,1,13]{2,1,0:T(1,128)} %bitcast), calls=%async_computation | async-start | bytes 131072 | tf_op jit(solution)/shard_map/all_to_all | solution.py:366
  16.6 1.8 %join.1.rest_0_ = bf16[4,1,512,128]{3,2,1,0:T(8,128)(2,1)} custom-call(bf16[1024,128]{1,0:T(8,128)(2,1)} %refs_0_.1, bf16[1024,128]{1,0:T(8,128)(2,1)S(1)} %collective-permute-done.refs_1_, bf16[1024,128]{1,0:T(8,128)(2,1)S(1)} %collective-permute-done.1.refs_2_, bf16[1024,128]{1,0:T(8,128)(2,1)S(1)} %collective-permute-done.2.refs_3_), custom_call_target="tpu_custom_call" | custom-call | flops 1150000000 | bytes 1 | tf_op jit(solution)/shard_map/join/pallas_call | solution.py:328
  18.3 1.5 %collective-permute-start.3 = (bf16[4,1,512,128]{3,2,1,0:T(8,128)(2,1)}, bf16[4,1,512,128]{3,2,1,0:T(8,128)(2,1)}, u32[]{:S(2)}, u32[]{:S(2)}) collective-permute-start(bf16[4,1,512,128]{3,2,1,0:T(8,128)(2,1)} %join.1.rest_0_), channel_id=1, source_target_pairs={{0,1},{1,2},{2,3},{3,0},{4,5},{5,6},{6,7},{7,4},{8,9},{9,10},{10,1... | collective-permute-start | bytes 1572872 | tf_op jit(solution)/shard_map/ppermute | solution.py:308
  19.8 1.3 %collective-permute-start.4 = (bf16[4,1,512,128]{3,2,1,0:T(8,128)(2,1)}, bf16[4,1,512,128]{3,2,1,0:T(8,128)(2,1)}, u32[]{:S(2)}, u32[]{:S(2)}) collective-permute-start(bf16[4,1,512,128]{3,2,1,0:T(8,128)(2,1)} %join.1.rest_0_), channel_id=1, source_target_pairs={{0,3},{1,0},{2,1},{3,2},{4,7},{5,4},{6,5},{7,6},{8,11},{9,8},{10,9... | collective-permute-start | bytes 1572872 | tf_op jit(solution)/shard_map/ppermute | solution.py:308
  21.2 1.6 %collective-permute-start.5 = (bf16[4,1,512,128]{3,2,1,0:T(8,128)(2,1)}, bf16[4,1,512,128]{3,2,1,0:T(8,128)(2,1)}, u32[]{:S(2)}, u32[]{:S(2)}) collective-permute-start(bf16[4,1,512,128]{3,2,1,0:T(8,128)(2,1)} %join.1.rest_0_), channel_id=1, source_target_pairs={{0,2},{1,3},{2,0},{3,1},{4,6},{5,7},{6,4},{7,5},{8,10},{9,11},{10,... | collective-permute-start | bytes 1572872 | tf_op jit(solution)/shard_map/ppermute | solution.py:308
  22.8 3.2 %all-to-all-done.served = s32[128,1,13]{2,1,0:T(1,128)S(1)} async-done(((s32[128,1,13]{2,1,0:T(1,128)}), s32[128,1,13]{2,1,0:T(1,128)S(1)}, u32[]{:S(2)}, u32[]{:S(2)}) %all-to-all-start) | async-done | bytes 6688 | tf_op jit(solution)/shard_map/all_to_all | solution.py:366
  26.0 6.4 %pick.1 = (bf16[1664,8,128]{2,1,0:T(8,128)(2,1)}, bf16[32,8,128]{2,1,0:T(8,128)(2,1)}) custom-call(s32[128,1,13]{2,1,0:T(1,128)S(1)} %all-to-all-done.served, s32[32]{0:T(128)} %target_rows.1, bf16[4096,1024]{1,0:T(8,128)(2,1)} %features.1), custom_call_target="tpu_custom_call" | custom-call | flops 8049999872 | bytes 1 | tf_op jit(solution)/shard_map/pick/pallas_call | solution.py:91
  32.5 5.8 %all-to-all-start.1 = ((bf16[128,104,128]{2,1,0:T(8,128)(2,1)}), bf16[128,104,128]{2,1,0:T(8,128)(2,1)S(1)}, u32[]{:S(2)}, u32[]{:S(2)}) async-start(bf16[128,104,128]{2,1,0:T(8,128)(2,1)} %bitcast.13), calls=%async_computation.1 | async-start | bytes 6815744 | tf_op jit(solution)/shard_map/all_to_all | solution.py:372
  41.0 1.3 %select_n.86 = s32[16]{0:T(128)} reshape(s32[4,4]{1,0:T(4,128)} %get-tuple-element.33) | data formatting | bytes 128 | tf_op jit(solution)/shard_map/jit(_where)/select_n | solution.py:349
  42.9 1.3 %broadcast_in_dim.76 = s32[2,16]{1,0:T(2,128)} broadcast(s32[2]{0:T(128)} %pad_add_fusion.1), dimensions={0} | broadcast | bytes 136 | tf_op jit(solution)/shard_map/broadcast_in_dim | solution.py:350
  44.2 0.7 stack_reshape.3
  44.9 0.7 copy.16
  45.6 1.7 %select_reduce_fusion.1 = s32[32,50]{0,1:T(8,128)S(1)} fusion(s32[128]{0:T(128)} %select_reduce_fusion.4, s32[32,50]{0,1:T(8,128)S(1)} %get-tuple-element.31), kind=kLoop, calls=%fused_computation.2 | loop fusion | flops 612800 | bytes 13312 | tf_op jit(solution)/shard_map/reduce_sum | solution.py:288
  47.4 1.6 %select_reduce_fusion = s32[32,800]{1,0:T(8,128)S(1)} fusion(s32[32,50]{0,1:T(8,128)} %copy.16, s32[32,50]{0,1:T(8,128)S(1)} %fusion.2), kind=kLoop, calls=%fused_computation | loop fusion | flops 3814400 | bytes 115200 | tf_op jit(solution)/shard_map/reduce_sum | solution.py:291
  49.0 1.1 %collective-permute-start.6 = (bf16[4,1,512,128]{3,2,1,0:T(8,128)(2,1)}, bf16[4,1,512,128]{3,2,1,0:T(8,128)(2,1)S(1)}, u32[]{:S(2)}, u32[]{:S(2)}) collective-permute-start(bf16[4,1,512,128]{3,2,1,0:T(8,128)(2,1)} %join.1.rest_0_), channel_id=1, source_target_pairs={{0,16},{16,0},{32,48},{48,32},{64,80},{80,64},{96,112},{112,96},{1... | collective-permute-start | bytes 1572872 | tf_op jit(solution)/shard_map/ppermute | solution.py:376
  50.7 0.8 add_bitcast_fusion
  52.2 0.8 select_reduce_fusion.3
  54.9 5.7 %prepare.1 = (bf16[1024,2048]{1,0:T(8,128)(2,1)}, f32[32,1024]{1,0:T(8,128)}, bf16[64,800]{1,0:T(8,128)(2,1)}, f32[32,128]{1,0:T(8,128)}) custom-call(s32[2,32]{1,0:T(2,128)S(1)} %pad_add_fusion.blocks, bf16[32,8,128]{2,1,0:T(8,128)(2,1)S(1)} %copy-done.1, f32[32,800]{1,0:T(8,128)S(1)} %convert_element_type.3.shares, bf16[3072,1024]{1,0:T(8,128)(2,1)} %output_weight.3, ...), custom_call_target="tpu_custom_call" | custom-call | flops 20700000256 | bytes 1 | tf_op jit(solution)/shard_map/prepare/pallas_call | solution.py:166
  60.6 21.4 %all-to-all-done.1 = bf16[128,104,128]{2,1,0:T(8,128)(2,1)S(1)} async-done(((bf16[128,104,128]{2,1,0:T(8,128)(2,1)}), bf16[128,104,128]{2,1,0:T(8,128)(2,1)S(1)}, u32[]{:S(2)}, u32[]{:S(2)}) %all-to-all-start.1) | async-done | bytes 3407904 | tf_op jit(solution)/shard_map/all_to_all | solution.py:372
  82.0 8.1 %finish.1 = bf16[32,1024]{1,0:T(8,128)(2,1)} custom-call(s32[800]{0:T(1024)} %iota_add_fusion.source_hbm, bf16[1664,8,128]{2,1,0:T(8,128)(2,1)S(1)} %bitcast.11, bf16[64,800]{1,0:T(8,128)(2,1)} %get-tuple-element.27.parts_hbm, f32[32,128]{1,0:T(8,128)} %get-tuple-element.28.total_hbm, f32[32,1024]{1,0:T(8,128)} %get-tuple-element.29.base_hbm, ...), custom_call_target="tpu_custom_call" | custom-call | tf_op jit(solution)/shard_map/finish/pallas_call | solution.py:256
  (46 shorter events, 6.5 us)
Async XLA Ops:
  0.0 16.5 %collective-permute-start = (bf16[1024,128]{1,0:T(8,128)(2,1)}, bf16[1024,128]{1,0:T(8,128)(2,1)S(1)}, u32[]{:S(2)}, u32[]{:S(2)}) collective-permute-start(bf16[1024,128]{1,0:T(8,128)(2,1)} %refs_0_.1), channel_id=1, source_target_pairs={{0,4},{1,5},{2,6},{3,7},{4,8},{5,9},{6,10},{7,11},{8,12},{9,13},{1... | collective-permute-start | bytes 786440 | tf_op jit(solution)/shard_map/ppermute | solution.py:308
  2.5 14.1 %collective-permute-start.1 = (bf16[1024,128]{1,0:T(8,128)(2,1)}, bf16[1024,128]{1,0:T(8,128)(2,1)S(1)}, u32[]{:S(2)}, u32[]{:S(2)}) collective-permute-start(bf16[1024,128]{1,0:T(8,128)(2,1)} %refs_0_.1), channel_id=1, source_target_pairs={{0,12},{1,13},{2,14},{3,15},{4,0},{5,1},{6,2},{7,3},{8,4},{9,5},{1... | collective-permute-start | bytes 786440 | tf_op jit(solution)/shard_map/ppermute | solution.py:308
  4.6 12.0 %collective-permute-start.2 = (bf16[1024,128]{1,0:T(8,128)(2,1)}, bf16[1024,128]{1,0:T(8,128)(2,1)S(1)}, u32[]{:S(2)}, u32[]{:S(2)}) collective-permute-start(bf16[1024,128]{1,0:T(8,128)(2,1)} %refs_0_.1), channel_id=1, source_target_pairs={{0,8},{1,9},{2,10},{3,11},{4,12},{5,13},{6,14},{7,15},{8,0},{9,1},... | collective-permute-start | bytes 786440 | tf_op jit(solution)/shard_map/ppermute | solution.py:308
  7.3 18.7 %all-to-all-start = ((s32[128,1,13]{2,1,0:T(1,128)}), s32[128,1,13]{2,1,0:T(1,128)S(1)}, u32[]{:S(2)}, u32[]{:S(2)}) async-start(s32[128,1,13]{2,1,0:T(1,128)} %bitcast), calls=%async_computation | async-start | bytes 131072 | tf_op jit(solution)/shard_map/all_to_all | solution.py:366
  18.3 19.9 %collective-permute-start.3 = (bf16[4,1,512,128]{3,2,1,0:T(8,128)(2,1)}, bf16[4,1,512,128]{3,2,1,0:T(8,128)(2,1)}, u32[]{:S(2)}, u32[]{:S(2)}) collective-permute-start(bf16[4,1,512,128]{3,2,1,0:T(8,128)(2,1)} %join.1.rest_0_), channel_id=1, source_target_pairs={{0,1},{1,2},{2,3},{3,0},{4,5},{5,6},{6,7},{7,4},{8,9},{9,10},{10,1... | collective-permute-start | bytes 1572872 | tf_op jit(solution)/shard_map/ppermute | solution.py:308
  19.8 18.5 %collective-permute-start.4 = (bf16[4,1,512,128]{3,2,1,0:T(8,128)(2,1)}, bf16[4,1,512,128]{3,2,1,0:T(8,128)(2,1)}, u32[]{:S(2)}, u32[]{:S(2)}) collective-permute-start(bf16[4,1,512,128]{3,2,1,0:T(8,128)(2,1)} %join.1.rest_0_), channel_id=1, source_target_pairs={{0,3},{1,0},{2,1},{3,2},{4,7},{5,4},{6,5},{7,6},{8,11},{9,8},{10,9... | collective-permute-start | bytes 1572872 | tf_op jit(solution)/shard_map/ppermute | solution.py:308
  21.2 17.1 %collective-permute-start.5 = (bf16[4,1,512,128]{3,2,1,0:T(8,128)(2,1)}, bf16[4,1,512,128]{3,2,1,0:T(8,128)(2,1)}, u32[]{:S(2)}, u32[]{:S(2)}) collective-permute-start(bf16[4,1,512,128]{3,2,1,0:T(8,128)(2,1)} %join.1.rest_0_), channel_id=1, source_target_pairs={{0,2},{1,3},{2,0},{3,1},{4,6},{5,7},{6,4},{7,5},{8,10},{9,11},{10,... | collective-permute-start | bytes 1572872 | tf_op jit(solution)/shard_map/ppermute | solution.py:308
  32.4 5.9 %copy-start.5 = (s32[4]{0:T(128)S(1)}, s32[4]{0:T(128)}, u32[]{:S(2)}) copy-start(s32[4]{0:T(128)} %constant.83.clone) | copy-start | bytes 52
  32.5 5.9 %copy-start.2 = (s32[32,50]{1,0:T(8,128)S(1)}, s32[32,50]{1,0:T(8,128)}, u32[]{:S(2)}) copy-start(s32[32,50]{1,0:T(8,128)} %param.13) | copy-start | bytes 19204
  32.5 12.5 %copy-start.3 = (s32[32,50]{1,0:T(8,128)S(1)}, s32[32,50]{1,0:T(8,128)}, u32[]{:S(2)}) copy-start(s32[32,50]{1,0:T(8,128)} %param.14) | copy-start | bytes 19204
  32.5 22.4 %copy-start = (f32[1024]{0:T(1024)S(1)}, f32[1024]{0:T(1024)}, u32[]{:S(2)}) copy-start(f32[1024]{0:T(1024)} %param.18) | copy-start | bytes 12292
  32.5 22.4 %copy-start.1 = (bf16[32,8,128]{2,1,0:T(8,128)(2,1)S(1)}, bf16[32,8,128]{2,1,0:T(8,128)(2,1)}, u32[]{:S(2)}) copy-start(bf16[32,8,128]{2,1,0:T(8,128)(2,1)} %get-tuple-element.21.own) | copy-start | bytes 196612
  32.5 49.5 %all-to-all-start.1 = ((bf16[128,104,128]{2,1,0:T(8,128)(2,1)}), bf16[128,104,128]{2,1,0:T(8,128)(2,1)S(1)}, u32[]{:S(2)}, u32[]{:S(2)}) async-start(bf16[128,104,128]{2,1,0:T(8,128)(2,1)} %bitcast.13), calls=%async_computation.1 | async-start | bytes 6815744 | tf_op jit(solution)/shard_map/all_to_all | solution.py:372
  39.2 1.3 %copy-start.4 = (s32[128]{0:T(128)}, s32[128]{0:T(128)S(1)}, u32[]{:S(2)}) copy-start(s32[128]{0:T(128)S(1)} %select_reduce_fusion.2) | copy-start | bytes 1540
  49.0 4.6 %collective-permute-start.6 = (bf16[4,1,512,128]{3,2,1,0:T(8,128)(2,1)}, bf16[4,1,512,128]{3,2,1,0:T(8,128)(2,1)S(1)}, u32[]{:S(2)}, u32[]{:S(2)}) collective-permute-start(bf16[4,1,512,128]{3,2,1,0:T(8,128)(2,1)} %join.1.rest_0_), channel_id=1, source_target_pairs={{0,16},{16,0},{32,48},{48,32},{64,80},{80,64},{96,112},{112,96},{1... | collective-permute-start | bytes 1572872 | tf_op jit(solution)/shard_map/ppermute | solution.py:376
  50.1 3.4 %collective-permute-start.7 = (bf16[4,1,512,128]{3,2,1,0:T(8,128)(2,1)}, bf16[4,1,512,128]{3,2,1,0:T(8,128)(2,1)S(1)}, u32[]{:S(2)}, u32[]{:S(2)}) collective-permute-start(bf16[4,1,512,128]{3,2,1,0:T(8,128)(2,1)} %collective-permute-done.3.rest_1_), channel_id=1, source_target_pairs={{0,16},{16,0},{32,48},{48,32},{64,80},{80,64},{96,112},{112,96},{1... | collective-permute-start | bytes 1572872 | tf_op jit(solution)/shard_map/ppermute | solution.py:376
  50.2 3.4 %collective-permute-start.8 = (bf16[4,1,512,128]{3,2,1,0:T(8,128)(2,1)}, bf16[4,1,512,128]{3,2,1,0:T(8,128)(2,1)S(1)}, u32[]{:S(2)}, u32[]{:S(2)}) collective-permute-start(bf16[4,1,512,128]{3,2,1,0:T(8,128)(2,1)} %collective-permute-done.4.rest_2_), channel_id=1, source_target_pairs={{0,16},{16,0},{32,48},{48,32},{64,80},{80,64},{96,112},{112,96},{1... | collective-permute-start | bytes 1572872 | tf_op jit(solution)/shard_map/ppermute | solution.py:376
  50.6 3.5 %collective-permute-start.9 = (bf16[4,1,512,128]{3,2,1,0:T(8,128)(2,1)}, bf16[4,1,512,128]{3,2,1,0:T(8,128)(2,1)S(1)}, u32[]{:S(2)}, u32[]{:S(2)}) collective-permute-start(bf16[4,1,512,128]{3,2,1,0:T(8,128)(2,1)} %collective-permute-done.5.rest_3_), channel_id=1, source_target_pairs={{0,16},{16,0},{32,48},{48,32},{64,80},{80,64},{96,112},{112,96},{1... | collective-permute-start | bytes 1572872 | tf_op jit(solution)/shard_map/ppermute | solution.py:376
  53.6 0.8 copy-start.6
  53.6 1.0 %copy-start.7 = (bf16[4,1,512,128]{3,2,1,0:T(8,128)(2,1)}, bf16[4,1,512,128]{3,2,1,0:T(8,128)(2,1)S(1)}, u32[]{:S(2)}) copy-start(bf16[4,1,512,128]{3,2,1,0:T(8,128)(2,1)S(1)} %collective-permute-done.7.rest_5_) | copy-start | bytes 1572868
  53.6 1.1 %copy-start.8 = (bf16[4,1,512,128]{3,2,1,0:T(8,128)(2,1)}, bf16[4,1,512,128]{3,2,1,0:T(8,128)(2,1)S(1)}, u32[]{:S(2)}) copy-start(bf16[4,1,512,128]{3,2,1,0:T(8,128)(2,1)S(1)} %collective-permute-done.8.rest_6_) | copy-start | bytes 1572868
  54.1 0.8 copy-start.9

commit v7 on v6

--- a/solution.py
+++ b/solution.py
@@ -44,10 +44,10 @@
         pltpu.make_async_copy(served, index, sems.at[loads]),
         pltpu.make_async_copy(target_rows, own_index, sems.at[loads + 1]),
     ]
+    for copy in lists:
+        copy.start()
     for step in range(loads):
         load(step).start()
-    for copy in lists:
-        copy.start()
     for step in range(loads):
         load(step).wait()
         part = pl.ds(step * ROWS_AT_ONCE, ROWS_AT_ONCE)

time: 90.7 us -> 90.7 us (level)
  no operation moved by 1% of the time
where the time goes in v7:
time: 90.7 us; the launch traced here: 90.3 us
  starting transfers between devices  27 us (30%)
  waiting for transfers between devices  25.2 us (28%)
  Pallas kernels  22 us (24%)
  other arithmetic  8.69 us (10%)
  local copies, waits for them, and re-layouts  6.96 us (8%)
    all_to_all x1, waiting for transfers between devices, on_device(): lax.all_to_all(blocks, AXES, split_axis=0, concat_axis=0, tiled=True)  21.4 us
    ppermute x6, starting transfers between devices, shifted(): return lax.ppermute(x, AXES, pairs)  10.3 us
    all_to_all x1, starting transfers between devices, on_device(): lax.all_to_all(requests.reshape(peers, 1, capacity), AXES, split_axis=0,...  9.18 us
    pallas_call x1, Pallas kernels, finish(): pl.pallas_call(finish_kernel, out_shape=jax.ShapeDtypeStruct((targets, un...  8.11 us
    pallas_call x1, Pallas kernels, pick(): pl.pallas_call(pick_kernel, out_shape=(pltpu.HBM((peers * capacity,) + ti...  6.42 us
    all_to_all x1, starting transfers between devices, on_device(): lax.all_to_all(blocks, AXES, split_axis=0, concat_axis=0, tiled=True)  5.76 us
    pallas_call x1, Pallas kernels, prepare(): pl.pallas_call(prepare_kernel, out_shape=(pltpu.HBM((width, hidden), jnp....  5.69 us
    all_to_all x1, waiting for transfers between devices, on_device(): lax.all_to_all(requests.reshape(peers, 1, capacity), AXES, split_axis=0,...  3.24 us
  transfers between devices with their start and end apart: 12, of which 3 were waited for; matrix products, arithmetic and copies ran while one was open for 16% of the time, Pallas kernels for 15%

profile of v7, /device:TPU:1, one launch (start us, length us, event | category | flops | bytes accessed | tf_op | source)
XLA Modules:
  0.0 90.3 jit_solution(14887568942715131654)
XLA Ops:
  0.0 2.5 %collective-permute-start = (bf16[1024,128]{1,0:T(8,128)(2,1)}, bf16[1024,128]{1,0:T(8,128)(2,1)S(1)}, u32[]{:S(2)}, u32[]{:S(2)}) collective-permute-start(bf16[1024,128]{1,0:T(8,128)(2,1)} %refs_0_.1), channel_id=1, source_target_pairs={{0,4},{1,5},{2,6},{3,7},{4,8},{5,9},{6,10},{7,11},{8,12},{9,13},{1... | collective-permute-start | bytes 786440 | tf_op jit(solution)/shard_map/ppermute | solution.py:308
  2.5 2.1 %collective-permute-start.1 = (bf16[1024,128]{1,0:T(8,128)(2,1)}, bf16[1024,128]{1,0:T(8,128)(2,1)S(1)}, u32[]{:S(2)}, u32[]{:S(2)}) collective-permute-start(bf16[1024,128]{1,0:T(8,128)(2,1)} %refs_0_.1), channel_id=1, source_target_pairs={{0,12},{1,13},{2,14},{3,15},{4,0},{5,1},{6,2},{7,3},{8,4},{9,5},{1... | collective-permute-start | bytes 786440 | tf_op jit(solution)/shard_map/ppermute | solution.py:308
  4.6 1.3 %collective-permute-start.2 = (bf16[1024,128]{1,0:T(8,128)(2,1)}, bf16[1024,128]{1,0:T(8,128)(2,1)S(1)}, u32[]{:S(2)}, u32[]{:S(2)}) collective-permute-start(bf16[1024,128]{1,0:T(8,128)(2,1)} %refs_0_.1), channel_id=1, source_target_pairs={{0,8},{1,9},{2,10},{3,11},{4,12},{5,13},{6,14},{7,15},{8,0},{9,1},... | collective-permute-start | bytes 786440 | tf_op jit(solution)/shard_map/ppermute | solution.py:308
  5.9 1.4 %copy.15 = s32[1,128,13]{2,1,0:T(8,128)} copy(s32[1,128,13]{1,0,2:T(1,128)} %param.11) | data formatting | bytes 13312 | tf_op args[1]
  7.3 9.2 %all-to-all-start = ((s32[128,1,13]{2,1,0:T(1,128)}), s32[128,1,13]{2,1,0:T(1,128)S(1)}, u32[]{:S(2)}, u32[]{:S(2)}) async-start(s32[128,1,13]{2,1,0:T(1,128)} %bitcast), calls=%async_computation | async-start | bytes 131072 | tf_op jit(solution)/shard_map/all_to_all | solution.py:366
  16.6 1.8 %join.1.rest_0_ = bf16[4,1,512,128]{3,2,1,0:T(8,128)(2,1)} custom-call(bf16[1024,128]{1,0:T(8,128)(2,1)} %refs_0_.1, bf16[1024,128]{1,0:T(8,128)(2,1)S(1)} %collective-permute-done.refs_1_, bf16[1024,128]{1,0:T(8,128)(2,1)S(1)} %collective-permute-done.1.refs_2_, bf16[1024,128]{1,0:T(8,128)(2,1)S(1)} %collective-permute-done.2.refs_3_), custom_call_target="tpu_custom_call" | custom-call | flops 1150000000 | bytes 1 | tf_op jit(solution)/shard_map/join/pallas_call | solution.py:328
  18.3 1.5 %collective-permute-start.3 = (bf16[4,1,512,128]{3,2,1,0:T(8,128)(2,1)}, bf16[4,1,512,128]{3,2,1,0:T(8,128)(2,1)}, u32[]{:S(2)}, u32[]{:S(2)}) collective-permute-start(bf16[4,1,512,128]{3,2,1,0:T(8,128)(2,1)} %join.1.rest_0_), channel_id=1, source_target_pairs={{0,1},{1,2},{2,3},{3,0},{4,5},{5,6},{6,7},{7,4},{8,9},{9,10},{10,1... | collective-permute-start | bytes 1572872 | tf_op jit(solution)/shard_map/ppermute | solution.py:308
  19.8 1.3 %collective-permute-start.4 = (bf16[4,1,512,128]{3,2,1,0:T(8,128)(2,1)}, bf16[4,1,512,128]{3,2,1,0:T(8,128)(2,1)}, u32[]{:S(2)}, u32[]{:S(2)}) collective-permute-start(bf16[4,1,512,128]{3,2,1,0:T(8,128)(2,1)} %join.1.rest_0_), channel_id=1, source_target_pairs={{0,3},{1,0},{2,1},{3,2},{4,7},{5,4},{6,5},{7,6},{8,11},{9,8},{10,9... | collective-permute-start | bytes 1572872 | tf_op jit(solution)/shard_map/ppermute | solution.py:308
  21.2 1.6 %collective-permute-start.5 = (bf16[4,1,512,128]{3,2,1,0:T(8,128)(2,1)}, bf16[4,1,512,128]{3,2,1,0:T(8,128)(2,1)}, u32[]{:S(2)}, u32[]{:S(2)}) collective-permute-start(bf16[4,1,512,128]{3,2,1,0:T(8,128)(2,1)} %join.1.rest_0_), channel_id=1, source_target_pairs={{0,2},{1,3},{2,0},{3,1},{4,6},{5,7},{6,4},{7,5},{8,10},{9,11},{10,... | collective-permute-start | bytes 1572872 | tf_op jit(solution)/shard_map/ppermute | solution.py:308
  22.8 3.2 %all-to-all-done.served = s32[128,1,13]{2,1,0:T(1,128)S(1)} async-done(((s32[128,1,13]{2,1,0:T(1,128)}), s32[128,1,13]{2,1,0:T(1,128)S(1)}, u32[]{:S(2)}, u32[]{:S(2)}) %all-to-all-start) | async-done | bytes 6688 | tf_op jit(solution)/shard_map/all_to_all | solution.py:366
  26.0 6.4 %pick.1 = (bf16[1664,8,128]{2,1,0:T(8,128)(2,1)}, bf16[32,8,128]{2,1,0:T(8,128)(2,1)}) custom-call(s32[128,1,13]{2,1,0:T(1,128)S(1)} %all-to-all-done.served, s32[32]{0:T(128)} %target_rows.1, bf16[4096,1024]{1,0:T(8,128)(2,1)} %features.1), custom_call_target="tpu_custom_call" | custom-call | flops 8049999872 | bytes 1 | tf_op jit(solution)/shard_map/pick/pallas_call | solution.py:91
  32.5 5.8 %all-to-all-start.1 = ((bf16[128,104,128]{2,1,0:T(8,128)(2,1)}), bf16[128,104,128]{2,1,0:T(8,128)(2,1)S(1)}, u32[]{:S(2)}, u32[]{:S(2)}) async-start(bf16[128,104,128]{2,1,0:T(8,128)(2,1)} %bitcast.13), calls=%async_computation.1 | async-start | bytes 6815744 | tf_op jit(solution)/shard_map/all_to_all | solution.py:372
  41.0 1.3 %select_n.86 = s32[16]{0:T(128)} reshape(s32[4,4]{1,0:T(4,128)} %get-tuple-element.33) | data formatting | bytes 128 | tf_op jit(solution)/shard_map/jit(_where)/select_n | solution.py:349
  42.9 1.3 %broadcast_in_dim.76 = s32[2,16]{1,0:T(2,128)} broadcast(s32[2]{0:T(128)} %pad_add_fusion.1), dimensions={0} | broadcast | bytes 136 | tf_op jit(solution)/shard_map/broadcast_in_dim | solution.py:350
  44.2 0.7 stack_reshape.3
  44.9 0.7 copy.16
  45.6 1.7 %select_reduce_fusion.1 = s32[32,50]{0,1:T(8,128)S(1)} fusion(s32[128]{0:T(128)} %select_reduce_fusion.4, s32[32,50]{0,1:T(8,128)S(1)} %get-tuple-element.31), kind=kLoop, calls=%fused_computation.2 | loop fusion | flops 612800 | bytes 13312 | tf_op jit(solution)/shard_map/reduce_sum | solution.py:288
  47.4 1.6 %select_reduce_fusion = s32[32,800]{1,0:T(8,128)S(1)} fusion(s32[32,50]{0,1:T(8,128)} %copy.16, s32[32,50]{0,1:T(8,128)S(1)} %fusion.2), kind=kLoop, calls=%fused_computation | loop fusion | flops 3814400 | bytes 115200 | tf_op jit(solution)/shard_map/reduce_sum | solution.py:291
  49.0 1.1 %collective-permute-start.6 = (bf16[4,1,512,128]{3,2,1,0:T(8,128)(2,1)}, bf16[4,1,512,128]{3,2,1,0:T(8,128)(2,1)S(1)}, u32[]{:S(2)}, u32[]{:S(2)}) collective-permute-start(bf16[4,1,512,128]{3,2,1,0:T(8,128)(2,1)} %join.1.rest_0_), channel_id=1, source_target_pairs={{0,16},{16,0},{32,48},{48,32},{64,80},{80,64},{96,112},{112,96},{1... | collective-permute-start | bytes 1572872 | tf_op jit(solution)/shard_map/ppermute | solution.py:376
  50.7 0.8 add_bitcast_fusion
  52.2 0.8 select_reduce_fusion.3
  54.9 5.7 %prepare.1 = (bf16[1024,2048]{1,0:T(8,128)(2,1)}, f32[32,1024]{1,0:T(8,128)}, bf16[64,800]{1,0:T(8,128)(2,1)}, f32[32,128]{1,0:T(8,128)}) custom-call(s32[2,32]{1,0:T(2,128)S(1)} %pad_add_fusion.blocks, bf16[32,8,128]{2,1,0:T(8,128)(2,1)S(1)} %copy-done.1, f32[32,800]{1,0:T(8,128)S(1)} %convert_element_type.3.shares, bf16[3072,1024]{1,0:T(8,128)(2,1)} %output_weight.3, ...), custom_call_target="tpu_custom_call" | custom-call | flops 20700000256 | bytes 1 | tf_op jit(solution)/shard_map/prepare/pallas_call | solution.py:166
  60.6 21.4 %all-to-all-done.1 = bf16[128,104,128]{2,1,0:T(8,128)(2,1)S(1)} async-done(((bf16[128,104,128]{2,1,0:T(8,128)(2,1)}), bf16[128,104,128]{2,1,0:T(8,128)(2,1)S(1)}, u32[]{:S(2)}, u32[]{:S(2)}) %all-to-all-start.1) | async-done | bytes 3407904 | tf_op jit(solution)/shard_map/all_to_all | solution.py:372
  82.0 8.1 %finish.1 = bf16[32,1024]{1,0:T(8,128)(2,1)} custom-call(s32[800]{0:T(1024)} %iota_add_fusion.source_hbm, bf16[1664,8,128]{2,1,0:T(8,128)(2,1)S(1)} %bitcast.11, bf16[64,800]{1,0:T(8,128)(2,1)} %get-tuple-element.27.parts_hbm, f32[32,128]{1,0:T(8,128)} %get-tuple-element.28.total_hbm, f32[32,1024]{1,0:T(8,128)} %get-tuple-element.29.base_hbm, ...), custom_call_target="tpu_custom_call" | custom-call | tf_op jit(solution)/shard_map/finish/pallas_call | solution.py:256
  (46 shorter events, 6.5 us)
Async XLA Ops:
  0.0 16.5 %collective-permute-start = (bf16[1024,128]{1,0:T(8,128)(2,1)}, bf16[1024,128]{1,0:T(8,128)(2,1)S(1)}, u32[]{:S(2)}, u32[]{:S(2)}) collective-permute-start(bf16[1024,128]{1,0:T(8,128)(2,1)} %refs_0_.1), channel_id=1, source_target_pairs={{0,4},{1,5},{2,6},{3,7},{4,8},{5,9},{6,10},{7,11},{8,12},{9,13},{1... | collective-permute-start | bytes 786440 | tf_op jit(solution)/shard_map/ppermute | solution.py:308
  2.5 14.1 %collective-permute-start.1 = (bf16[1024,128]{1,0:T(8,128)(2,1)}, bf16[1024,128]{1,0:T(8,128)(2,1)S(1)}, u32[]{:S(2)}, u32[]{:S(2)}) collective-permute-start(bf16[1024,128]{1,0:T(8,128)(2,1)} %refs_0_.1), channel_id=1, source_target_pairs={{0,12},{1,13},{2,14},{3,15},{4,0},{5,1},{6,2},{7,3},{8,4},{9,5},{1... | collective-permute-start | bytes 786440 | tf_op jit(solution)/shard_map/ppermute | solution.py:308
  4.6 12.0 %collective-permute-start.2 = (bf16[1024,128]{1,0:T(8,128)(2,1)}, bf16[1024,128]{1,0:T(8,128)(2,1)S(1)}, u32[]{:S(2)}, u32[]{:S(2)}) collective-permute-start(bf16[1024,128]{1,0:T(8,128)(2,1)} %refs_0_.1), channel_id=1, source_target_pairs={{0,8},{1,9},{2,10},{3,11},{4,12},{5,13},{6,14},{7,15},{8,0},{9,1},... | collective-permute-start | bytes 786440 | tf_op jit(solution)/shard_map/ppermute | solution.py:308
  7.3 18.7 %all-to-all-start = ((s32[128,1,13]{2,1,0:T(1,128)}), s32[128,1,13]{2,1,0:T(1,128)S(1)}, u32[]{:S(2)}, u32[]{:S(2)}) async-start(s32[128,1,13]{2,1,0:T(1,128)} %bitcast), calls=%async_computation | async-start | bytes 131072 | tf_op jit(solution)/shard_map/all_to_all | solution.py:366
  18.3 19.9 %collective-permute-start.3 = (bf16[4,1,512,128]{3,2,1,0:T(8,128)(2,1)}, bf16[4,1,512,128]{3,2,1,0:T(8,128)(2,1)}, u32[]{:S(2)}, u32[]{:S(2)}) collective-permute-start(bf16[4,1,512,128]{3,2,1,0:T(8,128)(2,1)} %join.1.rest_0_), channel_id=1, source_target_pairs={{0,1},{1,2},{2,3},{3,0},{4,5},{5,6},{6,7},{7,4},{8,9},{9,10},{10,1... | collective-permute-start | bytes 1572872 | tf_op jit(solution)/shard_map/ppermute | solution.py:308
  19.8 18.5 %collective-permute-start.4 = (bf16[4,1,512,128]{3,2,1,0:T(8,128)(2,1)}, bf16[4,1,512,128]{3,2,1,0:T(8,128)(2,1)}, u32[]{:S(2)}, u32[]{:S(2)}) collective-permute-start(bf16[4,1,512,128]{3,2,1,0:T(8,128)(2,1)} %join.1.rest_0_), channel_id=1, source_target_pairs={{0,3},{1,0},{2,1},{3,2},{4,7},{5,4},{6,5},{7,6},{8,11},{9,8},{10,9... | collective-permute-start | bytes 1572872 | tf_op jit(solution)/shard_map/ppermute | solution.py:308
  21.2 17.1 %collective-permute-start.5 = (bf16[4,1,512,128]{3,2,1,0:T(8,128)(2,1)}, bf16[4,1,512,128]{3,2,1,0:T(8,128)(2,1)}, u32[]{:S(2)}, u32[]{:S(2)}) collective-permute-start(bf16[4,1,512,128]{3,2,1,0:T(8,128)(2,1)} %join.1.rest_0_), channel_id=1, source_target_pairs={{0,2},{1,3},{2,0},{3,1},{4,6},{5,7},{6,4},{7,5},{8,10},{9,11},{10,... | collective-permute-start | bytes 1572872 | tf_op jit(solution)/shard_map/ppermute | solution.py:308
  32.5 5.9 %copy-start.5 = (s32[4]{0:T(128)S(1)}, s32[4]{0:T(128)}, u32[]{:S(2)}) copy-start(s32[4]{0:T(128)} %constant.83.clone) | copy-start | bytes 52
  32.5 5.9 %copy-start.2 = (s32[32,50]{1,0:T(8,128)S(1)}, s32[32,50]{1,0:T(8,128)}, u32[]{:S(2)}) copy-start(s32[32,50]{1,0:T(8,128)} %param.13) | copy-start | bytes 19204
  32.5 12.5 %copy-start.3 = (s32[32,50]{1,0:T(8,128)S(1)}, s32[32,50]{1,0:T(8,128)}, u32[]{:S(2)}) copy-start(s32[32,50]{1,0:T(8,128)} %param.14) | copy-start | bytes 19204
  32.5 22.4 %copy-start = (f32[1024]{0:T(1024)S(1)}, f32[1024]{0:T(1024)}, u32[]{:S(2)}) copy-start(f32[1024]{0:T(1024)} %param.18) | copy-start | bytes 12292
  32.5 22.4 %copy-start.1 = (bf16[32,8,128]{2,1,0:T(8,128)(2,1)S(1)}, bf16[32,8,128]{2,1,0:T(8,128)(2,1)}, u32[]{:S(2)}) copy-start(bf16[32,8,128]{2,1,0:T(8,128)(2,1)} %get-tuple-element.21.own) | copy-start | bytes 196612
  32.5 49.5 %all-to-all-start.1 = ((bf16[128,104,128]{2,1,0:T(8,128)(2,1)}), bf16[128,104,128]{2,1,0:T(8,128)(2,1)S(1)}, u32[]{:S(2)}, u32[]{:S(2)}) async-start(bf16[128,104,128]{2,1,0:T(8,128)(2,1)} %bitcast.13), calls=%async_computation.1 | async-start | bytes 6815744 | tf_op jit(solution)/shard_map/all_to_all | solution.py:372
  39.2 1.3 %copy-start.4 = (s32[128]{0:T(128)}, s32[128]{0:T(128)S(1)}, u32[]{:S(2)}) copy-start(s32[128]{0:T(128)S(1)} %select_reduce_fusion.2) | copy-start | bytes 1540
  49.0 4.6 %collective-permute-start.6 = (bf16[4,1,512,128]{3,2,1,0:T(8,128)(2,1)}, bf16[4,1,512,128]{3,2,1,0:T(8,128)(2,1)S(1)}, u32[]{:S(2)}, u32[]{:S(2)}) collective-permute-start(bf16[4,1,512,128]{3,2,1,0:T(8,128)(2,1)} %join.1.rest_0_), channel_id=1, source_target_pairs={{0,16},{16,0},{32,48},{48,32},{64,80},{80,64},{96,112},{112,96},{1... | collective-permute-start | bytes 1572872 | tf_op jit(solution)/shard_map/ppermute | solution.py:376
  50.1 3.4 %collective-permute-start.7 = (bf16[4,1,512,128]{3,2,1,0:T(8,128)(2,1)}, bf16[4,1,512,128]{3,2,1,0:T(8,128)(2,1)S(1)}, u32[]{:S(2)}, u32[]{:S(2)}) collective-permute-start(bf16[4,1,512,128]{3,2,1,0:T(8,128)(2,1)} %collective-permute-done.3.rest_1_), channel_id=1, source_target_pairs={{0,16},{16,0},{32,48},{48,32},{64,80},{80,64},{96,112},{112,96},{1... | collective-permute-start | bytes 1572872 | tf_op jit(solution)/shard_map/ppermute | solution.py:376
  50.2 3.4 %collective-permute-start.8 = (bf16[4,1,512,128]{3,2,1,0:T(8,128)(2,1)}, bf16[4,1,512,128]{3,2,1,0:T(8,128)(2,1)S(1)}, u32[]{:S(2)}, u32[]{:S(2)}) collective-permute-start(bf16[4,1,512,128]{3,2,1,0:T(8,128)(2,1)} %collective-permute-done.4.rest_2_), channel_id=1, source_target_pairs={{0,16},{16,0},{32,48},{48,32},{64,80},{80,64},{96,112},{112,96},{1... | collective-permute-start | bytes 1572872 | tf_op jit(solution)/shard_map/ppermute | solution.py:376
  50.6 3.5 %collective-permute-start.9 = (bf16[4,1,512,128]{3,2,1,0:T(8,128)(2,1)}, bf16[4,1,512,128]{3,2,1,0:T(8,128)(2,1)S(1)}, u32[]{:S(2)}, u32[]{:S(2)}) collective-permute-start(bf16[4,1,512,128]{3,2,1,0:T(8,128)(2,1)} %collective-permute-done.5.rest_3_), channel_id=1, source_target_pairs={{0,16},{16,0},{32,48},{48,32},{64,80},{80,64},{96,112},{112,96},{1... | collective-permute-start | bytes 1572872 | tf_op jit(solution)/shard_map/ppermute | solution.py:376
  53.6 0.8 copy-start.6
  53.6 1.0 %copy-start.7 = (bf16[4,1,512,128]{3,2,1,0:T(8,128)(2,1)}, bf16[4,1,512,128]{3,2,1,0:T(8,128)(2,1)S(1)}, u32[]{:S(2)}) copy-start(bf16[4,1,512,128]{3,2,1,0:T(8,128)(2,1)S(1)} %collective-permute-done.7.rest_5_) | copy-start | bytes 1572868
  53.6 1.1 %copy-start.8 = (bf16[4,1,512,128]{3,2,1,0:T(8,128)(2,1)}, bf16[4,1,512,128]{3,2,1,0:T(8,128)(2,1)S(1)}, u32[]{:S(2)}) copy-start(bf16[4,1,512,128]{3,2,1,0:T(8,128)(2,1)S(1)} %collective-permute-done.8.rest_6_) | copy-start | bytes 1572868
  54.1 0.8 copy-start.9

commit v8 on v7

--- a/solution.py
+++ b/solution.py
@@ -9,7 +9,7 @@
 
 LIVE = 800
 LANES = 128
-ROWS_AT_ONCE = 256
+ROWS_AT_ONCE = 128
 BLOCK = 1024
 GROUP = 32
 PEERS_AT_ONCE = 4
@@ -104,7 +104,7 @@
             pltpu.VMEM((peers * capacity,) + tile, features.dtype),
             pltpu.VMEM((targets,) + tile, features.dtype),
             pltpu.SemaphoreType.DMA((count // ROWS_AT_ONCE + 2,)),
-            pltpu.SemaphoreType.DMA((9,)),
+            pltpu.SemaphoreType.DMA((17,)),
         ],
         compiler_params=GRANT,
         cost_estimate=takes(COST_PICK),

time: 90.7 us -> 90.9 us (level)
  transfers between devices with their start and end apart: 12 -> 12, of which waited for: 3 -> 3; matrix products, arithmetic and copies ran while one was open for 16% -> 16% of each run, Pallas kernels for 15% -> 16%
where the time goes in v8:
time: 90.9 us; the launch traced here: 90.4 us
  starting transfers between devices  27 us (30%)
  waiting for transfers between devices  25.2 us (28%)
  Pallas kernels  22.2 us (24%)
  other arithmetic  8.69 us (10%)
  local copies, waits for them, and re-layouts  6.96 us (8%)
    all_to_all x1, waiting for transfers between devices, on_device(): lax.all_to_all(blocks, AXES, split_axis=0, concat_axis=0, tiled=True)  21.4 us
    ppermute x6, starting transfers between devices, shifted(): return lax.ppermute(x, AXES, pairs)  10.3 us
    all_to_all x1, starting transfers between devices, on_device(): lax.all_to_all(requests.reshape(peers, 1, capacity), AXES, split_axis=0,...  9.18 us
    pallas_call x1, Pallas kernels, finish(): pl.pallas_call(finish_kernel, out_shape=jax.ShapeDtypeStruct((targets, un...  8.11 us
    pallas_call x1, Pallas kernels, pick(): pl.pallas_call(pick_kernel, out_shape=(pltpu.HBM((peers * capacity,) + ti...  6.58 us
    all_to_all x1, starting transfers between devices, on_device(): lax.all_to_all(blocks, AXES, split_axis=0, concat_axis=0, tiled=True)  5.76 us
    pallas_call x1, Pallas kernels, prepare(): pl.pallas_call(prepare_kernel, out_shape=(pltpu.HBM((width, hidden), jnp....  5.69 us
    all_to_all x1, waiting for transfers between devices, on_device(): lax.all_to_all(requests.reshape(peers, 1, capacity), AXES, split_axis=0,...  3.24 us
  transfers between devices with their start and end apart: 12, of which 3 were waited for; matrix products, arithmetic and copies ran while one was open for 16% of the time, Pallas kernels for 16%

profile of v8, /device:TPU:1, one launch (start us, length us, event | category | flops | bytes accessed | tf_op | source)
XLA Modules:
  0.0 90.4 jit_solution(11553294404563857251)
XLA Ops:
  0.0 2.5 %collective-permute-start = (bf16[1024,128]{1,0:T(8,128)(2,1)}, bf16[1024,128]{1,0:T(8,128)(2,1)S(1)}, u32[]{:S(2)}, u32[]{:S(2)}) collective-permute-start(bf16[1024,128]{1,0:T(8,128)(2,1)} %refs_0_.1), channel_id=1, source_target_pairs={{0,4},{1,5},{2,6},{3,7},{4,8},{5,9},{6,10},{7,11},{8,12},{9,13},{1... | collective-permute-start | bytes 786440 | tf_op jit(solution)/shard_map/ppermute | solution.py:308
  2.5 2.1 %collective-permute-start.1 = (bf16[1024,128]{1,0:T(8,128)(2,1)}, bf16[1024,128]{1,0:T(8,128)(2,1)S(1)}, u32[]{:S(2)}, u32[]{:S(2)}) collective-permute-start(bf16[1024,128]{1,0:T(8,128)(2,1)} %refs_0_.1), channel_id=1, source_target_pairs={{0,12},{1,13},{2,14},{3,15},{4,0},{5,1},{6,2},{7,3},{8,4},{9,5},{1... | collective-permute-start | bytes 786440 | tf_op jit(solution)/shard_map/ppermute | solution.py:308
  4.6 1.3 %collective-permute-start.2 = (bf16[1024,128]{1,0:T(8,128)(2,1)}, bf16[1024,128]{1,0:T(8,128)(2,1)S(1)}, u32[]{:S(2)}, u32[]{:S(2)}) collective-permute-start(bf16[1024,128]{1,0:T(8,128)(2,1)} %refs_0_.1), channel_id=1, source_target_pairs={{0,8},{1,9},{2,10},{3,11},{4,12},{5,13},{6,14},{7,15},{8,0},{9,1},... | collective-permute-start | bytes 786440 | tf_op jit(solution)/shard_map/ppermute | solution.py:308
  5.9 1.4 %copy.15 = s32[1,128,13]{2,1,0:T(8,128)} copy(s32[1,128,13]{1,0,2:T(1,128)} %param.11) | data formatting | bytes 13312 | tf_op args[1]
  7.3 9.2 %all-to-all-start = ((s32[128,1,13]{2,1,0:T(1,128)}), s32[128,1,13]{2,1,0:T(1,128)S(1)}, u32[]{:S(2)}, u32[]{:S(2)}) async-start(s32[128,1,13]{2,1,0:T(1,128)} %bitcast), calls=%async_computation | async-start | bytes 131072 | tf_op jit(solution)/shard_map/all_to_all | solution.py:366
  16.6 1.8 %join.1.rest_0_ = bf16[4,1,512,128]{3,2,1,0:T(8,128)(2,1)} custom-call(bf16[1024,128]{1,0:T(8,128)(2,1)} %refs_0_.1, bf16[1024,128]{1,0:T(8,128)(2,1)S(1)} %collective-permute-done.refs_1_, bf16[1024,128]{1,0:T(8,128)(2,1)S(1)} %collective-permute-done.1.refs_2_, bf16[1024,128]{1,0:T(8,128)(2,1)S(1)} %collective-permute-done.2.refs_3_), custom_call_target="tpu_custom_call" | custom-call | flops 1150000000 | bytes 1 | tf_op jit(solution)/shard_map/join/pallas_call | solution.py:328
  18.3 1.5 %collective-permute-start.3 = (bf16[4,1,512,128]{3,2,1,0:T(8,128)(2,1)}, bf16[4,1,512,128]{3,2,1,0:T(8,128)(2,1)}, u32[]{:S(2)}, u32[]{:S(2)}) collective-permute-start(bf16[4,1,512,128]{3,2,1,0:T(8,128)(2,1)} %join.1.rest_0_), channel_id=1, source_target_pairs={{0,1},{1,2},{2,3},{3,0},{4,5},{5,6},{6,7},{7,4},{8,9},{9,10},{10,1... | collective-permute-start | bytes 1572872 | tf_op jit(solution)/shard_map/ppermute | solution.py:308
  19.8 1.3 %collective-permute-start.4 = (bf16[4,1,512,128]{3,2,1,0:T(8,128)(2,1)}, bf16[4,1,512,128]{3,2,1,0:T(8,128)(2,1)}, u32[]{:S(2)}, u32[]{:S(2)}) collective-permute-start(bf16[4,1,512,128]{3,2,1,0:T(8,128)(2,1)} %join.1.rest_0_), channel_id=1, source_target_pairs={{0,3},{1,0},{2,1},{3,2},{4,7},{5,4},{6,5},{7,6},{8,11},{9,8},{10,9... | collective-permute-start | bytes 1572872 | tf_op jit(solution)/shard_map/ppermute | solution.py:308
  21.2 1.6 %collective-permute-start.5 = (bf16[4,1,512,128]{3,2,1,0:T(8,128)(2,1)}, bf16[4,1,512,128]{3,2,1,0:T(8,128)(2,1)}, u32[]{:S(2)}, u32[]{:S(2)}) collective-permute-start(bf16[4,1,512,128]{3,2,1,0:T(8,128)(2,1)} %join.1.rest_0_), channel_id=1, source_target_pairs={{0,2},{1,3},{2,0},{3,1},{4,6},{5,7},{6,4},{7,5},{8,10},{9,11},{10,... | collective-permute-start | bytes 1572872 | tf_op jit(solution)/shard_map/ppermute | solution.py:308
  22.8 3.2 %all-to-all-done.served = s32[128,1,13]{2,1,0:T(1,128)S(1)} async-done(((s32[128,1,13]{2,1,0:T(1,128)}), s32[128,1,13]{2,1,0:T(1,128)S(1)}, u32[]{:S(2)}, u32[]{:S(2)}) %all-to-all-start) | async-done | bytes 6688 | tf_op jit(solution)/shard_map/all_to_all | solution.py:366
  26.0 6.6 %pick.1 = (bf16[1664,8,128]{2,1,0:T(8,128)(2,1)}, bf16[32,8,128]{2,1,0:T(8,128)(2,1)}) custom-call(s32[128,1,13]{2,1,0:T(1,128)S(1)} %all-to-all-done.served, s32[32]{0:T(128)} %target_rows.1, bf16[4096,1024]{1,0:T(8,128)(2,1)} %features.1), custom_call_target="tpu_custom_call" | custom-call | flops 8049999872 | bytes 1 | tf_op jit(solution)/shard_map/pick/pallas_call | solution.py:91
  32.7 5.8 %all-to-all-start.1 = ((bf16[128,104,128]{2,1,0:T(8,128)(2,1)}), bf16[128,104,128]{2,1,0:T(8,128)(2,1)S(1)}, u32[]{:S(2)}, u32[]{:S(2)}) async-start(bf16[128,104,128]{2,1,0:T(8,128)(2,1)} %bitcast.13), calls=%async_computation.1 | async-start | bytes 6815744 | tf_op jit(solution)/shard_map/all_to_all | solution.py:372
  41.2 1.3 %select_n.86 = s32[16]{0:T(128)} reshape(s32[4,4]{1,0:T(4,128)} %get-tuple-element.33) | data formatting | bytes 128 | tf_op jit(solution)/shard_map/jit(_where)/select_n | solution.py:349
  43.1 1.3 %broadcast_in_dim.76 = s32[2,16]{1,0:T(2,128)} broadcast(s32[2]{0:T(128)} %pad_add_fusion.1), dimensions={0} | broadcast | bytes 136 | tf_op jit(solution)/shard_map/broadcast_in_dim | solution.py:350
  44.4 0.7 stack_reshape.3
  45.1 0.7 copy.16
  45.8 1.7 %select_reduce_fusion.1 = s32[32,50]{0,1:T(8,128)S(1)} fusion(s32[128]{0:T(128)} %select_reduce_fusion.4, s32[32,50]{0,1:T(8,128)S(1)} %get-tuple-element.31), kind=kLoop, calls=%fused_computation.2 | loop fusion | flops 612800 | bytes 13312 | tf_op jit(solution)/shard_map/reduce_sum | solution.py:288
  47.5 1.6 %select_reduce_fusion = s32[32,800]{1,0:T(8,128)S(1)} fusion(s32[32,50]{0,1:T(8,128)} %copy.16, s32[32,50]{0,1:T(8,128)S(1)} %fusion.2), kind=kLoop, calls=%fused_computation | loop fusion | flops 3814400 | bytes 115200 | tf_op jit(solution)/shard_map/reduce_sum | solution.py:291
  49.1 1.1 %collective-permute-start.6 = (bf16[4,1,512,128]{3,2,1,0:T(8,128)(2,1)}, bf16[4,1,512,128]{3,2,1,0:T(8,128)(2,1)S(1)}, u32[]{:S(2)}, u32[]{:S(2)}) collective-permute-start(bf16[4,1,512,128]{3,2,1,0:T(8,128)(2,1)} %join.1.rest_0_), channel_id=1, source_target_pairs={{0,16},{16,0},{32,48},{48,32},{64,80},{80,64},{96,112},{112,96},{1... | collective-permute-start | bytes 1572872 | tf_op jit(solution)/shard_map/ppermute | solution.py:376
  50.9 0.8 add_bitcast_fusion
  52.3 0.8 select_reduce_fusion.3
  55.1 5.7 %prepare.1 = (bf16[1024,2048]{1,0:T(8,128)(2,1)}, f32[32,1024]{1,0:T(8,128)}, bf16[64,800]{1,0:T(8,128)(2,1)}, f32[32,128]{1,0:T(8,128)}) custom-call(s32[2,32]{1,0:T(2,128)S(1)} %pad_add_fusion.blocks, bf16[32,8,128]{2,1,0:T(8,128)(2,1)S(1)} %copy-done.1, f32[32,800]{1,0:T(8,128)S(1)} %convert_element_type.3.shares, bf16[3072,1024]{1,0:T(8,128)(2,1)} %output_weight.3, ...), custom_call_target="tpu_custom_call" | custom-call | flops 20700000256 | bytes 1 | tf_op jit(solution)/shard_map/prepare/pallas_call | solution.py:166
  60.8 21.4 %all-to-all-done.1 = bf16[128,104,128]{2,1,0:T(8,128)(2,1)S(1)} async-done(((bf16[128,104,128]{2,1,0:T(8,128)(2,1)}), bf16[128,104,128]{2,1,0:T(8,128)(2,1)S(1)}, u32[]{:S(2)}, u32[]{:S(2)}) %all-to-all-start.1) | async-done | bytes 3407904 | tf_op jit(solution)/shard_map/all_to_all | solution.py:372
  82.2 8.1 %finish.1 = bf16[32,1024]{1,0:T(8,128)(2,1)} custom-call(s32[800]{0:T(1024)} %iota_add_fusion.source_hbm, bf16[1664,8,128]{2,1,0:T(8,128)(2,1)S(1)} %bitcast.11, bf16[64,800]{1,0:T(8,128)(2,1)} %get-tuple-element.27.parts_hbm, f32[32,128]{1,0:T(8,128)} %get-tuple-element.28.total_hbm, f32[32,1024]{1,0:T(8,128)} %get-tuple-element.29.base_hbm, ...), custom_call_target="tpu_custom_call" | custom-call | tf_op jit(solution)/shard_map/finish/pallas_call | solution.py:256
  (46 shorter events, 6.5 us)
Async XLA Ops:
  0.0 16.5 %collective-permute-start = (bf16[1024,128]{1,0:T(8,128)(2,1)}, bf16[1024,128]{1,0:T(8,128)(2,1)S(1)}, u32[]{:S(2)}, u32[]{:S(2)}) collective-permute-start(bf16[1024,128]{1,0:T(8,128)(2,1)} %refs_0_.1), channel_id=1, source_target_pairs={{0,4},{1,5},{2,6},{3,7},{4,8},{5,9},{6,10},{7,11},{8,12},{9,13},{1... | collective-permute-start | bytes 786440 | tf_op jit(solution)/shard_map/ppermute | solution.py:308
  2.5 14.1 %collective-permute-start.1 = (bf16[1024,128]{1,0:T(8,128)(2,1)}, bf16[1024,128]{1,0:T(8,128)(2,1)S(1)}, u32[]{:S(2)}, u32[]{:S(2)}) collective-permute-start(bf16[1024,128]{1,0:T(8,128)(2,1)} %refs_0_.1), channel_id=1, source_target_pairs={{0,12},{1,13},{2,14},{3,15},{4,0},{5,1},{6,2},{7,3},{8,4},{9,5},{1... | collective-permute-start | bytes 786440 | tf_op jit(solution)/shard_map/ppermute | solution.py:308
  4.6 12.0 %collective-permute-start.2 = (bf16[1024,128]{1,0:T(8,128)(2,1)}, bf16[1024,128]{1,0:T(8,128)(2,1)S(1)}, u32[]{:S(2)}, u32[]{:S(2)}) collective-permute-start(bf16[1024,128]{1,0:T(8,128)(2,1)} %refs_0_.1), channel_id=1, source_target_pairs={{0,8},{1,9},{2,10},{3,11},{4,12},{5,13},{6,14},{7,15},{8,0},{9,1},... | collective-permute-start | bytes 786440 | tf_op jit(solution)/shard_map/ppermute | solution.py:308
  7.3 18.7 %all-to-all-start = ((s32[128,1,13]{2,1,0:T(1,128)}), s32[128,1,13]{2,1,0:T(1,128)S(1)}, u32[]{:S(2)}, u32[]{:S(2)}) async-start(s32[128,1,13]{2,1,0:T(1,128)} %bitcast), calls=%async_computation | async-start | bytes 131072 | tf_op jit(solution)/shard_map/all_to_all | solution.py:366
  18.3 20.1 %collective-permute-start.3 = (bf16[4,1,512,128]{3,2,1,0:T(8,128)(2,1)}, bf16[4,1,512,128]{3,2,1,0:T(8,128)(2,1)}, u32[]{:S(2)}, u32[]{:S(2)}) collective-permute-start(bf16[4,1,512,128]{3,2,1,0:T(8,128)(2,1)} %join.1.rest_0_), channel_id=1, source_target_pairs={{0,1},{1,2},{2,3},{3,0},{4,5},{5,6},{6,7},{7,4},{8,9},{9,10},{10,1... | collective-permute-start | bytes 1572872 | tf_op jit(solution)/shard_map/ppermute | solution.py:308
  19.8 18.6 %collective-permute-start.4 = (bf16[4,1,512,128]{3,2,1,0:T(8,128)(2,1)}, bf16[4,1,512,128]{3,2,1,0:T(8,128)(2,1)}, u32[]{:S(2)}, u32[]{:S(2)}) collective-permute-start(bf16[4,1,512,128]{3,2,1,0:T(8,128)(2,1)} %join.1.rest_0_), channel_id=1, source_target_pairs={{0,3},{1,0},{2,1},{3,2},{4,7},{5,4},{6,5},{7,6},{8,11},{9,8},{10,9... | collective-permute-start | bytes 1572872 | tf_op jit(solution)/shard_map/ppermute | solution.py:308
  21.2 17.3 %collective-permute-start.5 = (bf16[4,1,512,128]{3,2,1,0:T(8,128)(2,1)}, bf16[4,1,512,128]{3,2,1,0:T(8,128)(2,1)}, u32[]{:S(2)}, u32[]{:S(2)}) collective-permute-start(bf16[4,1,512,128]{3,2,1,0:T(8,128)(2,1)} %join.1.rest_0_), channel_id=1, source_target_pairs={{0,2},{1,3},{2,0},{3,1},{4,6},{5,7},{6,4},{7,5},{8,10},{9,11},{10,... | collective-permute-start | bytes 1572872 | tf_op jit(solution)/shard_map/ppermute | solution.py:308
  32.6 5.9 %copy-start.5 = (s32[4]{0:T(128)S(1)}, s32[4]{0:T(128)}, u32[]{:S(2)}) copy-start(s32[4]{0:T(128)} %constant.83.clone) | copy-start | bytes 52
  32.6 5.9 %copy-start.2 = (s32[32,50]{1,0:T(8,128)S(1)}, s32[32,50]{1,0:T(8,128)}, u32[]{:S(2)}) copy-start(s32[32,50]{1,0:T(8,128)} %param.13) | copy-start | bytes 19204
  32.6 12.5 %copy-start.3 = (s32[32,50]{1,0:T(8,128)S(1)}, s32[32,50]{1,0:T(8,128)}, u32[]{:S(2)}) copy-start(s32[32,50]{1,0:T(8,128)} %param.14) | copy-start | bytes 19204
  32.6 22.4 %copy-start = (f32[1024]{0:T(1024)S(1)}, f32[1024]{0:T(1024)}, u32[]{:S(2)}) copy-start(f32[1024]{0:T(1024)} %param.18) | copy-start | bytes 12292
  32.7 22.4 %copy-start.1 = (bf16[32,8,128]{2,1,0:T(8,128)(2,1)S(1)}, bf16[32,8,128]{2,1,0:T(8,128)(2,1)}, u32[]{:S(2)}) copy-start(bf16[32,8,128]{2,1,0:T(8,128)(2,1)} %get-tuple-element.21.own) | copy-start | bytes 196612
  32.7 49.5 %all-to-all-start.1 = ((bf16[128,104,128]{2,1,0:T(8,128)(2,1)}), bf16[128,104,128]{2,1,0:T(8,128)(2,1)S(1)}, u32[]{:S(2)}, u32[]{:S(2)}) async-start(bf16[128,104,128]{2,1,0:T(8,128)(2,1)} %bitcast.13), calls=%async_computation.1 | async-start | bytes 6815744 | tf_op jit(solution)/shard_map/all_to_all | solution.py:372
  39.3 1.3 %copy-start.4 = (s32[128]{0:T(128)}, s32[128]{0:T(128)S(1)}, u32[]{:S(2)}) copy-start(s32[128]{0:T(128)S(1)} %select_reduce_fusion.2) | copy-start | bytes 1540
  49.1 4.6 %collective-permute-start.6 = (bf16[4,1,512,128]{3,2,1,0:T(8,128)(2,1)}, bf16[4,1,512,128]{3,2,1,0:T(8,128)(2,1)S(1)}, u32[]{:S(2)}, u32[]{:S(2)}) collective-permute-start(bf16[4,1,512,128]{3,2,1,0:T(8,128)(2,1)} %join.1.rest_0_), channel_id=1, source_target_pairs={{0,16},{16,0},{32,48},{48,32},{64,80},{80,64},{96,112},{112,96},{1... | collective-permute-start | bytes 1572872 | tf_op jit(solution)/shard_map/ppermute | solution.py:376
  50.3 3.4 %collective-permute-start.7 = (bf16[4,1,512,128]{3,2,1,0:T(8,128)(2,1)}, bf16[4,1,512,128]{3,2,1,0:T(8,128)(2,1)S(1)}, u32[]{:S(2)}, u32[]{:S(2)}) collective-permute-start(bf16[4,1,512,128]{3,2,1,0:T(8,128)(2,1)} %collective-permute-done.3.rest_1_), channel_id=1, source_target_pairs={{0,16},{16,0},{32,48},{48,32},{64,80},{80,64},{96,112},{112,96},{1... | collective-permute-start | bytes 1572872 | tf_op jit(solution)/shard_map/ppermute | solution.py:376
  50.4 3.4 %collective-permute-start.8 = (bf16[4,1,512,128]{3,2,1,0:T(8,128)(2,1)}, bf16[4,1,512,128]{3,2,1,0:T(8,128)(2,1)S(1)}, u32[]{:S(2)}, u32[]{:S(2)}) collective-permute-start(bf16[4,1,512,128]{3,2,1,0:T(8,128)(2,1)} %collective-permute-done.4.rest_2_), channel_id=1, source_target_pairs={{0,16},{16,0},{32,48},{48,32},{64,80},{80,64},{96,112},{112,96},{1... | collective-permute-start | bytes 1572872 | tf_op jit(solution)/shard_map/ppermute | solution.py:376
  50.8 3.5 %collective-permute-start.9 = (bf16[4,1,512,128]{3,2,1,0:T(8,128)(2,1)}, bf16[4,1,512,128]{3,2,1,0:T(8,128)(2,1)S(1)}, u32[]{:S(2)}, u32[]{:S(2)}) collective-permute-start(bf16[4,1,512,128]{3,2,1,0:T(8,128)(2,1)} %collective-permute-done.5.rest_3_), channel_id=1, source_target_pairs={{0,16},{16,0},{32,48},{48,32},{64,80},{80,64},{96,112},{112,96},{1... | collective-permute-start | bytes 1572872 | tf_op jit(solution)/shard_map/ppermute | solution.py:376
  53.7 0.8 copy-start.6
  53.7 1.0 %copy-start.7 = (bf16[4,1,512,128]{3,2,1,0:T(8,128)(2,1)}, bf16[4,1,512,128]{3,2,1,0:T(8,128)(2,1)S(1)}, u32[]{:S(2)}) copy-start(bf16[4,1,512,128]{3,2,1,0:T(8,128)(2,1)S(1)} %collective-permute-done.7.rest_5_) | copy-start | bytes 1572868
  53.8 1.1 %copy-start.8 = (bf16[4,1,512,128]{3,2,1,0:T(8,128)(2,1)}, bf16[4,1,512,128]{3,2,1,0:T(8,128)(2,1)S(1)}, u32[]{:S(2)}) copy-start(bf16[4,1,512,128]{3,2,1,0:T(8,128)(2,1)S(1)} %collective-permute-done.8.rest_6_) | copy-start | bytes 1572868
  54.3 0.8 copy-start.9
